TPU v7x, 32 devices: a whole 2x2x4 slice. The times are simulated.
32 devices in a mesh: grp: 1, ep: 16 (over z, y, core), tp: 2 (over x).
Axes of the slice: x: 2, y: 2, z: 4, core: 2. Of those that a mesh axis runs over, the one named last changes fastest.
Arguments:
- tokens: bfloat16 [2560, 3072], P(('grp', 'ep'), 'tp'), may hold values from -6 to 6
- expert_ids: int32 [2560, 12], P(('grp', 'ep')), may hold values from 0 to 23, all different within a row; in each aligned block of 160 rows (0 to 159, 160 to 319, ...) at most 120 rows name the same one
- gate_weights: float32 [2560, 12], P(('grp', 'ep')), may hold values from 0.02 to 0.2
- expert_hidden: bfloat16 [16, 1920, 1024], P('ep', ('grp', 'tp')), may hold values from -6 to 6
- expert_down: bfloat16 [16, 1024, 3072], P('ep', None, 'tp'), may hold values from -0.1875 to 0.1875
- dense_hidden: bfloat16 [2560, 6144], P(('grp', 'ep'), 'tp'), may hold values from -6 to 6
- dense_down: bfloat16 [6144, 3072], P('tp', 'ep'), may hold values from -0.078125 to 0.078125
Outputs:
- mixed: bfloat16 [2560, 3072], P(('grp', 'ep'), 'tp')
Inputs may be any that keep to these rules, and one draw needn't show every extreme that they name: `expert_ids`: each row names 12 different ids; ids below 16 are experts with weights, the others zero experts. In each aligned block of 160 rows no id is named by more than 120 rows, a bound that some block reaches.
All inputs are finite; a program needn't handle non-finite values.
Results may differ from a plain program's by a relative error of at most 0.0038.
Values may be sent and summed in bfloat16 or wider, within the bound.
No kernel may reach another device: no remote copies, remote signals or barrier semaphores. Data moves between devices by JAX's collectives and lax.ppermute only.
A program may use at most 128 MiB of HBM per device.

v0:
```python
import jax
import jax.numpy as jnp
from jax import lax
from jax.sharding import PartitionSpec as P


def slot_numbers(block_ids, kinds):
    flat = block_ids.reshape(-1)
    labels = jnp.arange(kinds, dtype=jnp.int32)
    marks = (flat[:, None] == labels[None, :]).astype(jnp.int32)
    before = jnp.cumsum(marks, axis=0) - marks
    return jnp.sum(before * marks, axis=1).reshape(block_ids.shape)


def local(tokens, expert_ids, gate_weights, expert_hidden, expert_down, dense_hidden, dense_down):
    expert_ranks = lax.axis_size("ep")
    local_experts = expert_hidden.shape[0]
    experts = local_experts * expert_ranks
    capacity = expert_hidden.shape[1] * lax.axis_size("tp") // expert_ranks
    features = expert_down.shape[2]
    tok_rows = expert_ids.shape[0]
    outputs = jnp.einsum(
        "esh,ehd->esd",
        lax.all_gather(expert_hidden, "tp", axis=1, tiled=True),
        expert_down,
        preferred_element_type=jnp.float32,
    ).astype(jnp.bfloat16)
    returned = lax.all_to_all(outputs, "ep", split_axis=1, concat_axis=0, tiled=True)
    table = returned.reshape(experts * capacity, features)
    slots = slot_numbers(expert_ids, experts + experts // 2)
    genuine = expert_ids < experts
    column = jnp.where(genuine, expert_ids * capacity + slots, 0)
    weight_real = jnp.where(genuine, gate_weights, jnp.float32(0.0))
    row_index = jnp.broadcast_to(jnp.arange(tok_rows, dtype=jnp.int32)[:, None], expert_ids.shape)
    combine = (
        jnp.zeros((tok_rows, experts * capacity), jnp.float32)
        .at[row_index, column]
        .add(weight_real)
    )
    combine_high = combine.astype(jnp.bfloat16)
    combine_low = (combine - combine_high.astype(jnp.float32)).astype(jnp.bfloat16)
    routed = jnp.dot(combine_high, table, preferred_element_type=jnp.float32)
    routed = routed + jnp.dot(combine_low, table, preferred_element_type=jnp.float32)
    zero_gate = jnp.sum(jnp.where(genuine, jnp.float32(0.0), gate_weights), axis=1)
    identity = zero_gate[:, None] * tokens.astype(jnp.float32)
    columns = lax.all_gather(dense_down, "ep", axis=1, tiled=True)
    partial_value = jnp.dot(dense_hidden, columns, preferred_element_type=jnp.float32)
    dense = lax.psum_scatter(partial_value, "tp", scatter_dimension=1, tiled=True)
    return (dense + routed + identity).astype(jnp.bfloat16)


def solution(mesh):
    return jax.shard_map(
        local,
        mesh=mesh,
        in_specs=(
            P(("grp", "ep"), "tp"),
            P(("grp", "ep"), None),
            P(("grp", "ep"), None),
            P("ep", ("grp", "tp"), None),
            P("ep", None, "tp"),
            P(("grp", "ep"), "tp"),
            P("tp", "ep"),
        ),
        out_specs=P(("grp", "ep"), "tp"),
        check_vma=False,
    )
```

profile of v0, /device:TPU:13, one launch (start us, length us, event | category | flops | bytes accessed | tf_op | source)
XLA Modules:
  0.0 417.6 jit_solution(13954819183576420159)
XLA Ops:
  6.5 0.0 copy-start
  6.5 0.0 all-gather.5.cloned.1.call-start
  6.5 0.7 all-gather.5.cloned.1.call-update
  7.3 0.0 all-gather.3.cloned.1.call-start
  7.3 0.7 all-gather.3.cloned.1.call-update
  8.0 55.8 %all-gather.5.cloned.1.call-done = bf16[1,1920,1024]{2,1,0:T(8,128)(2,1)} async-done(((bf16[1,960,1024]{2,1,0:T(8,128)(2,1)}), bf16[1,1920,1024]{2,1,0:T(8,128)(2,1)}) %all-gather.5.cloned.1.call-update) | async-done | bytes 3932176 | tf_op jit(solution)/shard_map/all_gather | solution.py:24
  63.8 0.0 copy-done
  63.8 8.6 %fusion = bf16[1,1920,1536]{2,1,0:T(8,128)(2,1)S(1)} fusion(bf16[1,1920,1024]{2,1,0:T(8,128)(2,1)} %all-gather.5.cloned.1.call-done, bf16[1,1024,1536]{2,1,0:T(8,128)(2,1)S(1)} %copy-done), kind=kOutput, calls=%fused_computation.2 | convolution fusion | flops 6042746880 | bytes 12976128 | tf_op jit(solution)/shard_map/esh,ehd->esd/dot_general | solution.py:22
  72.5 36.6 %copy.59 = bf16[1,1920,1536]{2,0,1:T(2,128)(2,1)} copy(bf16[1,1920,1536]{2,1,0:T(8,128)(2,1)S(1)} %fusion) | data formatting | bytes 11796480 | tf_op jit(solution)/shard_map/convert_element_type | solution.py:27
  109.1 0.5 broadcast.57
  109.6 126.3 %reduce.4 = bf16[1920,1536]{1,0:T(8,128)(2,1)} reduce(bf16[1920,1,1536]{2,1,0:T(2,128)(2,1)} %bitcast.48, bf16[]{:T(256)} %broadcast.57), dimensions={1}, to_apply=%bitcast.46.reduce_sub_computation | reduce | bytes 11796482
  235.9 11.7 %reshape.65 = bf16[16,2,92160]{2,1,0:T(2,128)(2,1)} reshape(bf16[1920,1536]{1,0:T(8,128)(2,1)} %reduce.4) | data formatting | bytes 11796480
  247.6 0.0 copy-start.3
  247.6 6.5 %all-to-all-start = ((bf16[16,2,92160]{2,1,0:T(2,128)(2,1)}), bf16[16,2,92160]{2,1,0:T(2,128)(2,1)}, u32[]{:S(2)}, u32[]{:S(2)}) async-start(bf16[16,2,92160]{2,1,0:T(2,128)(2,1)} %reshape.65), calls=%async_computation.1 | async-start | bytes 11796480 | tf_op jit(solution)/shard_map/all_to_all | solution.py:28
  254.1 0.0 copy-start.4
  254.1 0.2 reduce-scatter.2.cloned.1.call-start
  254.3 0.0 all-gather.3.cloned.1.call-done
  254.4 0.0 copy-done.3
  254.4 14.0 %fusion.30 = f32[160,3072]{1,0:T(8,128)} fusion(bf16[160,3072]{1,0:T(8,128)(2,1)S(1)} %copy-done.3, bf16[3072,3072]{0,1:T(8,128)(2,1)} %all-gather.3.cloned.1.call-done), kind=kOutput, calls=%fused_computation.38 | convolution fusion | flops 3019898880 | bytes 21823488 | tf_op jit(solution)/shard_map/dot_general | solution.py:47
  268.4 0.0 copy-start.7
  268.4 0.0 copy-start.6
  268.4 0.0 copy-start.5
  268.4 0.0 reduce-scatter.2.cloned.1.call-update
  268.4 0.0 copy-done.4
  268.4 0.1 copy.36
  268.5 0.1 eq.29
  268.6 0.1 eq.25
  268.8 6.8 %reduce-window.6 = s32[24,15,128]{2,1,0:T(8,128)S(1)} reduce-window(s32[24,15,128]{2,1,0:T(8,128)S(1)} %fusion.25, s32[]{:T(128)} %constant.8.clone.1), window={size=1x1x128 pad=0_0x0_0x127_0}, to_apply=%region_1.2 | reduce-window | flops 5852160 | bytes 368644 | tf_op jit(solution)/shard_map/reduce-window
  275.6 0.1 slice.8
  275.7 0.2 copy.40
  275.9 0.1 copy.41
  276.0 0.1 broadcast_add_fusion
  276.1 0.1 fusion.28
  276.2 0.1 reshape.49
  276.4 0.1 copy.42
  276.5 0.0 copy-done.7
  276.5 0.1 multiply_reduce_fusion
  276.6 0.0 copy-done.6
  276.6 0.1 and_reduce_fusion
  276.7 0.1 copy.43
  276.8 0.1 reshape.57
  276.9 0.0 copy-done.5
  276.9 0.1 copy.44
  277.1 0.1 select_reduce_fusion
  277.2 0.1 reshape.59
  277.3 12.8 %scatter_custom_fusion = f32[307200]{0:T(1024)S(1)} fusion(s32[1920]{0:T(1024)S(1)} %reshape.57, f32[1920]{0:T(1024)S(1)} %reshape.59, f32[]{:T(128)} %constant.5.clone.1), kind=kCustom, calls=%fused_computation.16 | custom fusion | flops 1920 | bytes 1228804
  290.0 0.2 reshape.56
  290.3 0.0 copy-start.2
  290.3 92.8 %all-to-all-done = bf16[16,2,92160]{2,1,0:T(2,128)(2,1)} async-done(((bf16[16,2,92160]{2,1,0:T(2,128)(2,1)}), bf16[16,2,92160]{2,1,0:T(2,128)(2,1)}, u32[]{:S(2)}, u32[]{:S(2)}) %all-to-all-start) | async-done | bytes 5898272 | tf_op jit(solution)/shard_map/all_to_all | solution.py:28
  383.1 14.0 %reshape.66 = bf16[1920,1,1536]{2,1,0:T(2,128)(2,1)} reshape(bf16[16,2,92160]{2,1,0:T(2,128)(2,1)} %all-to-all-done) | data formatting | bytes 11796480
  397.1 0.0 copy-done.2
  397.1 6.5 %fusion.1 = f32[160,1536]{1,0:T(8,128)} fusion(bf16[1,1920,1536]{2,0,1:T(2,128)(2,1)} %bitcast.49, f32[160,1920]{1,0:T(8,128)S(1)} %reshape.56), kind=kOutput, calls=%fused_computation.3 | convolution fusion | flops 944947200 | bytes 8110080 | tf_op jit(solution)/shard_map/dot_general | solution.py:43
  403.6 0.0 reduce-scatter.2.cloned.1.call-done
  403.6 0.0 copy-start.1
  403.6 7.5 %fusion.16 = bf16[160,1536]{1,0:T(8,128)(2,1)} fusion(f32[160,1536]{1,0:T(8,128)} %reduce-scatter.2.cloned.1.call-done, f32[160,1536]{1,0:T(8,128)} %fusion.1, bf16[1,1920,1536]{2,0,1:T(2,128)(2,1)} %bitcast.50, bf16[160,1536]{1,0:T(8,128)(2,1)} %param.7, f32[160]{0:T(256)S(1)} %get-tuple-element.5, f32[160,1920]{1,0:T(8,128)} %copy-done.2), kind=kOutput, calls=%fused_computation.12 | convolution fusion | flops 945500160 | bytes 10076800 | tf_op jit(solution)/shard_map/dot_general | solution.py:42
  411.1 0.0 copy-done.1
  (5 shorter events, 0.1 us)
Async XLA Ops:
  6.5 57.3 %copy-start = (bf16[1,1024,1536]{2,1,0:T(8,128)(2,1)S(1)}, bf16[1,1024,1536]{2,1,0:T(8,128)(2,1)}, u32[]{:S(2)}) copy-start(bf16[1,1024,1536]{2,1,0:T(8,128)(2,1)} %param.11) | copy-start | bytes 9437188
  6.5 57.3 %all-gather.5.cloned.1.call-start = ((), (), s32[]{:S(2)}) async-start(), calls=%async_computation.4 | async-start | bytes 5898240 | tf_op jit(solution)/shard_map/all_gather | solution.py:24
  7.3 247.1 %all-gather.3.cloned.1.call-start = ((), (), s32[]{:S(2)}) async-start(), calls=%async_computation.2 | async-start | bytes 20054016 | tf_op jit(solution)/shard_map/all_gather | solution.py:46
  247.6 6.8 %copy-start.3 = (bf16[160,3072]{1,0:T(8,128)(2,1)S(1)}, bf16[160,3072]{1,0:T(8,128)(2,1)}, u32[]{:S(2)}) copy-start(bf16[160,3072]{1,0:T(8,128)(2,1)} %param.12) | copy-start | bytes 2949124
  247.6 135.5 %all-to-all-start = ((bf16[16,2,92160]{2,1,0:T(2,128)(2,1)}), bf16[16,2,92160]{2,1,0:T(2,128)(2,1)}, u32[]{:S(2)}, u32[]{:S(2)}) async-start(bf16[16,2,92160]{2,1,0:T(2,128)(2,1)} %reshape.65), calls=%async_computation.1 | async-start | bytes 11796480 | tf_op jit(solution)/shard_map/all_to_all | solution.py:28
  254.1 14.3 %copy-start.4 = (s32[160,12]{0,1:T(8,128)S(1)}, s32[160,12]{0,1:T(8,128)}, u32[]{:S(2)}) copy-start(s32[160,12]{0,1:T(8,128)} %param.8) | copy-start | bytes 23044
  254.1 149.5 %reduce-scatter.2.cloned.1.call-start = ((), (), s32[]{:S(2)}) async-start(), calls=%async_computation.3 | async-start | bytes 2949120 | tf_op jit(solution)/shard_map/reduce_scatter | solution.py:48
  268.4 8.1 %copy-start.7 = (s32[2]{0:T(128)S(1)}, s32[2]{0:T(128)}, u32[]{:S(2)}) copy-start(s32[2]{0:T(128)} %constant.20) | copy-start | bytes 28
  268.4 8.2 %copy-start.6 = (s32[2]{0:T(128)S(1)}, s32[2]{0:T(128)}, u32[]{:S(2)}) copy-start(s32[2]{0:T(128)} %constant.23) | copy-start | bytes 28
  268.4 8.6 %copy-start.5 = (f32[160,12]{0,1:T(8,128)S(1)}, f32[160,12]{0,1:T(8,128)}, u32[]{:S(2)}) copy-start(f32[160,12]{0,1:T(8,128)} %param.9) | copy-start | bytes 23044
  290.3 106.8 %copy-start.2 = (f32[160,1920]{1,0:T(8,128)}, f32[160,1920]{1,0:T(8,128)S(1)}, u32[]{:S(2)}) copy-start(f32[160,1920]{1,0:T(8,128)S(1)} %reshape.56) | copy-start | bytes 3686404
  403.6 7.5 %copy-start.1 = (bf16[1,1024,1536]{2,1,0:T(8,128)(2,1)S(1)}, bf16[1,1024,1536]{2,1,0:T(8,128)(2,1)}, u32[]{:S(2)}) copy-start(bf16[1,1024,1536]{2,1,0:T(8,128)(2,1)} %param.11) | copy-start | bytes 9437188
Sparse Core Ops, SparseCore 0:
  8.9 54.8 all-gather.4
  65.4 99.1 all-gather.2
  268.5 30.1 reduce-scatter.1
where the time goes:
time: 418 us
  waiting for transfers between devices  150 us (36%)
  other arithmetic  147 us (35%)
  local copies, waits for them, and re-layouts  64.4 us (15%)
  matrix products  36.6 us (9%)
  between operations  13.3 us (3%)
  starting transfers between devices  6.76 us (2%)
    unnamed x5, other arithmetic  139 us
    all_to_all x1, waiting for transfers between devices, local(): lax.all_to_all(outputs, 'ep', split_axis=1, concat_axis=0, tiled=True)  92.8 us
    all_gather x1, waiting for transfers between devices, local(): lax.all_gather(expert_hidden, 'tp', axis=1, tiled=True)  55.8 us
    convert_element_type x1, local copies, waits for them, and re-layouts, local(): outputs = jnp.einsum('esh,ehd->esd', lax.all_gather(expert_hidden, 'tp',...  36.6 us
    unnamed x23, local copies, waits for them, and re-layouts  26.7 us
    dot_general x1, matrix products, local(): jnp.dot(dense_hidden, columns, preferred_element_type=jnp.float32)  14 us
    dot_general x1, matrix products, local(): jnp.einsum('esh,ehd->esd', lax.all_gather(expert_hidden, 'tp', axis=1, ti...  8.62 us
  transfers between devices with their start and end apart: 4, of which 2 were waited for; matrix products, arithmetic and copies ran while one was open for 57% of the time, Pallas kernels for 0%

commit v1 on v0

v1 whole, which is shorter than its diff:
```python
import jax
import jax.numpy as jnp
from jax import lax
from jax.sharding import Mesh, PartitionSpec as P

F32 = jnp.float32
BF16 = jnp.bfloat16
SWAP = ((0, 1), (1, 0))


def pick(array, index, axis=0):
    return lax.dynamic_index_in_dim(array, index, axis, keepdims=False)


def gate_rows(expert_ids, gate_weights, experts):
    ids, gates = expert_ids.T, gate_weights.T
    labels = jnp.arange(experts, dtype=jnp.int32)[:, None, None]
    return jnp.max(jnp.where(ids[None] == labels, gates[None], F32(-1.0)), axis=1)


def spread_gates(rows, zs, y, z):
    c = lax.axis_index("c")
    rows = rows.reshape(zs, 2, 2, rows.shape[-1])
    mine = pick(rows, y, 1)
    other = lax.ppermute(pick(rows, 1 - y, 1), "y", SWAP)
    both = jnp.stack([jnp.where(y == 0, mine, other), jnp.where(y == 0, other, mine)], 1)
    both = jnp.stack([pick(both, c, 2), pick(both, 1 - c, 2)], 2)
    got = [pick(both, z)]
    for shift in range(1, zs):
        got.append(lax.ppermute(pick(both, (z + shift) % zs), "z", [(i, (i + shift) % zs) for i in range(zs)]))
    got = jnp.stack(got)
    return jnp.stack([pick(got, (z - i) % zs) for i in range(zs)])


def placement(gates, capacity):
    tokens = gates.shape[-1]
    picked = gates >= 0
    order = jnp.arange(tokens)
    earlier = (order[:, None] < order[None, :]).astype(BF16)
    slots = jnp.dot(picked.astype(BF16), earlier, preferred_element_type=F32).astype(jnp.int32)
    slots = jnp.where(picked, slots, -1)
    places = jnp.arange(capacity, dtype=jnp.int32)
    table = jnp.where(slots[..., None] == places, gates[..., None], F32(0.0))
    table = jnp.moveaxis(table, -3, -2)
    table = table.reshape(table.shape[:-2] + (2 * capacity,))
    high = table.astype(BF16)
    low = (table - high.astype(F32)).astype(BF16)
    return high, low


def local(tokens, expert_ids, gate_weights, expert_hidden, expert_down, dense_hidden, dense_down):
    zs, tp = lax.axis_size("z"), lax.axis_size("tp")
    z, y, c, x = (lax.axis_index(name) for name in ("z", "y", "c", "tp"))
    experts = zs * 4
    zt = zs // tp
    rows = tokens.shape[0]
    hidden, down = expert_hidden[0], expert_down[0]
    capacity = hidden.shape[0] // (zt * 4)
    features = down.shape[1]

    hidden = hidden.reshape(zt, 4 * capacity, hidden.shape[1])

    def turn(owner, k):
        return jnp.where(2 * owner < tp, k, zt - 1 - k)

    def turn_of(owner, k):
        return k if 2 * owner < tp else zt - 1 - k

    chunks = []
    for k in range(zt):
        chunks.append((0, k, pick(hidden, turn(x, k))))
    for shift in range(1, tp):
        for k in range(zt):
            sent = chunks[k][2]
            moved = lax.ppermute(sent, "tp", [((i + shift) % tp, i) for i in range(tp)])
            chunks.append((shift, k, moved))

    right = [(i, i + 1) for i in range(zs - 1)]
    left = [(i + 1, i) for i in range(zs - 1)]
    acts = jnp.stack([dense_hidden, lax.ppermute(dense_hidden, "y", SWAP)])
    acts = acts.reshape(2 * rows, -1)
    columns = dense_down.shape[1]

    def product(weights):
        sibling = lax.ppermute(weights, "c", SWAP)
        first = jnp.where(c == 0, weights, sibling)
        second = jnp.where(c == 0, sibling, weights)
        both = jnp.concatenate([first, second], 1)
        return jnp.dot(acts, both, preferred_element_type=F32).astype(BF16)

    sheet = jnp.zeros((zs, 2 * rows, 2 * columns), BF16)
    if zs <= 4:
        sheet = lax.dynamic_update_index_in_dim(sheet, product(dense_down), z, 0)
        from_left = from_right = dense_down
        for step in range(1, zs):
            from_left = lax.ppermute(from_left, "z", right)
            from_right = lax.ppermute(from_right, "z", left)
            for value, at in ((from_left, z - step), (from_right, z + step)):
                inside = (at >= 0) & (at < zs)
                at = jnp.clip(at, 0, zs - 1)
                value = jnp.where(inside, product(value), pick(sheet, at))
                sheet = lax.dynamic_update_index_in_dim(sheet, value, at, 0)
    else:
        every = lax.all_gather(dense_down, "z")
        for i in range(zs):
            sheet = lax.dynamic_update_index_in_dim(sheet, product(every[i]), i, 0)

    gates = spread_gates(gate_rows(expert_ids, gate_weights, experts), zs, y, z)
    high, low = placement(gates, capacity)

    def partial_sum(chunk, at):
        out = jnp.dot(chunk, down, preferred_element_type=F32).astype(BF16)
        out = out.reshape(2, 2, capacity, features)
        sibling = lax.ppermute(pick(out, 1 - c, 1), "c", SWAP)
        table = jnp.concatenate([pick(out, c, 1), sibling], 1)
        p_high, p_low = pick(high, at), pick(low, at)

        def combined(which):
            t = pick(table, which)
            return jnp.dot(pick(p_high, which), t, preferred_element_type=F32) + jnp.dot(
                pick(p_low, which), t, preferred_element_type=F32
            )

        sent = lax.ppermute(combined(1 - y).astype(BF16), "y", SWAP)
        return combined(y) + sent.astype(F32)

    routed = jnp.zeros((rows, features), F32)
    if zs <= 4:
        for shift, k, chunk in chunks:
            owner = (x + shift) % tp
            at = owner * zt + turn(owner, k)
            total = partial_sum(chunk, at)
            goals = [((i + shift) % tp) * zt + turn_of((i + shift) % tp, k) for i in range(tp)]
            for distance in range(zs - 1, 0, -1):
                sent = total.astype(BF16)
                first, second = {}, {}
                for i in range(tp):
                    for way in (1, -1):
                        start = goals[i] - way * distance
                        if 0 <= start < zs:
                            end = (start + way) * tp + i
                            (second if end in first else first)[end] = start * tp + i
                for links in (first, second):
                    if links:
                        moved = lax.ppermute(sent, ("z", "tp"), [(a, b) for b, a in links.items()])
                        total = total + moved.astype(F32)
            routed = jnp.where(z == at, total, routed)
    else:
        totals = jnp.zeros((zs, rows, features), BF16)
        for shift, k, chunk in chunks:
            owner = (x + shift) % tp
            at = owner * zt + turn(owner, k)
            totals = lax.dynamic_update_index_in_dim(totals, partial_sum(chunk, at).astype(BF16), at, 0)
        routed = lax.psum_scatter(totals, "z", scatter_dimension=0).astype(F32)

    sheet = sheet.reshape(tp, zt, 2 * rows, 2 * columns)
    dense = pick(sheet, x).astype(F32)
    for shift in range(1, tp):
        sent = pick(sheet, (x + shift) % tp)
        dense = dense + lax.ppermute(sent, "tp", [(i, (i + shift) % tp) for i in range(tp)]).astype(F32)
    dense = dense.reshape(zt, 2, rows, 2 * columns)
    theirs = lax.ppermute(dense[:, 1].astype(BF16), "y", SWAP).astype(F32)
    mine = dense[:, 0]
    both = jnp.stack([jnp.where(y == 0, mine, theirs), jnp.where(y == 0, theirs, mine)], 1)
    dense = jnp.moveaxis(both, 2, 0).reshape(rows, features)

    zero_gate = jnp.sum(jnp.where(expert_ids < experts, F32(0.0), gate_weights), axis=1)
    identity = zero_gate[:, None] * tokens.astype(F32)
    return (dense + routed + identity).astype(BF16)


def solution(mesh):
    groups, ranks, tp = mesh.devices.shape
    split = Mesh(mesh.devices.reshape(groups, ranks // 4, 2, 2, tp), ("grp", "z", "y", "c", "tp"))
    ep = ("z", "y", "c")
    return jax.shard_map(
        local,
        mesh=split,
        in_specs=(
            P(("grp",) + ep, "tp"),
            P(("grp",) + ep, None),
            P(("grp",) + ep, None),
            P(ep, ("grp", "tp"), None),
            P(ep, None, "tp"),
            P(("grp",) + ep, "tp"),
            P("tp", ep),
        ),
        out_specs=P(("grp",) + ep, "tp"),
        check_vma=False,
    )
```

time: 418 us -> 327 us (0.78)
  the two profiles are of different devices: /device:TPU:13 before, /device:TPU:24 now
where the time goes in v1:
time: 327 us; the launch traced here: 326 us
  waiting for transfers between devices  134 us (41%)
  starting transfers between devices  111 us (34%)
  matrix products  30.6 us (9%)
  local copies, waits for them, and re-layouts  29.5 us (9%)
  other arithmetic  20.2 us (6%)
    ppermute x1, starting transfers between devices, local(): lax.ppermute(sent, 'tp', [(i, (i + shift) % tp) for i in range(tp)])  55.1 us
    ppermute x2, waiting for transfers between devices, local(): moved = lax.ppermute(sent, 'tp', [((i + shift) % tp, i) for i in range(tp)])  31.4 us
    ppermute x4, waiting for transfers between devices, partial_sum(): sent = lax.ppermute(combined(1 - y).astype(BF16), 'y', SWAP)  25.7 us
    ppermute x12, starting transfers between devices, local(): moved = lax.ppermute(sent, ('z', 'tp'), [(a, b) for b, a in links.items()])  20.2 us
    ppermute x12, waiting for transfers between devices, local(): moved = lax.ppermute(sent, ('z', 'tp'), [(a, b) for b, a in links.items()])  17.6 us
    ppermute x3, waiting for transfers between devices, local(): from_left = lax.ppermute(from_left, 'z', right)  16.5 us
    ppermute x3, waiting for transfers between devices, local(): from_right = lax.ppermute(from_right, 'z', left)  15.9 us
    ppermute x3, starting transfers between devices, local(): from_right = lax.ppermute(from_right, 'z', left)  14.5 us
  transfers between devices with their start and end apart: 42, of which 16 were waited for; matrix products, arithmetic and copies ran while one was open for 22% of the time, Pallas kernels for 0%

profile of v1, /device:TPU:24, one launch (start us, length us, event | category | flops | bytes accessed | tf_op | source)
XLA Modules:
  0.0 325.5 jit_solution(6687381653121406464)
XLA Ops:
  0.0 1.6 collective-permute-start.2
  2.4 1.6 collective-permute-start.16
  4.0 1.7 dynamic-slice_bitcast_fusion.1
  5.7 2.8 fusion.17
  8.5 2.8 fusion.14
  11.3 2.7 dynamic-slice_bitcast_fusion.2
  14.0 1.3 dynamic-slice_bitcast_fusion.4
  15.4 2.7 collective-permute-start.19
  18.1 1.4 collective-permute-start.18
  19.4 1.5 collective-permute-start.17
  21.0 9.7 %collective-permute-done.19 = f32[2,2,160]{2,1,0:T(2,128)S(1)} collective-permute-done((f32[2,2,160]{2,1,0:T(2,128)S(1)}, f32[2,2,160]{2,1,0:T(2,128)S(1)}, u32[]{:S(2)}, u32[]{:S(2)}) %collective-permute-start.19) | collective-permute-done | bytes 2592 | tf_op jit(solution)/shard_map/ppermute | solution.py:30
  30.7 2.3 collective-permute-start.4
  34.8 3.9 %broadcast_in_dim.85 = f32[4,2,160,2,120]{4,3,2,1,0:T(2,128)} broadcast(f32[4,2,160,2]{3,2,1,0:T(8,128)} %copy.25), dimensions={0,1,2,3} | broadcast | bytes 1239040 | tf_op jit(solution)/shard_map/jit(_where)/broadcast_in_dim | solution.py:43
  38.6 2.9 broadcast_in_dim.86
  42.8 5.7 %eq.90 = s32[4,2,160,2,120]{4,3,2,1,0:T(2,128)} broadcast(s32[4,2,160,2]{3,2,1,0:T(8,128)} %copy.24), dimensions={0,1,2,3} | broadcast | bytes 1239040 | tf_op jit(solution)/shard_map/eq | solution.py:43
  48.5 2.9 eq.91
  51.4 2.1 subtract_convert_fusion
  55.1 1.5 collective-permute-start.26
  56.6 1.3 fusion.165
  57.9 1.4 fusion.168
  59.9 1.3 fusion.171
  61.2 1.3 fusion.174
  62.5 1.3 fusion.27
  63.8 1.4 fusion.26
  65.2 14.5 %collective-permute-done.26 = bf16[480,1024]{1,0:T(8,128)(2,1)S(1)} collective-permute-done((bf16[480,1024]{1,0:T(8,128)(2,1)S(1)}, bf16[480,1024]{1,0:T(8,128)(2,1)S(1)}, u32[]{:S(2)}, u32[]{:S(2)}) %collective-permute-start.26) | collective-permute-done | bytes 983072 | tf_op jit(solution)/shard_map/ppermute | solution.py:75
  79.7 1.5 collective-permute-start
  81.2 1.7 fusion.11
  83.1 16.8 %collective-permute-done.20 = bf16[480,1024]{1,0:T(8,128)(2,1)S(1)} collective-permute-done((bf16[480,1024]{1,0:T(8,128)(2,1)S(1)}, bf16[480,1024]{1,0:T(8,128)(2,1)S(1)}, u32[]{:S(2)}, u32[]{:S(2)}) %collective-permute-start.20) | collective-permute-done | bytes 983072 | tf_op jit(solution)/shard_map/ppermute | solution.py:75
  99.9 1.5 collective-permute-start.38
  101.4 1.7 fusion.8
  105.2 1.4 broadcast_select_fusion.13
  106.6 7.5 %collective-permute-done.38 = bf16[160,1536]{1,0:T(8,128)(2,1)S(1)} collective-permute-done((bf16[160,1536]{1,0:T(8,128)(2,1)S(1)}, bf16[160,1536]{1,0:T(8,128)(2,1)S(1)}, u32[]{:S(2)}, u32[]{:S(2)}) %collective-permute-start.38) | collective-permute-done | bytes 491552 | tf_op jit(solution)/shard_map/ppermute | solution.py:124
  114.1 1.3 fusion.257
  115.4 1.3 collective-permute-start.39
  118.2 4.7 %collective-permute-done.33 = bf16[160,1536]{1,0:T(8,128)(2,1)S(1)} collective-permute-done((bf16[160,1536]{1,0:T(8,128)(2,1)S(1)}, bf16[160,1536]{1,0:T(8,128)(2,1)S(1)}, u32[]{:S(2)}, u32[]{:S(2)}) %collective-permute-start.33) | collective-permute-done | bytes 491552 | tf_op jit(solution)/shard_map/ppermute | solution.py:124
  122.8 1.3 fusion.258
  124.1 1.3 collective-permute-start.6
  126.2 4.3 %collective-permute-start.34 = (bf16[160,1536]{1,0:T(8,128)(2,1)S(1)}, bf16[160,1536]{1,0:T(8,128)(2,1)S(1)}, u32[]{:S(2)}, u32[]{:S(2)}) collective-permute-start(bf16[160,1536]{1,0:T(8,128)(2,1)S(1)} %get-tuple-element.47), channel_id=1, source_target_pairs={{24,16},{1,9},{26,18},{3,11},{28,20},{5,13},{30,22},{7,15}} | collective-permute-start | bytes 1474568 | tf_op jit(solution)/shard_map/ppermute | solution.py:145
  131.4 10.0 %collective-permute-done.34 = bf16[160,1536]{1,0:T(8,128)(2,1)S(1)} collective-permute-done((bf16[160,1536]{1,0:T(8,128)(2,1)S(1)}, bf16[160,1536]{1,0:T(8,128)(2,1)S(1)}, u32[]{:S(2)}, u32[]{:S(2)}) %collective-permute-start.34) | collective-permute-done | bytes 491552 | tf_op jit(solution)/shard_map/ppermute | solution.py:145
  143.0 1.5 collective-permute-start.28
  146.9 10.2 %collective-permute-done.28 = bf16[160,1536]{1,0:T(8,128)(2,1)S(1)} collective-permute-done((bf16[160,1536]{1,0:T(8,128)(2,1)S(1)}, bf16[160,1536]{1,0:T(8,128)(2,1)S(1)}, u32[]{:S(2)}, u32[]{:S(2)}) %collective-permute-start.28) | collective-permute-done | bytes 491552 | tf_op jit(solution)/shard_map/ppermute | solution.py:124
  157.1 5.3 %collective-permute-start.8 = (bf16[3072,192]{0,1:T(8,128)(2,1)}, bf16[3072,192]{0,1:T(8,128)(2,1)S(1)}, u32[]{:S(2)}, u32[]{:S(2)}) collective-permute-start(bf16[3072,192]{0,1:T(8,128)(2,1)} %collective-permute-done.4), channel_id=1, source_target_pairs={{8,0},{16,8},{24,16},{9,1},{17,9},{25,17},{10,2},{18,10},{26,18},{... | collective-permute-start | bytes 3538952 | tf_op jit(solution)/shard_map/ppermute | solution.py:97
  162.8 3.3 %collective-permute-done.22 = bf16[160,1536]{1,0:T(8,128)(2,1)S(1)} collective-permute-done((bf16[160,1536]{1,0:T(8,128)(2,1)S(1)}, bf16[160,1536]{1,0:T(8,128)(2,1)S(1)}, u32[]{:S(2)}, u32[]{:S(2)}) %collective-permute-start.22) | collective-permute-done | bytes 491552 | tf_op jit(solution)/shard_map/ppermute | solution.py:124
  167.1 1.5 collective-permute-start.35
  168.6 1.4 broadcast_select_fusion.11
  170.8 1.4 broadcast_select_fusion.9
  173.6 1.2 fusion.100
  174.9 1.5 collective-permute-start.41
  176.4 8.4 %collective-permute-done.8 = bf16[3072,192]{0,1:T(8,128)(2,1)S(1)} collective-permute-done((bf16[3072,192]{0,1:T(8,128)(2,1)}, bf16[3072,192]{0,1:T(8,128)(2,1)S(1)}, u32[]{:S(2)}, u32[]{:S(2)}) %collective-permute-start.8) | collective-permute-done | bytes 1179680 | tf_op jit(solution)/shard_map/ppermute | solution.py:97
  184.8 1.3 collective-permute-start.10
  187.7 1.4 collective-permute-done.9
  189.1 6.9 %collective-permute-start.12 = (bf16[3072,192]{0,1:T(8,128)(2,1)S(1)}, bf16[3072,192]{0,1:T(8,128)(2,1)S(1)}, u32[]{:S(2)}, u32[]{:S(2)}) collective-permute-start(bf16[3072,192]{0,1:T(8,128)(2,1)S(1)} %collective-permute-done.8), channel_id=1, source_target_pairs={{8,0},{16,8},{24,16},{9,1},{17,9},{25,17},{10,2},{18,10},{26,18},{... | collective-permute-start | bytes 3538952 | tf_op jit(solution)/shard_map/ppermute | solution.py:97
  195.9 16.5 %collective-permute-done.10 = bf16[3072,192]{0,1:T(8,128)(2,1)S(1)} collective-permute-done((bf16[3072,192]{0,1:T(8,128)(2,1)S(1)}, bf16[3072,192]{0,1:T(8,128)(2,1)S(1)}, u32[]{:S(2)}, u32[]{:S(2)}) %collective-permute-start.10) | collective-permute-done | bytes 1179680 | tf_op jit(solution)/shard_map/ppermute | solution.py:96
  213.8 7.5 %collective-permute-done.12 = bf16[3072,192]{0,1:T(8,128)(2,1)S(1)} collective-permute-done((bf16[3072,192]{0,1:T(8,128)(2,1)S(1)}, bf16[3072,192]{0,1:T(8,128)(2,1)S(1)}, u32[]{:S(2)}, u32[]{:S(2)}) %collective-permute-start.12) | collective-permute-done | bytes 1179680 | tf_op jit(solution)/shard_map/ppermute | solution.py:97
  223.6 1.4 collective-permute-done.13
  227.2 55.1 %collective-permute-start.14 = (bf16[2,320,384]{2,1,0:T(8,128)(2,1)S(1)}, bf16[2,320,384]{2,1,0:T(8,128)(2,1)S(1)}, u32[]{:S(2)}, u32[]{:S(2)}) collective-permute-start(bf16[2,320,384]{2,1,0:T(8,128)(2,1)S(1)} %dynamic-slice_bitcast_fusion.10), channel_id=1, source_target_pairs={{0,1},{1,0},{2,3},{3,2},{4,5},{5,4},{6,7},{7,6},{8,9},{9,8},{10,11... | collective-permute-start | bytes 1474568 | tf_op jit(solution)/shard_map/ppermute | solution.py:160
  283.2 10.2 %collective-permute-done.14 = bf16[2,320,384]{2,1,0:T(8,128)(2,1)S(1)} collective-permute-done((bf16[2,320,384]{2,1,0:T(8,128)(2,1)S(1)}, bf16[2,320,384]{2,1,0:T(8,128)(2,1)S(1)}, u32[]{:S(2)}, u32[]{:S(2)}) %collective-permute-start.14) | collective-permute-done | bytes 491552 | tf_op jit(solution)/shard_map/ppermute | solution.py:160
  293.4 5.2 %collective-permute-start.25 = (bf16[160,1536]{1,0:T(8,128)(2,1)}, bf16[160,1536]{1,0:T(8,128)(2,1)}, u32[]{:S(2)}, u32[]{:S(2)}) collective-permute-start(bf16[160,1536]{1,0:T(8,128)(2,1)} %fusion.155), channel_id=1, source_target_pairs={{24,16},{17,9},{26,18},{19,11},{28,20},{21,13},{30,22},{23,15}} | collective-permute-start | bytes 1474568 | tf_op jit(solution)/shard_map/ppermute | solution.py:145
  300.5 1.5 collective-permute-start.24
  301.9 3.9 %collective-permute-done.15 = bf16[2,160,384]{2,0,1:T(2,128)(2,1)S(1)} collective-permute-done((bf16[2,160,384]{2,0,1:T(2,128)(2,1)S(1)}, bf16[2,160,384]{2,0,1:T(2,128)(2,1)S(1)}, u32[]{:S(2)}, u32[]{:S(2)}) %collective-permute-start.15) | collective-permute-done | bytes 245792 | tf_op jit(solution)/shard_map/ppermute | solution.py:162
  305.8 1.5 collective-permute-start.31
  309.8 1.8 reshape.74
  311.6 7.5 %collective-permute-done.31 = bf16[160,1536]{1,0:T(8,128)(2,1)} collective-permute-done((bf16[160,1536]{1,0:T(8,128)(2,1)}, bf16[160,1536]{1,0:T(8,128)(2,1)}, u32[]{:S(2)}, u32[]{:S(2)}) %collective-permute-start.31) | collective-permute-done | bytes 491552 | tf_op jit(solution)/shard_map/ppermute | solution.py:145
  319.1 6.4 %add_convert_fusion = bf16[160,1536]{1,0:T(8,128)(2,1)} fusion(bf16[160,1536]{1,0:T(8,128)(2,1)} %param.7, f32[160,1536]{1,0:T(8,128)} %reshape.74, bf16[160,1536]{1,0:T(8,128)(2,1)} %collective-permute-done.41, bf16[160,1536]{1,0:T(8,128)(2,1)} %copy-done.23, bf16[160,1536]{1,0:T(8,128)(2,1)} %collective-permute-done.35, ...), kind=kLoop, calls=%fused_computation.121 | loop fusion | flops 8110080 | bytes 11797124 | tf_op jit(solution)/shard_map/convert_element_type | solution.py:169
  (164 shorter events, 31.3 us)
Async XLA Ops:
  0.0 5.7 %copy-start = (bf16[1,1024,1536]{2,1,0:T(8,128)(2,1)S(1)}, bf16[1,1024,1536]{2,1,0:T(8,128)(2,1)}, u32[]{:S(2)}) copy-start(bf16[1,1024,1536]{2,1,0:T(8,128)(2,1)} %param.11) | copy-start | bytes 9437188
  0.0 104.1 %collective-permute-start.1 = (bf16[3072,192]{0,1:T(8,128)(2,1)}, bf16[3072,192]{0,1:T(8,128)(2,1)}, u32[]{:S(2)}, u32[]{:S(2)}) collective-permute-start(bf16[3072,192]{0,1:T(8,128)(2,1)} %param.13), channel_id=1, source_target_pairs={{0,2},{2,0},{1,3},{3,1},{4,6},{6,4},{5,7},{7,5},{8,10},{10,8},{9,1... | collective-permute-start | bytes 3538952 | tf_op jit(solution)/shard_map/ppermute | solution.py:85
  0.0 118.1 %collective-permute-start.2 = (bf16[3072,192]{0,1:T(8,128)(2,1)}, bf16[3072,192]{0,1:T(8,128)(2,1)}, u32[]{:S(2)}, u32[]{:S(2)}) collective-permute-start(bf16[3072,192]{0,1:T(8,128)(2,1)} %param.13), channel_id=1, source_target_pairs={{0,8},{8,16},{16,24},{1,9},{9,17},{17,25},{2,10},{10,18},{18,26},{... | collective-permute-start | bytes 3538952 | tf_op jit(solution)/shard_map/ppermute | solution.py:96
  2.4 12.9 %collective-permute-start.16 = (f32[4,2,160]{2,0,1:T(4,128)S(1)}, f32[4,2,160]{2,0,1:T(4,128)S(1)}, u32[]{:S(2)}, u32[]{:S(2)}) collective-permute-start(f32[4,2,160]{2,0,1:T(4,128)S(1)} %bitcast.269), channel_id=1, source_target_pairs={{0,4},{4,0},{1,5},{5,1},{2,6},{6,2},{3,7},{7,3},{8,12},{12,8},{9,1... | collective-permute-start | bytes 15368 | tf_op jit(solution)/shard_map/ppermute | solution.py:25
  5.7 2.8 copy-start.20
  5.7 2.8 copy-start.18
  11.3 2.7 copy-start.16
  15.4 15.3 %collective-permute-start.19 = (f32[2,2,160]{2,1,0:T(2,128)S(1)}, f32[2,2,160]{2,1,0:T(2,128)S(1)}, u32[]{:S(2)}, u32[]{:S(2)}) collective-permute-start(f32[2,2,160]{2,1,0:T(2,128)S(1)} %bitcast.272), channel_id=1, source_target_pairs={{0,24},{8,0},{16,8},{24,16},{1,25},{9,1},{17,9},{25,17},{2,26},{10... | collective-permute-start | bytes 7688 | tf_op jit(solution)/shard_map/ppermute | solution.py:30
  18.1 14.9 %collective-permute-start.18 = (f32[2,2,160]{2,1,0:T(2,128)S(1)}, f32[2,2,160]{2,1,0:T(2,128)S(1)}, u32[]{:S(2)}, u32[]{:S(2)}) collective-permute-start(f32[2,2,160]{2,1,0:T(2,128)S(1)} %bitcast.271), channel_id=1, source_target_pairs={{0,16},{8,24},{16,0},{24,8},{1,17},{9,25},{17,1},{25,9},{2,18},{10... | collective-permute-start | bytes 7688 | tf_op jit(solution)/shard_map/ppermute | solution.py:30
  19.4 13.6 %collective-permute-start.17 = (f32[2,2,160]{2,1,0:T(2,128)S(1)}, f32[2,2,160]{2,1,0:T(2,128)S(1)}, u32[]{:S(2)}, u32[]{:S(2)}) collective-permute-start(f32[2,2,160]{2,1,0:T(2,128)S(1)} %bitcast.270), channel_id=1, source_target_pairs={{0,8},{8,16},{16,24},{24,0},{1,9},{9,17},{17,25},{25,1},{2,10},{10... | collective-permute-start | bytes 7688 | tf_op jit(solution)/shard_map/ppermute | solution.py:30
  30.7 93.5 %collective-permute-start.4 = (bf16[3072,192]{0,1:T(8,128)(2,1)}, bf16[3072,192]{0,1:T(8,128)(2,1)}, u32[]{:S(2)}, u32[]{:S(2)}) collective-permute-start(bf16[3072,192]{0,1:T(8,128)(2,1)} %param.13), channel_id=1, source_target_pairs={{8,0},{16,8},{24,16},{9,1},{17,9},{25,17},{10,2},{18,10},{26,18},{... | collective-permute-start | bytes 3538952 | tf_op jit(solution)/shard_map/ppermute | solution.py:97
  33.0 21.2 %collective-permute-start.37 = (bf16[2,120,1536]{2,1,0:T(8,128)(2,1)}, bf16[2,120,1536]{2,1,0:T(8,128)(2,1)}, u32[]{:S(2)}, u32[]{:S(2)}) collective-permute-start(bf16[2,120,1536]{2,1,0:T(8,128)(2,1)} %get-tuple-element.27), channel_id=1, source_target_pairs={{0,2},{2,0},{1,3},{3,1},{4,6},{6,4},{5,7},{7,5},{8,10},{10,8},{9,1... | collective-permute-start | bytes 2211848 | tf_op jit(solution)/shard_map/ppermute | solution.py:114
  33.0 26.3 %collective-permute-start.32 = (bf16[2,120,1536]{2,1,0:T(8,128)(2,1)}, bf16[2,120,1536]{2,1,0:T(8,128)(2,1)}, u32[]{:S(2)}, u32[]{:S(2)}) collective-permute-start(bf16[2,120,1536]{2,1,0:T(8,128)(2,1)} %get-tuple-element.25), channel_id=1, source_target_pairs={{0,2},{2,0},{1,3},{3,1},{4,6},{6,4},{5,7},{7,5},{8,10},{10,8},{9,1... | collective-permute-start | bytes 2211848 | tf_op jit(solution)/shard_map/ppermute | solution.py:114
  51.4 2.1 copy-start.6
  51.4 2.5 copy-start.7
  53.9 2.7 copy-start.3
  55.1 24.6 %collective-permute-start.26 = (bf16[480,1024]{1,0:T(8,128)(2,1)S(1)}, bf16[480,1024]{1,0:T(8,128)(2,1)S(1)}, u32[]{:S(2)}, u32[]{:S(2)}) collective-permute-start(bf16[480,1024]{1,0:T(8,128)(2,1)S(1)} %copy-done.21), channel_id=1, source_target_pairs={{1,0},{0,1},{3,2},{2,3},{5,4},{4,5},{7,6},{6,7},{9,8},{8,9},{11,10... | collective-permute-start | bytes 2949128 | tf_op jit(solution)/shard_map/ppermute | solution.py:75
  59.3 40.6 %collective-permute-start.20 = (bf16[480,1024]{1,0:T(8,128)(2,1)S(1)}, bf16[480,1024]{1,0:T(8,128)(2,1)S(1)}, u32[]{:S(2)}, u32[]{:S(2)}) collective-permute-start(bf16[480,1024]{1,0:T(8,128)(2,1)S(1)} %copy-done.19), channel_id=1, source_target_pairs={{1,0},{0,1},{3,2},{2,3},{5,4},{4,5},{7,6},{6,7},{9,8},{8,9},{11,10... | collective-permute-start | bytes 2949128 | tf_op jit(solution)/shard_map/ppermute | solution.py:75
  63.8 15.9 %copy-start.22 = (bf16[160,3072]{1,0:T(8,128)(2,1)S(1)}, bf16[160,3072]{1,0:T(8,128)(2,1)}, u32[]{:S(2)}) copy-start(bf16[160,3072]{1,0:T(8,128)(2,1)} %param.12) | copy-start | bytes 2949124
  79.7 23.6 %collective-permute-start = (bf16[160,3072]{1,0:T(8,128)(2,1)S(1)}, bf16[160,3072]{1,0:T(8,128)(2,1)S(1)}, u32[]{:S(2)}, u32[]{:S(2)}) collective-permute-start(bf16[160,3072]{1,0:T(8,128)(2,1)S(1)} %copy-done.22), channel_id=1, source_target_pairs={{0,4},{4,0},{1,5},{5,1},{2,6},{6,2},{3,7},{7,3},{8,12},{12,8},{9,1... | collective-permute-start | bytes 2949128 | tf_op jit(solution)/shard_map/ppermute | solution.py:80
  99.9 14.2 %collective-permute-start.38 = (bf16[160,1536]{1,0:T(8,128)(2,1)S(1)}, bf16[160,1536]{1,0:T(8,128)(2,1)S(1)}, u32[]{:S(2)}, u32[]{:S(2)}) collective-permute-start(bf16[160,1536]{1,0:T(8,128)(2,1)S(1)} %fusion.27), channel_id=1, source_target_pairs={{0,4},{4,0},{1,5},{5,1},{2,6},{6,2},{3,7},{7,3},{8,12},{12,8},{9,1... | collective-permute-start | bytes 1474568 | tf_op jit(solution)/shard_map/ppermute | solution.py:124
  103.3 19.5 %collective-permute-start.33 = (bf16[160,1536]{1,0:T(8,128)(2,1)S(1)}, bf16[160,1536]{1,0:T(8,128)(2,1)S(1)}, u32[]{:S(2)}, u32[]{:S(2)}) collective-permute-start(bf16[160,1536]{1,0:T(8,128)(2,1)S(1)} %fusion.26), channel_id=1, source_target_pairs={{0,4},{4,0},{1,5},{5,1},{2,6},{6,2},{3,7},{7,3},{8,12},{12,8},{9,1... | collective-permute-start | bytes 1474568 | tf_op jit(solution)/shard_map/ppermute | solution.py:124
  104.1 22.1 %collective-permute-start.27 = (bf16[2,120,1536]{2,1,0:T(8,128)(2,1)S(1)}, bf16[2,120,1536]{2,1,0:T(8,128)(2,1)S(1)}, u32[]{:S(2)}, u32[]{:S(2)}) collective-permute-start(bf16[2,120,1536]{2,1,0:T(8,128)(2,1)S(1)} %get-tuple-element.23), channel_id=1, source_target_pairs={{0,2},{2,0},{1,3},{3,1},{4,6},{6,4},{5,7},{7,5},{8,10},{10,8},{9,1... | collective-permute-start | bytes 2211848 | tf_op jit(solution)/shard_map/ppermute | solution.py:114
  115.4 30.6 %copy-start.4 = (f32[160,1536]{1,0:T(8,128)}, f32[160,1536]{1,0:T(8,128)S(1)}, u32[]{:S(2)}) copy-start(f32[160,1536]{1,0:T(8,128)S(1)} %get-tuple-element.46) | copy-start | bytes 2949124
  115.4 10.1 %collective-permute-start.39 = (bf16[160,1536]{1,0:T(8,128)(2,1)S(1)}, bf16[160,1536]{1,0:T(8,128)(2,1)S(1)}, u32[]{:S(2)}, u32[]{:S(2)}) collective-permute-start(bf16[160,1536]{1,0:T(8,128)(2,1)S(1)} %get-tuple-element.45), channel_id=1, source_target_pairs={{24,16},{1,9},{26,18},{3,11},{28,20},{5,13},{30,22},{7,15}} | collective-permute-start | bytes 1474568 | tf_op jit(solution)/shard_map/ppermute | solution.py:145
  118.1 24.9 %collective-permute-start.21 = (bf16[2,120,1536]{2,1,0:T(8,128)(2,1)S(1)}, bf16[2,120,1536]{2,1,0:T(8,128)(2,1)S(1)}, u32[]{:S(2)}, u32[]{:S(2)}) collective-permute-start(bf16[2,120,1536]{2,1,0:T(8,128)(2,1)S(1)} %get-tuple-element.21), channel_id=1, source_target_pairs={{0,2},{2,0},{1,3},{3,1},{4,6},{6,4},{5,7},{7,5},{8,10},{10,8},{9,1... | collective-permute-start | bytes 2211848 | tf_op jit(solution)/shard_map/ppermute | solution.py:114
  122.8 44.3 %collective-permute-start.3 = (bf16[3072,192]{0,1:T(8,128)(2,1)}, bf16[3072,192]{0,1:T(8,128)(2,1)S(1)}, u32[]{:S(2)}, u32[]{:S(2)}) collective-permute-start(bf16[3072,192]{0,1:T(8,128)(2,1)} %collective-permute-done.2), channel_id=1, source_target_pairs={{0,2},{2,0},{1,3},{3,1},{4,6},{6,4},{5,7},{7,5},{8,10},{10,8},{9,1... | collective-permute-start | bytes 3538952 | tf_op jit(solution)/shard_map/ppermute | solution.py:85
  124.1 17.9 %copy-start.8 = (f32[160,1536]{1,0:T(8,128)}, f32[160,1536]{1,0:T(8,128)S(1)}, u32[]{:S(2)}) copy-start(f32[160,1536]{1,0:T(8,128)S(1)} %get-tuple-element.48) | copy-start | bytes 2949124
  124.1 48.0 %collective-permute-start.6 = (bf16[3072,192]{0,1:T(8,128)(2,1)}, bf16[3072,192]{0,1:T(8,128)(2,1)S(1)}, u32[]{:S(2)}, u32[]{:S(2)}) collective-permute-start(bf16[3072,192]{0,1:T(8,128)(2,1)} %collective-permute-done.2), channel_id=1, source_target_pairs={{0,8},{8,16},{16,24},{1,9},{9,17},{17,25},{2,10},{10,18},{18,26},{... | collective-permute-start | bytes 3538952 | tf_op jit(solution)/shard_map/ppermute | solution.py:96
  125.5 20.5 %copy-start.10 = (bf16[160,1536]{1,0:T(8,128)(2,1)}, bf16[160,1536]{1,0:T(8,128)(2,1)S(1)}, u32[]{:S(2)}) copy-start(bf16[160,1536]{1,0:T(8,128)(2,1)S(1)} %collective-permute-done.39) | copy-start | bytes 1474564
  125.5 44.6 %collective-permute-start.5 = (bf16[3072,192]{0,1:T(8,128)(2,1)}, bf16[3072,192]{0,1:T(8,128)(2,1)S(1)}, u32[]{:S(2)}, u32[]{:S(2)}) collective-permute-start(bf16[3072,192]{0,1:T(8,128)(2,1)} %collective-permute-done.4), channel_id=1, source_target_pairs={{0,2},{2,0},{1,3},{3,1},{4,6},{6,4},{5,7},{7,5},{8,10},{10,8},{9,1... | collective-permute-start | bytes 3538952 | tf_op jit(solution)/shard_map/ppermute | solution.py:85
  126.2 15.2 %collective-permute-start.34 = (bf16[160,1536]{1,0:T(8,128)(2,1)S(1)}, bf16[160,1536]{1,0:T(8,128)(2,1)S(1)}, u32[]{:S(2)}, u32[]{:S(2)}) collective-permute-start(bf16[160,1536]{1,0:T(8,128)(2,1)S(1)} %get-tuple-element.47), channel_id=1, source_target_pairs={{24,16},{1,9},{26,18},{3,11},{28,20},{5,13},{30,22},{7,15}} | collective-permute-start | bytes 1474568 | tf_op jit(solution)/shard_map/ppermute | solution.py:145
  141.4 3.5 %copy-start.14 = (bf16[160,1536]{1,0:T(8,128)(2,1)}, bf16[160,1536]{1,0:T(8,128)(2,1)S(1)}, u32[]{:S(2)}) copy-start(bf16[160,1536]{1,0:T(8,128)(2,1)S(1)} %collective-permute-done.34) | copy-start | bytes 1474564
  141.4 4.1 %collective-permute-start.40 = (bf16[160,1536]{1,0:T(8,128)(2,1)S(1)}, bf16[160,1536]{1,0:T(8,128)(2,1)S(1)}, u32[]{:S(2)}, u32[]{:S(2)}) collective-permute-start(bf16[160,1536]{1,0:T(8,128)(2,1)S(1)} %fusion.158), channel_id=1, source_target_pairs={{16,8},{9,17},{18,10},{11,19},{20,12},{13,21},{22,14},{15,23}} | collective-permute-start | bytes 1474568 | tf_op jit(solution)/shard_map/ppermute | solution.py:145
  143.0 14.2 %collective-permute-start.28 = (bf16[160,1536]{1,0:T(8,128)(2,1)S(1)}, bf16[160,1536]{1,0:T(8,128)(2,1)S(1)}, u32[]{:S(2)}, u32[]{:S(2)}) collective-permute-start(bf16[160,1536]{1,0:T(8,128)(2,1)S(1)} %fusion.25), channel_id=1, source_target_pairs={{0,4},{4,0},{1,5},{5,1},{2,6},{6,2},{3,7},{7,3},{8,12},{12,8},{9,1... | collective-permute-start | bytes 1474568 | tf_op jit(solution)/shard_map/ppermute | solution.py:124
  145.4 17.3 %copy-start.12 = (bf16[160,1536]{1,0:T(8,128)(2,1)}, bf16[160,1536]{1,0:T(8,128)(2,1)S(1)}, u32[]{:S(2)}) copy-start(bf16[160,1536]{1,0:T(8,128)(2,1)S(1)} %collective-permute-done.40) | copy-start | bytes 1474564
  145.4 20.7 %collective-permute-start.22 = (bf16[160,1536]{1,0:T(8,128)(2,1)S(1)}, bf16[160,1536]{1,0:T(8,128)(2,1)S(1)}, u32[]{:S(2)}, u32[]{:S(2)}) collective-permute-start(bf16[160,1536]{1,0:T(8,128)(2,1)S(1)} %fusion.24), channel_id=1, source_target_pairs={{0,4},{4,0},{1,5},{5,1},{2,6},{6,2},{3,7},{7,3},{8,12},{12,8},{9,1... | collective-permute-start | bytes 1474568 | tf_op jit(solution)/shard_map/ppermute | solution.py:124
  157.1 27.7 %collective-permute-start.8 = (bf16[3072,192]{0,1:T(8,128)(2,1)}, bf16[3072,192]{0,1:T(8,128)(2,1)S(1)}, u32[]{:S(2)}, u32[]{:S(2)}) collective-permute-start(bf16[3072,192]{0,1:T(8,128)(2,1)} %collective-permute-done.4), channel_id=1, source_target_pairs={{8,0},{16,8},{24,16},{9,1},{17,9},{25,17},{10,2},{18,10},{26,18},{... | collective-permute-start | bytes 3538952 | tf_op jit(solution)/shard_map/ppermute | solution.py:97
  162.8 136.8 %copy-start.5 = (f32[160,1536]{1,0:T(8,128)}, f32[160,1536]{1,0:T(8,128)S(1)}, u32[]{:S(2)}) copy-start(f32[160,1536]{1,0:T(8,128)S(1)} %get-tuple-element.50) | copy-start | bytes 2949124
  166.1 134.3 %collective-permute-start.36 = (bf16[160,1536]{1,0:T(8,128)(2,1)}, bf16[160,1536]{1,0:T(8,128)(2,1)S(1)}, u32[]{:S(2)}, u32[]{:S(2)}) collective-permute-start(bf16[160,1536]{1,0:T(8,128)(2,1)} %fusion.157), channel_id=1, source_target_pairs={{16,8},{25,17},{18,10},{27,19},{20,12},{29,21},{22,14},{31,23}} | collective-permute-start | bytes 1474568 | tf_op jit(solution)/shard_map/ppermute | solution.py:145
  167.1 115.1 %copy-start.9 = (f32[160,1536]{1,0:T(8,128)}, f32[160,1536]{1,0:T(8,128)S(1)}, u32[]{:S(2)}) copy-start(f32[160,1536]{1,0:T(8,128)S(1)} %get-tuple-element.52) | copy-start | bytes 2949124
  167.1 144.5 %collective-permute-start.35 = (bf16[160,1536]{1,0:T(8,128)(2,1)}, bf16[160,1536]{1,0:T(8,128)(2,1)}, u32[]{:S(2)}, u32[]{:S(2)}) collective-permute-start(bf16[160,1536]{1,0:T(8,128)(2,1)} %fusion.157), channel_id=1, source_target_pairs={{0,8},{9,17},{2,10},{11,19},{4,12},{13,21},{6,14},{15,23}} | collective-permute-start | bytes 1474568 | tf_op jit(solution)/shard_map/ppermute | solution.py:145
  170.1 4.8 %collective-permute-start.29 = (bf16[160,1536]{1,0:T(8,128)(2,1)S(1)}, bf16[160,1536]{1,0:T(8,128)(2,1)S(1)}, u32[]{:S(2)}, u32[]{:S(2)}) collective-permute-start(bf16[160,1536]{1,0:T(8,128)(2,1)S(1)} %get-tuple-element.49), channel_id=1, source_target_pairs={{0,8},{25,17},{2,10},{27,19},{4,12},{29,21},{6,14},{31,23}} | collective-permute-start | bytes 1474568 | tf_op jit(solution)/shard_map/ppermute | solution.py:145
  172.2 13.9 %collective-permute-start.7 = (bf16[3072,192]{0,1:T(8,128)(2,1)S(1)}, bf16[3072,192]{0,1:T(8,128)(2,1)S(1)}, u32[]{:S(2)}, u32[]{:S(2)}) collective-permute-start(bf16[3072,192]{0,1:T(8,128)(2,1)S(1)} %collective-permute-done.6), channel_id=1, source_target_pairs={{0,2},{2,0},{1,3},{3,1},{4,6},{6,4},{5,7},{7,5},{8,10},{10,8},{9,1... | collective-permute-start | bytes 3538952 | tf_op jit(solution)/shard_map/ppermute | solution.py:85
  174.9 124.7 %copy-start.11 = (bf16[160,1536]{1,0:T(8,128)(2,1)}, bf16[160,1536]{1,0:T(8,128)(2,1)S(1)}, u32[]{:S(2)}) copy-start(bf16[160,1536]{1,0:T(8,128)(2,1)S(1)} %collective-permute-done.29) | copy-start | bytes 1474564
  174.9 136.7 %collective-permute-start.41 = (bf16[160,1536]{1,0:T(8,128)(2,1)}, bf16[160,1536]{1,0:T(8,128)(2,1)}, u32[]{:S(2)}, u32[]{:S(2)}) collective-permute-start(bf16[160,1536]{1,0:T(8,128)(2,1)} %fusion.162), channel_id=1, source_target_pairs={{8,0},{17,25},{10,2},{19,27},{12,4},{21,29},{14,6},{23,31}} | collective-permute-start | bytes 1474568 | tf_op jit(solution)/shard_map/ppermute | solution.py:145
  184.8 27.5 %collective-permute-start.10 = (bf16[3072,192]{0,1:T(8,128)(2,1)S(1)}, bf16[3072,192]{0,1:T(8,128)(2,1)S(1)}, u32[]{:S(2)}, u32[]{:S(2)}) collective-permute-start(bf16[3072,192]{0,1:T(8,128)(2,1)S(1)} %collective-permute-done.6), channel_id=1, source_target_pairs={{0,8},{8,16},{16,24},{1,9},{9,17},{17,25},{2,10},{10,18},{18,26},{... | collective-permute-start | bytes 3538952 | tf_op jit(solution)/shard_map/ppermute | solution.py:96
  186.1 2.9 collective-permute-start.9
  189.1 32.3 %collective-permute-start.12 = (bf16[3072,192]{0,1:T(8,128)(2,1)S(1)}, bf16[3072,192]{0,1:T(8,128)(2,1)S(1)}, u32[]{:S(2)}, u32[]{:S(2)}) collective-permute-start(bf16[3072,192]{0,1:T(8,128)(2,1)S(1)} %collective-permute-done.8), channel_id=1, source_target_pairs={{8,0},{16,8},{24,16},{9,1},{17,9},{25,17},{10,2},{18,10},{26,18},{... | collective-permute-start | bytes 3538952 | tf_op jit(solution)/shard_map/ppermute | solution.py:97
  212.4 9.7 %collective-permute-start.11 = (bf16[3072,192]{0,1:T(8,128)(2,1)S(1)}, bf16[3072,192]{0,1:T(8,128)(2,1)S(1)}, u32[]{:S(2)}, u32[]{:S(2)}) collective-permute-start(bf16[3072,192]{0,1:T(8,128)(2,1)S(1)} %collective-permute-done.10), channel_id=1, source_target_pairs={{0,2},{2,0},{1,3},{3,1},{4,6},{6,4},{5,7},{7,5},{8,10},{10,8},{9,1... | collective-permute-start | bytes 3538952 | tf_op jit(solution)/shard_map/ppermute | solution.py:85
  221.4 5.8 %collective-permute-start.23 = (bf16[160,1536]{1,0:T(8,128)(2,1)S(1)}, bf16[160,1536]{1,0:T(8,128)(2,1)S(1)}, u32[]{:S(2)}, u32[]{:S(2)}) collective-permute-start(bf16[160,1536]{1,0:T(8,128)(2,1)S(1)} %get-tuple-element.51), channel_id=1, source_target_pairs={{0,8},{25,17},{2,10},{27,19},{4,12},{29,21},{6,14},{31,23}} | collective-permute-start | bytes 1474568 | tf_op jit(solution)/shard_map/ppermute | solution.py:145
  222.1 2.9 collective-permute-start.13
  225.0 74.0 %collective-permute-start.30 = (bf16[160,1536]{1,0:T(8,128)(2,1)S(1)}, bf16[160,1536]{1,0:T(8,128)(2,1)S(1)}, u32[]{:S(2)}, u32[]{:S(2)}) collective-permute-start(bf16[160,1536]{1,0:T(8,128)(2,1)S(1)} %fusion.156), channel_id=1, source_target_pairs={{8,16},{17,9},{10,18},{19,11},{12,20},{21,13},{14,22},{23,15}} | collective-permute-start | bytes 1474568 | tf_op jit(solution)/shard_map/ppermute | solution.py:145
  227.2 71.5 %copy-start.15 = (bf16[160,1536]{1,0:T(8,128)(2,1)}, bf16[160,1536]{1,0:T(8,128)(2,1)S(1)}, u32[]{:S(2)}) copy-start(bf16[160,1536]{1,0:T(8,128)(2,1)S(1)} %collective-permute-done.23) | copy-start | bytes 1474564
  227.2 66.2 %collective-permute-start.14 = (bf16[2,320,384]{2,1,0:T(8,128)(2,1)S(1)}, bf16[2,320,384]{2,1,0:T(8,128)(2,1)S(1)}, u32[]{:S(2)}, u32[]{:S(2)}) collective-permute-start(bf16[2,320,384]{2,1,0:T(8,128)(2,1)S(1)} %dynamic-slice_bitcast_fusion.10), channel_id=1, source_target_pairs={{0,1},{1,0},{2,3},{3,2},{4,5},{5,4},{6,7},{7,6},{8,9},{9,8},{10,11... | collective-permute-start | bytes 1474568 | tf_op jit(solution)/shard_map/ppermute | solution.py:160
  293.4 18.2 %collective-permute-start.25 = (bf16[160,1536]{1,0:T(8,128)(2,1)}, bf16[160,1536]{1,0:T(8,128)(2,1)}, u32[]{:S(2)}, u32[]{:S(2)}) collective-permute-start(bf16[160,1536]{1,0:T(8,128)(2,1)} %fusion.155), channel_id=1, source_target_pairs={{24,16},{17,9},{26,18},{19,11},{28,20},{21,13},{30,22},{23,15}} | collective-permute-start | bytes 1474568 | tf_op jit(solution)/shard_map/ppermute | solution.py:145
  298.7 8.6 %copy-start.24 = (f32[160,12]{0,1:T(8,128)S(1)}, f32[160,12]{0,1:T(8,128)}, u32[]{:S(2)}) copy-start(f32[160,12]{0,1:T(8,128)} %param.9) | copy-start | bytes 23044
  298.7 8.6 %copy-start.25 = (s32[160,12]{0,1:T(8,128)S(1)}, s32[160,12]{0,1:T(8,128)}, u32[]{:S(2)}) copy-start(s32[160,12]{0,1:T(8,128)} %param.8) | copy-start | bytes 23044
  299.0 8.5 %copy-start.13 = (bf16[160,1536]{1,0:T(8,128)(2,1)}, bf16[160,1536]{1,0:T(8,128)(2,1)S(1)}, u32[]{:S(2)}) copy-start(bf16[160,1536]{1,0:T(8,128)(2,1)S(1)} %collective-permute-done.30) | copy-start | bytes 1474564
  299.0 6.8 %collective-permute-start.15 = (bf16[2,160,384]{2,0,1:T(2,128)(2,1)S(1)}, bf16[2,160,384]{2,0,1:T(2,128)(2,1)S(1)}, u32[]{:S(2)}, u32[]{:S(2)}) collective-permute-start(bf16[2,160,384]{2,0,1:T(2,128)(2,1)S(1)} %bitcast.266), channel_id=1, source_target_pairs={{0,4},{4,0},{1,5},{5,1},{2,6},{6,2},{3,7},{7,3},{8,12},{12,8},{9,1... | collective-permute-start | bytes 737288 | tf_op jit(solution)/shard_map/ppermute | solution.py:162
  300.5 7.9 %copy-start.23 = (bf16[160,1536]{1,0:T(8,128)(2,1)}, bf16[160,1536]{1,0:T(8,128)(2,1)S(1)}, u32[]{:S(2)}) copy-start(bf16[160,1536]{1,0:T(8,128)(2,1)S(1)} %collective-permute-done.36) | copy-start | bytes 1474564
  300.5 11.1 %collective-permute-start.24 = (bf16[160,1536]{1,0:T(8,128)(2,1)}, bf16[160,1536]{1,0:T(8,128)(2,1)}, u32[]{:S(2)}, u32[]{:S(2)}) collective-permute-start(bf16[160,1536]{1,0:T(8,128)(2,1)} %fusion.155), channel_id=1, source_target_pairs={{8,16},{1,9},{10,18},{3,11},{12,20},{5,13},{14,22},{7,15}} | collective-permute-start | bytes 1474568 | tf_op jit(solution)/shard_map/ppermute | solution.py:145
  305.8 13.3 %collective-permute-start.31 = (bf16[160,1536]{1,0:T(8,128)(2,1)}, bf16[160,1536]{1,0:T(8,128)(2,1)}, u32[]{:S(2)}, u32[]{:S(2)}) collective-permute-start(bf16[160,1536]{1,0:T(8,128)(2,1)} %fusion.161), channel_id=1, source_target_pairs={{16,24},{9,1},{18,26},{11,3},{20,28},{13,5},{22,30},{15,7}} | collective-permute-start | bytes 1474568 | tf_op jit(solution)/shard_map/ppermute | solution.py:145
  319.1 6.4 %copy-start.1 = (bf16[1,1024,1536]{2,1,0:T(8,128)(2,1)S(1)}, bf16[1,1024,1536]{2,1,0:T(8,128)(2,1)}, u32[]{:S(2)}) copy-start(bf16[1,1024,1536]{2,1,0:T(8,128)(2,1)} %param.11) | copy-start | bytes 9437188
  (4 other events, 6.0 us)

commit v2 on v1

--- a/solution.py
+++ b/solution.py
@@ -1,11 +1,14 @@
 import jax
 import jax.numpy as jnp
 from jax import lax
+from jax.experimental import pallas as pl
+from jax.experimental.pallas import tpu as pltpu
 from jax.sharding import Mesh, PartitionSpec as P
 
 F32 = jnp.float32
 BF16 = jnp.bfloat16
 SWAP = ((0, 1), (1, 0))
+FREE = pl.CostEstimate(flops=0, bytes_accessed=0, transcendentals=0)
 
 
 def pick(array, index, axis=0):
@@ -48,7 +51,221 @@
     return high, low
 
 
-def local(tokens, expert_ids, gate_weights, expert_hidden, expert_down, dense_hidden, dense_down):
+def combine_kernel(at, gates, mine, sibling, out):
+    capacity, tokens = mine.shape[1], gates.shape[2]
+    steps = pl.num_programs(0)
+    order = lax.broadcasted_iota(jnp.int32, (tokens, tokens), 0)
+    earlier = (order < lax.broadcasted_iota(jnp.int32, (tokens, tokens), 1)).astype(BF16)
+    places = lax.broadcasted_iota(jnp.int32, (capacity, tokens), 0)
+    total = None
+    for e, table in enumerate((mine, sibling)):
+        gate = gates[0, pl.ds(at[3 * steps + e], 1), :]
+        picked = gate >= 0
+        marks = jnp.broadcast_to(jnp.where(picked, F32(1.0), F32(0.0)), (8, tokens)).astype(BF16)
+        slot = jnp.dot(marks, earlier, preferred_element_type=F32)[0:1].astype(jnp.int32)
+        place = jnp.where((slot == places) & picked, gate, F32(0.0))
+        high = place.astype(BF16)
+        low = (place - high.astype(F32)).astype(BF16)
+        for part in (high, low):
+            term = lax.dot_general(part, table[0], (((0,), (0,)), ((), ())), preferred_element_type=F32)
+            total = term if total is None else total + term
+    out[0] = total.astype(out.dtype)
+
+
+def combine(at, steps, gates, table, sibling, dtype):
+    _, capacity, features = table.shape
+    tokens = gates.shape[2]
+    return pl.pallas_call(
+        combine_kernel,
+        out_shape=jax.ShapeDtypeStruct((steps, tokens, features), dtype),
+        grid_spec=pltpu.PrefetchScalarGridSpec(
+            num_scalar_prefetch=1,
+            grid=(steps,),
+            in_specs=[
+                pl.BlockSpec((1,) + gates.shape[1:], lambda i, at: (at[i], 0, 0)),
+                pl.BlockSpec((1, capacity, features), lambda i, at: (at[steps + i], 0, 0)),
+                pl.BlockSpec((1, capacity, features), lambda i, at: (at[2 * steps + i], 0, 0)),
+            ],
+            out_specs=pl.BlockSpec((1, tokens, features), lambda i, at: (i, 0, 0)),
+        ),
+        compiler_params=pltpu.CompilerParams(vmem_limit_bytes=32 << 20),
+        cost_estimate=FREE,
+    )(at, gates, table, sibling)
+
+
+def tables_kernel(core, hidden, down, sent, kept):
+    steps = pl.num_programs(0)
+    value = jnp.dot(hidden[0, 0], down[...], preferred_element_type=F32).astype(sent.dtype)
+
+    @pl.when(2 * pl.program_id(0) < steps)
+    def _():
+        sent[0] = value
+
+    @pl.when(2 * pl.program_id(0) >= steps)
+    def _():
+        kept[0] = value
+
+
+def expert_tables(core, hidden, down):
+    blocks, _, capacity, units = hidden.shape
+    features = down.shape[1]
+    shape = jax.ShapeDtypeStruct((blocks, capacity, features), hidden.dtype)
+    return pl.pallas_call(
+        tables_kernel,
+        out_shape=(shape, shape),
+        grid_spec=pltpu.PrefetchScalarGridSpec(
+            num_scalar_prefetch=1,
+            grid=(2 * blocks,),
+            in_specs=[
+                pl.BlockSpec(
+                    (1, 1, capacity, units),
+                    lambda i, core: (lax.rem(i, blocks), jnp.where(i < blocks, 1 - core[0], core[0]), 0, 0),
+                ),
+                pl.BlockSpec((units, features), lambda i, core: (0, 0)),
+            ],
+            out_specs=[
+                pl.BlockSpec((1, capacity, features), lambda i, core: (jnp.minimum(i, blocks - 1), 0, 0)),
+                pl.BlockSpec((1, capacity, features), lambda i, core: (jnp.maximum(i - blocks, 0), 0, 0)),
+            ],
+        ),
+        compiler_params=pltpu.CompilerParams(vmem_limit_bytes=32 << 20),
+        cost_estimate=FREE,
+    )(core, hidden, down)
+
+
+def product_kernel(acts_a, acts_b, acts_c, acts_d, first, second, out):
+    start = pl.program_id(0) == 0
+    for w, weights in enumerate((first, second)):
+        for i, acts in enumerate((acts_a, acts_b, acts_c, acts_d)):
+            term = lax.dot_general(acts[...], weights[...], (((1,), (1,)), ((), ())), preferred_element_type=F32)
+            out[w, i] = jnp.where(start, term, out[w, i] + term)
+
+
+def products(acts, first, second):
+    rows, depth = acts[0].shape
+    columns = first.shape[0]
+    step = depth // 4
+    shape = (2, 4, rows, columns)
+    return pl.pallas_call(
+        product_kernel,
+        out_shape=jax.ShapeDtypeStruct(shape, F32),
+        grid=(depth // step,),
+        in_specs=[pl.BlockSpec((rows, step), lambda i: (0, i))] * 4 + [pl.BlockSpec((columns, step), lambda i: (0, i))] * 2,
+        out_specs=pl.BlockSpec(shape, lambda i: (0, 0, 0, 0)),
+        compiler_params=pltpu.CompilerParams(vmem_limit_bytes=32 << 20),
+        cost_estimate=FREE,
+    )(*acts, first, second)
+
+
+def four_by_two(tokens, expert_ids, gate_weights, expert_hidden, expert_down, dense_hidden, dense_down):
+    z, y, c, x = (lax.axis_index(name) for name in ("z", "y", "c", "tp"))
+    experts = 16
+    rows = tokens.shape[0]
+    hidden, down = expert_hidden[0], expert_down[0]
+    capacity = hidden.shape[0] // 8
+    features = down.shape[1]
+    columns = dense_down.shape[1]
+    right = [(0, 1), (1, 2), (2, 3)]
+    left = [(1, 0), (2, 1), (3, 2)]
+    tie = lax.optimization_barrier
+
+    core = jnp.reshape(c, (1,))
+
+    def tables(chunk):
+        sent, kept = expert_tables(core, chunk.reshape(-1, 2, capacity, chunk.shape[-1]), down)
+        return kept, lax.ppermute(sent, "c", SWAP)
+
+    def sums(tables, gates, goals, away, dtype):
+        side = 1 - y if away else y
+        at = [goal * 2 + side for goal, _ in goals]
+        at += [place * 2 + side for _, place in goals] * 2
+        at = jnp.stack(at + [c, 1 - c]).astype(jnp.int32)
+        return combine(at, len(goals), gates, *tables, dtype)
+
+    halves = hidden.reshape(2, 4 * capacity, hidden.shape[1])
+    hidden_0 = lax.ppermute(pick(halves, x), "tp", SWAP)
+    weights = dense_down.T
+    weights_r1 = lax.ppermute(weights, "z", right)
+    weights_l1 = lax.ppermute(weights, "z", left)
+    acts_y = lax.ppermute(dense_hidden, "y", SWAP)
+    gates = gate_rows(expert_ids, gate_weights, experts).reshape(8, 2, rows)
+    gates = lax.all_to_all(gates, ("z", "y"), 0, 0, tiled=True)
+    own = tables(hidden)
+    own_goals = ((3 * x, x), (1 + x, 1 - x))
+    given_own = sums(own, gates, own_goals, 1, BF16)
+    given_own, acts_y, acts_c = tie((given_own, acts_y, dense_hidden))
+    acts_c = lax.ppermute(acts_c, "c", SWAP)
+    got_own = lax.ppermute(given_own, "y", SWAP)
+    acts_cy = lax.ppermute(acts_y, "c", SWAP)
+    acts = (dense_hidden, acts_y, acts_c, acts_cy)
+
+    hidden_1, hidden_0, weights_r1, weights_l1 = tie((pick(halves, 1 - x), hidden_0, weights_r1, weights_l1))
+    hidden_1 = lax.ppermute(hidden_1, "tp", SWAP)
+    weights_r2 = lax.ppermute(weights_r1, "z", right)
+    weights_l2 = lax.ppermute(weights_l1, "z", left)
+    outer = tables(hidden_0)
+    given_outer = sums(outer, gates, ((3 * (1 - x), 0),), 1, BF16)
+    given_outer, got_own = tie((given_outer, got_own))
+    got_outer = lax.ppermute(given_outer, "y", SWAP)
+    sum_own = sums(own, gates, own_goals, 0, F32) + got_own.astype(F32)
+    sheets = [products(acts, weights, weights), products(acts, weights_r1, weights_l1)]
+
+    weights_r2, weights_l2, hidden_1, sheets = tie((weights_r2, weights_l2, hidden_1, sheets))
+    weights_r3 = lax.ppermute(weights_r2, "z", right)
+    weights_l3 = lax.ppermute(weights_l2, "z", left)
+    inner = tables(hidden_1)
+    given_inner = sums(inner, gates, ((2 - x, 0),), 1, BF16)
+    given_inner, got_outer = tie((given_inner, got_outer))
+    got_inner = lax.ppermute(given_inner, "y", SWAP)
+    sum_outer = (sums(outer, gates, ((3 * (1 - x), 0),), 0, F32) + got_outer.astype(F32))[0]
+    goal_0 = jnp.where(x == 0, sum_own[0], sum_outer)
+    goal_3 = jnp.where(x == 0, sum_outer, sum_own[0])
+    up = lax.ppermute(goal_3.astype(BF16), "z", [(0, 1)])
+    low = lax.ppermute(goal_0.astype(BF16), "z", [(3, 2)])
+    sheets = sheets + [products(acts, weights_r2, weights_l2)]
+    sum_inner = (sums(inner, gates, ((2 - x, 0),), 0, F32) + got_inner.astype(F32))[0]
+    goal_1 = jnp.where(x == 0, sum_own[1], sum_inner)
+    goal_2 = jnp.where(x == 0, sum_inner, sum_own[1])
+
+    up = jnp.where(z == 0, goal_2, goal_3 + up.astype(F32)).astype(BF16)
+    low = jnp.where(z == 3, goal_1, goal_0 + low.astype(F32)).astype(BF16)
+    up, low, weights_r3, weights_l3, sheets = tie((up, low, weights_r3, weights_l3, sheets))
+    up = lax.ppermute(up, "z", [(0, 1), (1, 2)])
+    low = lax.ppermute(low, "z", [(3, 2), (2, 1)])
+    sheets = sheets + [products(acts, weights_r3, weights_l3)]
+    sheet = [sheets[i][0] for i in (3, 2, 1, 0)] + [sheets[i][1] for i in (1, 2, 3)]
+    sheet = jnp.stack(sheet)
+    theirs = lax.dynamic_slice_in_dim(sheet, 3 - z + 2 * (1 - x), 2).astype(BF16)
+    dense = lax.dynamic_slice_in_dim(sheet, 3 - z + 2 * x, 2)
+    dense = dense + lax.ppermute(theirs, "tp", SWAP).astype(F32)
+
+    up = jnp.where(z == 0, goal_1, jnp.where(z == 1, goal_2, goal_3) + up.astype(F32)).astype(BF16)
+    low = jnp.where(z == 3, goal_2, jnp.where(z == 2, goal_1, goal_0) + low.astype(F32)).astype(BF16)
+    up = lax.ppermute(up, "z", right)
+    low = lax.ppermute(low, "z", left)
+    routed = jnp.where(z == 0, goal_0, jnp.where(z == 1, goal_1, jnp.where(z == 2, goal_2, goal_3)))
+    routed = routed + (up.astype(F32) + low.astype(F32))
+
+    dense = dense.reshape(2, 2, 2, rows, columns)
+    near = dense[:, 0, 0]
+    by_c = lax.ppermute(dense[:, 1, 0].astype(BF16), "c", SWAP).astype(F32)
+    by_y = lax.ppermute(dense[:, 0, 1].astype(BF16), "y", SWAP).astype(F32)
+    by_both = lax.ppermute(dense[:, 1, 1].astype(BF16), ("y", "c"), [(0, 3), (1, 2), (2, 1), (3, 0)]).astype(F32)
+
+    def ordered(first, second, swap):
+        return jnp.where(swap, second, first), jnp.where(swap, first, second)
+
+    same = jnp.concatenate(ordered(near, by_c, c == 1), 2)
+    across = jnp.concatenate(ordered(by_y, by_both, c == 1), 2)
+    pair = ordered(same, across, y == 1)
+    dense = jnp.concatenate([pair[0][0], pair[1][0], pair[0][1], pair[1][1]], 1)
+
+    zero_gate = jnp.sum(jnp.where(expert_ids < experts, F32(0.0), gate_weights), axis=1)
+    identity = zero_gate[:, None] * tokens.astype(F32)
+    return (dense + routed + identity).astype(BF16)
+
+
+def any_mesh(tokens, expert_ids, gate_weights, expert_hidden, expert_down, dense_hidden, dense_down):
     zs, tp = lax.axis_size("z"), lax.axis_size("tp")
     z, y, c, x = (lax.axis_index(name) for name in ("z", "y", "c", "tp"))
     experts = zs * 4
@@ -63,9 +280,6 @@
     def turn(owner, k):
         return jnp.where(2 * owner < tp, k, zt - 1 - k)
 
-    def turn_of(owner, k):
-        return k if 2 * owner < tp else zt - 1 - k
-
     chunks = []
     for k in range(zt):
         chunks.append((0, k, pick(hidden, turn(x, k))))
@@ -75,8 +289,6 @@
             moved = lax.ppermute(sent, "tp", [((i + shift) % tp, i) for i in range(tp)])
             chunks.append((shift, k, moved))
 
-    right = [(i, i + 1) for i in range(zs - 1)]
-    left = [(i + 1, i) for i in range(zs - 1)]
     acts = jnp.stack([dense_hidden, lax.ppermute(dense_hidden, "y", SWAP)])
     acts = acts.reshape(2 * rows, -1)
     columns = dense_down.shape[1]
@@ -89,21 +301,9 @@
         return jnp.dot(acts, both, preferred_element_type=F32).astype(BF16)
 
     sheet = jnp.zeros((zs, 2 * rows, 2 * columns), BF16)
-    if zs <= 4:
-        sheet = lax.dynamic_update_index_in_dim(sheet, product(dense_down), z, 0)
-        from_left = from_right = dense_down
-        for step in range(1, zs):
-            from_left = lax.ppermute(from_left, "z", right)
-            from_right = lax.ppermute(from_right, "z", left)
-            for value, at in ((from_left, z - step), (from_right, z + step)):
-                inside = (at >= 0) & (at < zs)
-                at = jnp.clip(at, 0, zs - 1)
-                value = jnp.where(inside, product(value), pick(sheet, at))
-                sheet = lax.dynamic_update_index_in_dim(sheet, value, at, 0)
-    else:
-        every = lax.all_gather(dense_down, "z")
-        for i in range(zs):
-            sheet = lax.dynamic_update_index_in_dim(sheet, product(every[i]), i, 0)
+    every = lax.all_gather(dense_down, "z")
+    for i in range(zs):
+        sheet = lax.dynamic_update_index_in_dim(sheet, product(every[i]), i, 0)
 
     gates = spread_gates(gate_rows(expert_ids, gate_weights, experts), zs, y, z)
     high, low = placement(gates, capacity)
@@ -124,34 +324,12 @@
         sent = lax.ppermute(combined(1 - y).astype(BF16), "y", SWAP)
         return combined(y) + sent.astype(F32)
 
-    routed = jnp.zeros((rows, features), F32)
-    if zs <= 4:
-        for shift, k, chunk in chunks:
-            owner = (x + shift) % tp
-            at = owner * zt + turn(owner, k)
-            total = partial_sum(chunk, at)
-            goals = [((i + shift) % tp) * zt + turn_of((i + shift) % tp, k) for i in range(tp)]
-            for distance in range(zs - 1, 0, -1):
-                sent = total.astype(BF16)
-                first, second = {}, {}
-                for i in range(tp):
-                    for way in (1, -1):
-                        start = goals[i] - way * distance
-                        if 0 <= start < zs:
-                            end = (start + way) * tp + i
-                            (second if end in first else first)[end] = start * tp + i
-                for links in (first, second):
-                    if links:
-                        moved = lax.ppermute(sent, ("z", "tp"), [(a, b) for b, a in links.items()])
-                        total = total + moved.astype(F32)
-            routed = jnp.where(z == at, total, routed)
-    else:
-        totals = jnp.zeros((zs, rows, features), BF16)
-        for shift, k, chunk in chunks:
-            owner = (x + shift) % tp
-            at = owner * zt + turn(owner, k)
-            totals = lax.dynamic_update_index_in_dim(totals, partial_sum(chunk, at).astype(BF16), at, 0)
-        routed = lax.psum_scatter(totals, "z", scatter_dimension=0).astype(F32)
+    totals = jnp.zeros((zs, rows, features), BF16)
+    for shift, k, chunk in chunks:
+        owner = (x + shift) % tp
+        at = owner * zt + turn(owner, k)
+        totals = lax.dynamic_update_index_in_dim(totals, partial_sum(chunk, at).astype(BF16), at, 0)
+    routed = lax.psum_scatter(totals, "z", scatter_dimension=0).astype(F32)
 
     sheet = sheet.reshape(tp, zt, 2 * rows, 2 * columns)
     dense = pick(sheet, x).astype(F32)
@@ -174,7 +352,7 @@
     split = Mesh(mesh.devices.reshape(groups, ranks // 4, 2, 2, tp), ("grp", "z", "y", "c", "tp"))
     ep = ("z", "y", "c")
     return jax.shard_map(
-        local,
+        four_by_two if ranks == 16 and tp == 2 else any_mesh,
         mesh=split,
         in_specs=(
             P(("grp",) + ep, "tp"),

time: 327 us -> 193 us (0.59)
  the two profiles are of different devices: /device:TPU:24 before, /device:TPU:0 now
where the time goes in v2:
time: 193 us; the launch traced here: 192 us
  waiting for transfers between devices  59.8 us (31%)
  Pallas kernels  53.3 us (28%)
  starting transfers between devices  50.2 us (26%)
  local copies, waits for them, and re-layouts  18.3 us (9%)
  other arithmetic  10.1 us (5%)
    pallas_call x4, Pallas kernels, products(): pl.pallas_call(product_kernel, out_shape=jax.ShapeDtypeStruct(shape, F32)...  20.7 us
    pallas_call x6, Pallas kernels, combine(): pl.pallas_call(combine_kernel, out_shape=jax.ShapeDtypeStruct((steps, tok...  18.7 us
    all_to_all x1, waiting for transfers between devices, four_by_two(): gates = lax.all_to_all(gates, ('z', 'y'), 0, 0, tiled=True)  18.7 us
    unnamed x68, local copies, waits for them, and re-layouts  14 us
    pallas_call x3, Pallas kernels, expert_tables(): pl.pallas_call(tables_kernel, out_shape=(shape, shape), grid_spec=pltpu.P...  14 us
    ppermute x1, waiting for transfers between devices, four_by_two(): up = lax.ppermute(goal_3.astype(BF16), 'z', [(0, 1)])  9.52 us
    ppermute x1, waiting for transfers between devices, four_by_two(): dense = dense + lax.ppermute(theirs, 'tp', SWAP).astype(F32)  9.25 us
    ppermute x1, waiting for transfers between devices, four_by_two(): low = lax.ppermute(low, 'z', left)  8.47 us
  transfers between devices with their start and end apart: 28, of which 10 were waited for; matrix products, arithmetic and copies ran while one was open for 7% of the time, Pallas kernels for 22%

profile of v2, /device:TPU:0, one launch (start us, length us, event | category | flops | bytes accessed | tf_op | source)
XLA Modules:
  0.0 192.3 jit_solution(5075544456851165271)
XLA Ops:
  0.0 1.9 copy-done
  1.9 1.5 copy-done.6
  3.4 5.9 %shard_map.73 = (bf16[4,120,1536]{2,1,0:T(8,128)(2,1)}, bf16[4,120,1536]{2,1,0:T(8,128)(2,1)S(1)}) custom-call(s32[1]{0:T(128)} %bitcast.4.core, bf16[4,2,120,1024]{3,2,1,0:T(8,128)(2,1)S(1)} %bitcast.101, bf16[1024,1536]{1,0:T(8,128)(2,1)S(1)} %bitcast.97), custom_call_target="tpu_custom_call" | custom-call | tf_op jit(solution)/shard_map/pallas_call | solution.py:113
  9.4 0.5 collective-permute-start
  9.8 2.6 %collective-permute-start.1 = (bf16[160,3072]{1,0:T(8,128)(2,1)S(1)}, bf16[160,3072]{1,0:T(8,128)(2,1)S(1)}, u32[]{:S(2)}, u32[]{:S(2)}) collective-permute-start(bf16[160,3072]{1,0:T(8,128)(2,1)S(1)} %copy-done.2), channel_id=1, source_target_pairs={{0,4},{4,0},{1,5},{5,1},{2,6},{6,2},{3,7},{7,3},{8,12},{12,8},{9,1... | collective-permute-start | bytes 2949128 | tf_op jit(solution)/shard_map/ppermute | solution.py:190
  12.4 4.5 %collective-permute-start.5 = (bf16[192,3072]{1,0:T(8,128)(2,1)}, bf16[192,3072]{1,0:T(8,128)(2,1)}, u32[]{:S(2)}, u32[]{:S(2)}) collective-permute-start(bf16[192,3072]{1,0:T(8,128)(2,1)} %bitcast.15.first.second), channel_id=1, source_target_pairs={{0,8},{8,16},{16,24},{1,9},{9,17},{17,25},{2,10},{10,18},{18,26},{... | collective-permute-start | bytes 3538952 | tf_op jit(solution)/shard_map/ppermute | solution.py:188
  16.9 1.3 collective-permute-start.6
  18.3 2.9 %dynamic-slice_bitcast_fusion = (bf16[480,1024]{1,0:T(8,128)(2,1)}, bf16[480,1024]{1,0:T(8,128)(2,1)}) fusion(bf16[2,480,1024]{2,1,0:T(8,128)(2,1)} %bitcast.100, s32[]{:T(128)S(6)} %select_n.135, s32[]{:T(128)S(6)} %select_n.134), kind=kLoop, calls=%fused_computation.28 | loop fusion | bytes 3932168 | tf_op jit(solution)/shard_map/jit(dynamic_index_in_dim)/squeeze | solution.py:15
  21.2 1.5 collective-permute-start.4
  22.7 0.6 reshape.27
  23.3 5.9 %all-to-all-start = ((f32[8,2,160]{2,1,0:T(2,128)}), f32[8,2,160]{2,1,0:T(2,128)S(1)}, u32[]{:S(2)}, u32[]{:S(2)}) async-start(f32[8,2,160]{2,1,0:T(2,128)} %reshape.27), calls=%async_computation | async-start | bytes 32768 | tf_op jit(solution)/shard_map/all_to_all | solution.py:192
  29.3 18.7 %all-to-all-done.gates = f32[8,2,160]{2,1,0:T(2,128)S(1)} async-done(((f32[8,2,160]{2,1,0:T(2,128)}), f32[8,2,160]{2,1,0:T(2,128)S(1)}, u32[]{:S(2)}, u32[]{:S(2)}) %all-to-all-start) | async-done | bytes 10272 | tf_op jit(solution)/shard_map/all_to_all | solution.py:192
  48.0 4.7 %shard_map.74 = bf16[2,160,1536]{2,1,0:T(8,128)(2,1)} custom-call(s32[8]{0:T(128)S(1)} %stack.95.at, f32[8,2,160]{2,1,0:T(2,128)S(1)} %all-to-all-done.gates, bf16[4,120,1536]{2,1,0:T(8,128)(2,1)S(1)} %get-tuple-element.34.mine, bf16[4,120,1536]{2,1,0:T(8,128)(2,1)} %collective-permute-done.sibling), custom_call_target="tpu_custom_call" | custom-call | tf_op jit(solution)/shard_map/pallas_call | solution.py:78
  52.7 0.5 collective-permute-start.3
  53.3 3.5 %collective-permute-start.7 = (bf16[192,3072]{1,0:T(8,128)(2,1)}, bf16[192,3072]{1,0:T(8,128)(2,1)}, u32[]{:S(2)}, u32[]{:S(2)}) collective-permute-start(bf16[192,3072]{1,0:T(8,128)(2,1)} %collective-permute-done.5.first), channel_id=1, source_target_pairs={{0,8},{8,16},{16,24},{1,9},{9,17},{17,25},{2,10},{10,18},{18,26},{... | collective-permute-start | bytes 3538952 | tf_op jit(solution)/shard_map/ppermute | solution.py:204
  56.8 1.3 collective-permute-start.8
  58.1 1.5 collective-permute-start.9
  59.6 1.4 collective-permute-start.12
  61.1 4.7 %shard_map.80 = (bf16[2,120,1536]{2,1,0:T(8,128)(2,1)}, bf16[2,120,1536]{2,1,0:T(8,128)(2,1)S(1)}) custom-call(s32[1]{0:T(128)} %bitcast.4.core, bf16[2,2,120,1024]{3,2,1,0:T(8,128)(2,1)} %bitcast.20.hidden, bf16[1024,1536]{1,0:T(8,128)(2,1)S(1)} %bitcast.98), custom_call_target="tpu_custom_call" | custom-call | tf_op jit(solution)/shard_map/pallas_call | solution.py:113
  65.8 0.9 copy-done.14
  66.7 5.3 %shard_map.75 = f32[2,4,160,192]{3,2,1,0:T(8,128)S(1)} custom-call(bf16[160,3072]{1,0:T(8,128)(2,1)S(1)} %copy-done.2, bf16[160,3072]{1,0:T(8,128)(2,1)S(1)} %collective-permute-done.1.acts_b, bf16[160,3072]{1,0:T(8,128)(2,1)S(1)} %collective-permute-done.2.acts_c, bf16[160,3072]{1,0:T(8,128)(2,1)S(1)} %collective-permute-done.3.acts_d, ...), custom_call_target="tpu_custom_call" | custom-call | tf_op jit(solution)/shard_map/pallas_call | solution.py:149
  72.0 1.0 copy-done.16
  73.1 5.1 %shard_map.76 = f32[2,4,160,192]{3,2,1,0:T(8,128)S(1)} custom-call(bf16[160,3072]{1,0:T(8,128)(2,1)S(1)} %copy-done.2, bf16[160,3072]{1,0:T(8,128)(2,1)S(1)} %collective-permute-done.1.acts_b, bf16[160,3072]{1,0:T(8,128)(2,1)S(1)} %collective-permute-done.2.acts_c, bf16[160,3072]{1,0:T(8,128)(2,1)S(1)} %collective-permute-done.3.acts_d, ...), custom_call_target="tpu_custom_call" | custom-call | tf_op jit(solution)/shard_map/pallas_call | solution.py:149
  78.1 1.1 copy-done.9
  79.2 2.6 %collective-permute-done.9 = bf16[480,1024]{1,0:T(8,128)(2,1)S(1)} collective-permute-done((bf16[480,1024]{1,0:T(8,128)(2,1)}, bf16[480,1024]{1,0:T(8,128)(2,1)S(1)}, u32[]{:S(2)}, u32[]{:S(2)}) %collective-permute-start.9) | collective-permute-done | bytes 983072 | tf_op jit(solution)/shard_map/ppermute | solution.py:203
  81.8 4.8 %collective-permute-done.8.second = bf16[192,3072]{1,0:T(8,128)(2,1)} collective-permute-done((bf16[192,3072]{1,0:T(8,128)(2,1)}, bf16[192,3072]{1,0:T(8,128)(2,1)}, u32[]{:S(2)}, u32[]{:S(2)}) %collective-permute-start.8) | collective-permute-done | bytes 1179680 | tf_op jit(solution)/shard_map/ppermute | solution.py:205
  86.6 3.3 %shard_map.77 = (bf16[2,120,1536]{2,1,0:T(8,128)(2,1)}, bf16[2,120,1536]{2,1,0:T(8,128)(2,1)S(1)}) custom-call(s32[1]{0:T(128)} %bitcast.4.core, bf16[2,2,120,1024]{3,2,1,0:T(8,128)(2,1)S(1)} %bitcast.102, bf16[1024,1536]{1,0:T(8,128)(2,1)S(1)} %bitcast.99), custom_call_target="tpu_custom_call" | custom-call | tf_op jit(solution)/shard_map/pallas_call | solution.py:113
  90.0 0.9 copy-done.11
  91.2 1.4 copy-done.8
  92.6 3.6 %shard_map.82 = f32[2,160,1536]{2,1,0:T(8,128)S(1)} custom-call(s32[8]{0:T(128)S(1)} %stack.108.at, f32[8,2,160]{2,1,0:T(2,128)S(1)} %all-to-all-done.gates, bf16[4,120,1536]{2,1,0:T(8,128)(2,1)S(1)} %copy-done.8, bf16[4,120,1536]{2,1,0:T(8,128)(2,1)} %collective-permute-done.sibling), custom_call_target="tpu_custom_call" | custom-call | tf_op jit(solution)/shard_map/pallas_call | solution.py:78
  96.3 2.6 %shard_map.83 = f32[1,160,1536]{2,1,0:T(8,128)S(1)} custom-call(s32[5]{0:T(128)S(1)} %stack.110.at, f32[8,2,160]{2,1,0:T(2,128)S(1)} %all-to-all-done.gates, bf16[2,120,1536]{2,1,0:T(8,128)(2,1)S(1)} %copy-done.15, bf16[2,120,1536]{2,1,0:T(8,128)(2,1)} %collective-permute-done.11.sibling), custom_call_target="tpu_custom_call" | custom-call | tf_op jit(solution)/shard_map/pallas_call | solution.py:78
  98.8 2.6 %shard_map.81 = bf16[1,160,1536]{2,1,0:T(8,128)(2,1)S(1)} custom-call(s32[5]{0:T(128)S(1)} %stack.103.at, f32[8,2,160]{2,1,0:T(2,128)S(1)} %all-to-all-done.gates, bf16[2,120,1536]{2,1,0:T(8,128)(2,1)S(1)} %copy-done.15, bf16[2,120,1536]{2,1,0:T(8,128)(2,1)} %collective-permute-done.11.sibling), custom_call_target="tpu_custom_call" | custom-call | tf_op jit(solution)/shard_map/pallas_call | solution.py:78
  101.4 1.5 collective-permute-start.13
  102.9 2.5 %collective-permute-start.17 = (bf16[192,3072]{1,0:T(8,128)(2,1)}, bf16[192,3072]{1,0:T(8,128)(2,1)}, u32[]{:S(2)}, u32[]{:S(2)}) collective-permute-start(bf16[192,3072]{1,0:T(8,128)(2,1)} %collective-permute-done.7.first), channel_id=1, source_target_pairs={{0,8},{8,16},{16,24},{1,9},{9,17},{17,25},{2,10},{10,18},{18,26},{... | collective-permute-start | bytes 3538952 | tf_op jit(solution)/shard_map/ppermute | solution.py:214
  105.4 1.3 collective-permute-start.18
  106.7 1.4 convert_add_fusion
  108.2 2.7 %shard_map.79 = bf16[1,160,1536]{2,1,0:T(8,128)(2,1)S(1)} custom-call(s32[5]{0:T(128)S(1)} %stack.101.at, f32[8,2,160]{2,1,0:T(2,128)S(1)} %all-to-all-done.gates, bf16[2,120,1536]{2,1,0:T(8,128)(2,1)S(1)} %copy-done.12, bf16[2,120,1536]{2,1,0:T(8,128)(2,1)} %collective-permute-done.10.sibling), custom_call_target="tpu_custom_call" | custom-call | tf_op jit(solution)/shard_map/pallas_call | solution.py:78
  110.8 4.3 %collective-permute-done.13 = bf16[1,160,1536]{2,1,0:T(8,128)(2,1)S(1)} collective-permute-done((bf16[1,160,1536]{2,1,0:T(8,128)(2,1)S(1)}, bf16[1,160,1536]{2,1,0:T(8,128)(2,1)S(1)}, u32[]{:S(2)}, u32[]{:S(2)}) %collective-permute-start.13) | collective-permute-done | bytes 491552 | tf_op jit(solution)/shard_map/ppermute | solution.py:209
  115.1 1.8 bitcast_convert_fusion
  116.9 1.5 collective-permute-start.16
  118.4 1.4 collective-permute-start.14
  119.8 2.2 %collective-permute-start.15 = (bf16[160,1536]{1,0:T(8,128)(2,1)}, bf16[160,1536]{1,0:T(8,128)(2,1)}, u32[]{:S(2)}, u32[]{:S(2)}) collective-permute-start(bf16[160,1536]{1,0:T(8,128)(2,1)} %get-tuple-element.73), channel_id=1, source_target_pairs={{0,8},{1,9},{2,10},{3,11},{4,12},{5,13},{6,14},{7,15}} | collective-permute-start | bytes 1474568 | tf_op jit(solution)/shard_map/ppermute | solution.py:223
  122.1 1.2 copy-done.4
  123.3 5.2 %shard_map.84 = f32[2,4,160,192]{3,2,1,0:T(8,128)S(1)} custom-call(bf16[160,3072]{1,0:T(8,128)(2,1)S(1)} %copy-done.2, bf16[160,3072]{1,0:T(8,128)(2,1)S(1)} %collective-permute-done.1.acts_b, bf16[160,3072]{1,0:T(8,128)(2,1)S(1)} %collective-permute-done.2.acts_c, bf16[160,3072]{1,0:T(8,128)(2,1)S(1)} %copy-done.4, ...), custom_call_target="tpu_custom_call" | custom-call | tf_op jit(solution)/shard_map/pallas_call | solution.py:149
  128.6 2.6 %shard_map.78 = f32[1,160,1536]{2,1,0:T(8,128)S(1)} custom-call(s32[5]{0:T(128)S(1)} %stack.98.at, f32[8,2,160]{2,1,0:T(2,128)S(1)} %all-to-all-done.gates, bf16[2,120,1536]{2,1,0:T(8,128)(2,1)S(1)} %copy-done.13, bf16[2,120,1536]{2,1,0:T(8,128)(2,1)} %collective-permute-done.10.sibling), custom_call_target="tpu_custom_call" | custom-call | tf_op jit(solution)/shard_map/pallas_call | solution.py:78
  131.4 9.5 %collective-permute-done.15 = bf16[160,1536]{1,0:T(8,128)(2,1)} collective-permute-done((bf16[160,1536]{1,0:T(8,128)(2,1)}, bf16[160,1536]{1,0:T(8,128)(2,1)}, u32[]{:S(2)}, u32[]{:S(2)}) %collective-permute-start.15) | collective-permute-done | bytes 491552 | tf_op jit(solution)/shard_map/ppermute | solution.py:223
  140.9 3.2 %fusion.3 = (bf16[160,1536]{1,0:T(8,128)(2,1)S(1)}, f32[1,160,1536]{2,1,0:T(8,128)}, bf16[160,1536]{1,0:T(8,128)(2,1)}, f32[1,160,1536]{2,1,0:T(8,128)}) fusion(f32[1,160,1536]{2,1,0:T(8,128)S(1)} %copy-done.18, bf16[160,1536]{1,0:T(8,128)(2,1)} %collective-permute-done.16, pred[]{:T(512)S(6)} %eq.50, f32[1,160,1536]{2,1,0:T(8,128)S(1)} %shard_map.78, ...), kind=kLoop, calls=%fused_computation.11 | loop fusion | flops 2457600 | bytes 8355843 | tf_op jit(solution)/shard_map/convert_element_type | solution.py:231
  144.1 5.1 %shard_map.85 = f32[2,4,160,192]{3,2,1,0:T(8,128)S(1)} custom-call(bf16[160,3072]{1,0:T(8,128)(2,1)S(1)} %copy-done.2, bf16[160,3072]{1,0:T(8,128)(2,1)S(1)} %collective-permute-done.1.acts_b, bf16[160,3072]{1,0:T(8,128)(2,1)S(1)} %collective-permute-done.2.acts_c, bf16[160,3072]{1,0:T(8,128)(2,1)S(1)} %copy-done.5, ...), custom_call_target="tpu_custom_call" | custom-call | tf_op jit(solution)/shard_map/pallas_call | solution.py:149
  149.3 1.2 copy-done.10
  151.1 2.1 %copy-done.26 = f32[7,4,160,192]{3,2,1,0:T(8,128)} copy-done((f32[7,4,160,192]{3,2,1,0:T(8,128)}, f32[7,4,160,192]{3,2,1,0:T(8,128)S(1)}, u32[]{:S(2)}) %copy-start.26) | copy-done | bytes 3440664
  153.3 1.5 collective-permute-start.19
  155.0 4.7 %collective-permute-start.23 = (bf16[160,1536]{1,0:T(8,128)(2,1)S(1)}, bf16[160,1536]{1,0:T(8,128)(2,1)S(1)}, u32[]{:S(2)}, u32[]{:S(2)}) collective-permute-start(bf16[160,1536]{1,0:T(8,128)(2,1)S(1)} %copy-done.28), channel_id=1, source_target_pairs={{0,8},{8,16},{1,9},{9,17},{2,10},{10,18},{3,11},{11,19},{4,12},{12... | collective-permute-start | bytes 1474568 | tf_op jit(solution)/shard_map/ppermute | solution.py:233
  159.6 0.7 collective-permute-start.25
  160.3 9.3 %collective-permute-done.19 = bf16[2,4,160,192]{3,2,1,0:T(8,128)(2,1)S(1)} collective-permute-done((bf16[2,4,160,192]{3,2,1,0:T(8,128)(2,1)S(1)}, bf16[2,4,160,192]{3,2,1,0:T(8,128)(2,1)S(1)}, u32[]{:S(2)}, u32[]{:S(2)}) %collective-permute-start.19) | collective-permute-done | bytes 491552 | tf_op jit(solution)/shard_map/ppermute | solution.py:240
  169.6 1.4 convert_add_fusion.1
  171.2 0.7 collective-permute-start.21
  171.9 1.2 collective-permute-start.20
  173.1 0.5 fusion.8
  173.6 1.3 collective-permute-start.26
  174.9 5.0 %collective-permute-start.24 = (bf16[160,1536]{1,0:T(8,128)(2,1)S(1)}, bf16[160,1536]{1,0:T(8,128)(2,1)S(1)}, u32[]{:S(2)}, u32[]{:S(2)}) collective-permute-start(bf16[160,1536]{1,0:T(8,128)(2,1)S(1)} %get-tuple-element.75), channel_id=1, source_target_pairs={{0,8},{8,16},{16,24},{1,9},{9,17},{17,25},{2,10},{10,18},{18,26},{... | collective-permute-start | bytes 1474568 | tf_op jit(solution)/shard_map/ppermute | solution.py:244
  180.0 0.8 collective-permute-done.20
  181.2 8.5 %collective-permute-done.26 = bf16[160,1536]{1,0:T(8,128)(2,1)S(1)} collective-permute-done((bf16[160,1536]{1,0:T(8,128)(2,1)S(1)}, bf16[160,1536]{1,0:T(8,128)(2,1)S(1)}, u32[]{:S(2)}, u32[]{:S(2)}) %collective-permute-start.26) | collective-permute-done | bytes 491552 | tf_op jit(solution)/shard_map/ppermute | solution.py:245
  189.7 1.2 collective-permute-done.24
  190.9 1.4 fusion.1
  (96 shorter events, 2.2 us)
Async XLA Ops:
  0.0 1.9 copy-start
  1.9 1.5 copy-start.6
  3.4 6.4 %copy-start.2 = (bf16[160,3072]{1,0:T(8,128)(2,1)S(1)}, bf16[160,3072]{1,0:T(8,128)(2,1)}, u32[]{:S(2)}) copy-start(bf16[160,3072]{1,0:T(8,128)(2,1)} %acts_a.7) | copy-start | bytes 2949124
  9.4 38.6 %copy-start.7 = (bf16[4,120,1536]{2,1,0:T(8,128)(2,1)}, bf16[4,120,1536]{2,1,0:T(8,128)(2,1)S(1)}, u32[]{:S(2)}) copy-start(bf16[4,120,1536]{2,1,0:T(8,128)(2,1)S(1)} %get-tuple-element.34.mine) | copy-start | bytes 4423684
  9.4 38.6 %collective-permute-start = (bf16[4,120,1536]{2,1,0:T(8,128)(2,1)}, bf16[4,120,1536]{2,1,0:T(8,128)(2,1)}, u32[]{:S(2)}, u32[]{:S(2)}) collective-permute-start(bf16[4,120,1536]{2,1,0:T(8,128)(2,1)} %get-tuple-element.35), channel_id=1, source_target_pairs={{0,2},{2,0},{1,3},{3,1},{4,6},{6,4},{5,7},{7,5},{8,10},{10,8},{9,1... | collective-permute-start | bytes 4423688 | tf_op jit(solution)/shard_map/ppermute | solution.py:176
  9.8 42.9 %collective-permute-start.1 = (bf16[160,3072]{1,0:T(8,128)(2,1)S(1)}, bf16[160,3072]{1,0:T(8,128)(2,1)S(1)}, u32[]{:S(2)}, u32[]{:S(2)}) collective-permute-start(bf16[160,3072]{1,0:T(8,128)(2,1)S(1)} %copy-done.2), channel_id=1, source_target_pairs={{0,4},{4,0},{1,5},{5,1},{2,6},{6,2},{3,7},{7,3},{8,12},{12,8},{9,1... | collective-permute-start | bytes 2949128 | tf_op jit(solution)/shard_map/ppermute | solution.py:190
  12.4 40.8 %collective-permute-start.5 = (bf16[192,3072]{1,0:T(8,128)(2,1)}, bf16[192,3072]{1,0:T(8,128)(2,1)}, u32[]{:S(2)}, u32[]{:S(2)}) collective-permute-start(bf16[192,3072]{1,0:T(8,128)(2,1)} %bitcast.15.first.second), channel_id=1, source_target_pairs={{0,8},{8,16},{16,24},{1,9},{9,17},{17,25},{2,10},{10,18},{18,26},{... | collective-permute-start | bytes 3538952 | tf_op jit(solution)/shard_map/ppermute | solution.py:188
  16.9 36.3 %collective-permute-start.6 = (bf16[192,3072]{1,0:T(8,128)(2,1)}, bf16[192,3072]{1,0:T(8,128)(2,1)}, u32[]{:S(2)}, u32[]{:S(2)}) collective-permute-start(bf16[192,3072]{1,0:T(8,128)(2,1)} %bitcast.15.first.second), channel_id=1, source_target_pairs={{8,0},{16,8},{24,16},{9,1},{17,9},{25,17},{10,2},{18,10},{26,18},{... | collective-permute-start | bytes 3538952 | tf_op jit(solution)/shard_map/ppermute | solution.py:189
  18.2 4.5 %copy-start.29 = (f32[160,12]{0,1:T(8,128)S(1)}, f32[160,12]{0,1:T(8,128)}, u32[]{:S(2)}) copy-start(f32[160,12]{0,1:T(8,128)} %param.9) | copy-start | bytes 23044
  18.2 4.4 %copy-start.30 = (s32[160,12]{0,1:T(8,128)S(1)}, s32[160,12]{0,1:T(8,128)}, u32[]{:S(2)}) copy-start(s32[160,12]{0,1:T(8,128)} %param.8) | copy-start | bytes 23044
  21.2 32.1 %collective-permute-start.4 = (bf16[480,1024]{1,0:T(8,128)(2,1)}, bf16[480,1024]{1,0:T(8,128)(2,1)}, u32[]{:S(2)}, u32[]{:S(2)}) collective-permute-start(bf16[480,1024]{1,0:T(8,128)(2,1)} %get-tuple-element.77), channel_id=1, source_target_pairs={{0,1},{1,0},{2,3},{3,2},{4,5},{5,4},{6,7},{7,6},{8,9},{9,8},{10,11... | collective-permute-start | bytes 2949128 | tf_op jit(solution)/shard_map/ppermute | solution.py:186
  23.3 24.7 %all-to-all-start = ((f32[8,2,160]{2,1,0:T(2,128)}), f32[8,2,160]{2,1,0:T(2,128)S(1)}, u32[]{:S(2)}, u32[]{:S(2)}) async-start(f32[8,2,160]{2,1,0:T(2,128)} %reshape.27), calls=%async_computation | async-start | bytes 32768 | tf_op jit(solution)/shard_map/all_to_all | solution.py:192
  48.0 13.0 %copy-start.1 = (bf16[1,1024,1536]{2,1,0:T(8,128)(2,1)S(1)}, bf16[1,1024,1536]{2,1,0:T(8,128)(2,1)}, u32[]{:S(2)}) copy-start(bf16[1,1024,1536]{2,1,0:T(8,128)(2,1)} %param.11) | copy-start | bytes 9437188
  52.7 6.9 %collective-permute-start.2 = (bf16[160,3072]{1,0:T(8,128)(2,1)S(1)}, bf16[160,3072]{1,0:T(8,128)(2,1)S(1)}, u32[]{:S(2)}, u32[]{:S(2)}) collective-permute-start(bf16[160,3072]{1,0:T(8,128)(2,1)S(1)} %copy-done.2), channel_id=1, source_target_pairs={{0,2},{2,0},{1,3},{3,1},{4,6},{6,4},{5,7},{7,5},{8,10},{10,8},{9,1... | collective-permute-start | bytes 2949128 | tf_op jit(solution)/shard_map/ppermute | solution.py:197
  52.7 13.9 %collective-permute-start.3 = (bf16[160,3072]{1,0:T(8,128)(2,1)S(1)}, bf16[160,3072]{1,0:T(8,128)(2,1)S(1)}, u32[]{:S(2)}, u32[]{:S(2)}) collective-permute-start(bf16[160,3072]{1,0:T(8,128)(2,1)S(1)} %collective-permute-done.1.acts_b), channel_id=1, source_target_pairs={{0,2},{2,0},{1,3},{3,1},{4,6},{6,4},{5,7},{7,5},{8,10},{10,8},{9,1... | collective-permute-start | bytes 2949128 | tf_op jit(solution)/shard_map/ppermute | solution.py:199
  53.3 28.5 %collective-permute-start.7 = (bf16[192,3072]{1,0:T(8,128)(2,1)}, bf16[192,3072]{1,0:T(8,128)(2,1)}, u32[]{:S(2)}, u32[]{:S(2)}) collective-permute-start(bf16[192,3072]{1,0:T(8,128)(2,1)} %collective-permute-done.5.first), channel_id=1, source_target_pairs={{0,8},{8,16},{16,24},{1,9},{9,17},{17,25},{2,10},{10,18},{18,26},{... | collective-permute-start | bytes 3538952 | tf_op jit(solution)/shard_map/ppermute | solution.py:204
  56.8 29.9 %collective-permute-start.8 = (bf16[192,3072]{1,0:T(8,128)(2,1)}, bf16[192,3072]{1,0:T(8,128)(2,1)}, u32[]{:S(2)}, u32[]{:S(2)}) collective-permute-start(bf16[192,3072]{1,0:T(8,128)(2,1)} %collective-permute-done.6.second), channel_id=1, source_target_pairs={{8,0},{16,8},{24,16},{9,1},{17,9},{25,17},{10,2},{18,10},{26,18},{... | collective-permute-start | bytes 3538952 | tf_op jit(solution)/shard_map/ppermute | solution.py:205
  58.1 23.7 %collective-permute-start.9 = (bf16[480,1024]{1,0:T(8,128)(2,1)}, bf16[480,1024]{1,0:T(8,128)(2,1)S(1)}, u32[]{:S(2)}, u32[]{:S(2)}) collective-permute-start(bf16[480,1024]{1,0:T(8,128)(2,1)} %get-tuple-element.40), channel_id=1, source_target_pairs={{0,1},{1,0},{2,3},{3,2},{4,5},{5,4},{6,7},{7,6},{8,9},{9,8},{10,11... | collective-permute-start | bytes 2949128 | tf_op jit(solution)/shard_map/ppermute | solution.py:203
  59.6 41.8 %collective-permute-start.12 = (bf16[2,160,1536]{2,1,0:T(8,128)(2,1)}, bf16[2,160,1536]{2,1,0:T(8,128)(2,1)}, u32[]{:S(2)}, u32[]{:S(2)}) collective-permute-start(bf16[2,160,1536]{2,1,0:T(8,128)(2,1)} %shard_map.74), channel_id=1, source_target_pairs={{0,4},{4,0},{1,5},{5,1},{2,6},{6,2},{3,7},{7,3},{8,12},{12,8},{9,1... | collective-permute-start | bytes 2949128 | tf_op jit(solution)/shard_map/ppermute | solution.py:198
  65.8 0.9 copy-start.14
  66.7 5.4 %copy-start.3 = (bf16[160,3072]{1,0:T(8,128)(2,1)}, bf16[160,3072]{1,0:T(8,128)(2,1)S(1)}, u32[]{:S(2)}) copy-start(bf16[160,3072]{1,0:T(8,128)(2,1)S(1)} %collective-permute-done.3.acts_d) | copy-start | bytes 2949124
  66.7 29.6 %collective-permute-start.11 = (bf16[2,120,1536]{2,1,0:T(8,128)(2,1)}, bf16[2,120,1536]{2,1,0:T(8,128)(2,1)}, u32[]{:S(2)}, u32[]{:S(2)}) collective-permute-start(bf16[2,120,1536]{2,1,0:T(8,128)(2,1)} %get-tuple-element.46), channel_id=1, source_target_pairs={{0,2},{2,0},{1,3},{3,1},{4,6},{6,4},{5,7},{7,5},{8,10},{10,8},{9,1... | collective-permute-start | bytes 2211848 | tf_op jit(solution)/shard_map/ppermute | solution.py:176
  72.0 1.1 copy-start.16
  78.1 1.1 copy-start.9
  90.0 0.9 copy-start.11
  90.9 17.3 %collective-permute-start.10 = (bf16[2,120,1536]{2,1,0:T(8,128)(2,1)}, bf16[2,120,1536]{2,1,0:T(8,128)(2,1)}, u32[]{:S(2)}, u32[]{:S(2)}) collective-permute-start(bf16[2,120,1536]{2,1,0:T(8,128)(2,1)} %get-tuple-element.43), channel_id=1, source_target_pairs={{0,2},{2,0},{1,3},{3,1},{4,6},{6,4},{5,7},{7,5},{8,10},{10,8},{9,1... | collective-permute-start | bytes 2211848 | tf_op jit(solution)/shard_map/ppermute | solution.py:176
  91.2 1.4 copy-start.8
  92.6 3.7 %copy-start.15 = (bf16[2,120,1536]{2,1,0:T(8,128)(2,1)S(1)}, bf16[2,120,1536]{2,1,0:T(8,128)(2,1)}, u32[]{:S(2)}) copy-start(bf16[2,120,1536]{2,1,0:T(8,128)(2,1)} %copy-done.14) | copy-start | bytes 2211844
  101.4 6.8 %copy-start.12 = (bf16[2,120,1536]{2,1,0:T(8,128)(2,1)S(1)}, bf16[2,120,1536]{2,1,0:T(8,128)(2,1)}, u32[]{:S(2)}) copy-start(bf16[2,120,1536]{2,1,0:T(8,128)(2,1)} %copy-done.11) | copy-start | bytes 2211844
  101.4 13.7 %collective-permute-start.13 = (bf16[1,160,1536]{2,1,0:T(8,128)(2,1)S(1)}, bf16[1,160,1536]{2,1,0:T(8,128)(2,1)S(1)}, u32[]{:S(2)}, u32[]{:S(2)}) collective-permute-start(bf16[1,160,1536]{2,1,0:T(8,128)(2,1)S(1)} %shard_map.81), channel_id=1, source_target_pairs={{0,4},{4,0},{1,5},{5,1},{2,6},{6,2},{3,7},{7,3},{8,12},{12,8},{9,1... | collective-permute-start | bytes 1474568 | tf_op jit(solution)/shard_map/ppermute | solution.py:209
  102.9 41.2 %collective-permute-start.17 = (bf16[192,3072]{1,0:T(8,128)(2,1)}, bf16[192,3072]{1,0:T(8,128)(2,1)}, u32[]{:S(2)}, u32[]{:S(2)}) collective-permute-start(bf16[192,3072]{1,0:T(8,128)(2,1)} %collective-permute-done.7.first), channel_id=1, source_target_pairs={{0,8},{8,16},{16,24},{1,9},{9,17},{17,25},{2,10},{10,18},{18,26},{... | collective-permute-start | bytes 3538952 | tf_op jit(solution)/shard_map/ppermute | solution.py:214
  105.4 38.7 %collective-permute-start.18 = (bf16[192,3072]{1,0:T(8,128)(2,1)}, bf16[192,3072]{1,0:T(8,128)(2,1)}, u32[]{:S(2)}, u32[]{:S(2)}) collective-permute-start(bf16[192,3072]{1,0:T(8,128)(2,1)} %collective-permute-done.8.second), channel_id=1, source_target_pairs={{8,0},{16,8},{24,16},{9,1},{17,9},{25,17},{10,2},{18,10},{26,18},{... | collective-permute-start | bytes 3538952 | tf_op jit(solution)/shard_map/ppermute | solution.py:215
  108.1 8.8 %copy-start.24 = (f32[2,160,1536]{2,1,0:T(8,128)}, f32[2,160,1536]{2,1,0:T(8,128)S(1)}, u32[]{:S(2)}) copy-start(f32[2,160,1536]{2,1,0:T(8,128)S(1)} %convert_add_fusion) | copy-start | bytes 5898244
  116.9 14.3 %collective-permute-start.16 = (bf16[160,1536]{1,0:T(8,128)(2,1)}, bf16[160,1536]{1,0:T(8,128)(2,1)}, u32[]{:S(2)}, u32[]{:S(2)}) collective-permute-start(bf16[160,1536]{1,0:T(8,128)(2,1)} %get-tuple-element.65), channel_id=1, source_target_pairs={{24,16},{25,17},{26,18},{27,19},{28,20},{29,21},{30,22},{31,23}} | collective-permute-start | bytes 1474568 | tf_op jit(solution)/shard_map/ppermute | solution.py:224
  118.4 13.0 %collective-permute-start.14 = (bf16[1,160,1536]{2,1,0:T(8,128)(2,1)S(1)}, bf16[1,160,1536]{2,1,0:T(8,128)(2,1)}, u32[]{:S(2)}, u32[]{:S(2)}) collective-permute-start(bf16[1,160,1536]{2,1,0:T(8,128)(2,1)S(1)} %shard_map.79), channel_id=1, source_target_pairs={{0,4},{4,0},{1,5},{5,1},{2,6},{6,2},{3,7},{7,3},{8,12},{12,8},{9,1... | collective-permute-start | bytes 1474568 | tf_op jit(solution)/shard_map/ppermute | solution.py:219
  119.8 21.1 %collective-permute-start.15 = (bf16[160,1536]{1,0:T(8,128)(2,1)}, bf16[160,1536]{1,0:T(8,128)(2,1)}, u32[]{:S(2)}, u32[]{:S(2)}) collective-permute-start(bf16[160,1536]{1,0:T(8,128)(2,1)} %get-tuple-element.73), channel_id=1, source_target_pairs={{0,8},{1,9},{2,10},{3,11},{4,12},{5,13},{6,14},{7,15}} | collective-permute-start | bytes 1474568 | tf_op jit(solution)/shard_map/ppermute | solution.py:223
  122.1 1.2 copy-start.4
  123.3 5.2 %copy-start.13 = (bf16[2,120,1536]{2,1,0:T(8,128)(2,1)S(1)}, bf16[2,120,1536]{2,1,0:T(8,128)(2,1)}, u32[]{:S(2)}) copy-start(bf16[2,120,1536]{2,1,0:T(8,128)(2,1)} %copy-done.11) | copy-start | bytes 2211844
  123.3 17.6 %copy-start.25 = (f32[2,160,1536]{2,1,0:T(8,128)S(1)}, f32[2,160,1536]{2,1,0:T(8,128)}, u32[]{:S(2)}) copy-start(f32[2,160,1536]{2,1,0:T(8,128)} %copy-done.24) | copy-start | bytes 5898244
  128.6 12.4 %copy-start.18 = (f32[1,160,1536]{2,1,0:T(8,128)S(1)}, f32[1,160,1536]{2,1,0:T(8,128)}, u32[]{:S(2)}) copy-start(f32[1,160,1536]{2,1,0:T(8,128)} %get-tuple-element.66) | copy-start | bytes 2949124
  128.6 12.4 %copy-start.20 = (f32[1,160,1536]{2,1,0:T(8,128)S(1)}, f32[1,160,1536]{2,1,0:T(8,128)}, u32[]{:S(2)}) copy-start(f32[1,160,1536]{2,1,0:T(8,128)} %get-tuple-element.74) | copy-start | bytes 2949124
  140.9 3.2 %copy-start.5 = (bf16[160,3072]{1,0:T(8,128)(2,1)S(1)}, bf16[160,3072]{1,0:T(8,128)(2,1)}, u32[]{:S(2)}) copy-start(bf16[160,3072]{1,0:T(8,128)(2,1)} %copy-done.3) | copy-start | bytes 2949124
  149.2 1.3 copy-start.10
  149.2 1.7 copy-start.17
  151.0 3.9 %copy-start.28 = (bf16[160,1536]{1,0:T(8,128)(2,1)S(1)}, bf16[160,1536]{1,0:T(8,128)(2,1)}, u32[]{:S(2)}) copy-start(bf16[160,1536]{1,0:T(8,128)(2,1)} %get-tuple-element.61) | copy-start | bytes 1474564
  151.1 2.2 %copy-start.26 = (f32[7,4,160,192]{3,2,1,0:T(8,128)}, f32[7,4,160,192]{3,2,1,0:T(8,128)S(1)}, u32[]{:S(2)}) copy-start(f32[7,4,160,192]{3,2,1,0:T(8,128)S(1)} %slice_dynamic-update-slice_fusion) | copy-start | bytes 10321924
  153.3 16.3 %collective-permute-start.19 = (bf16[2,4,160,192]{3,2,1,0:T(8,128)(2,1)S(1)}, bf16[2,4,160,192]{3,2,1,0:T(8,128)(2,1)S(1)}, u32[]{:S(2)}, u32[]{:S(2)}) collective-permute-start(bf16[2,4,160,192]{3,2,1,0:T(8,128)(2,1)S(1)} %dynamic-slice_convert_fusion), channel_id=1, source_target_pairs={{0,1},{1,0},{2,3},{3,2},{4,5},{5,4},{6,7},{7,6},{8,9},{9,8},{10,11... | collective-permute-start | bytes 1474568 | tf_op jit(solution)/shard_map/ppermute | solution.py:240
  154.9 18.1 %copy-start.19 = (f32[1,160,1536]{2,1,0:T(8,128)S(1)}, f32[1,160,1536]{2,1,0:T(8,128)}, u32[]{:S(2)}) copy-start(f32[1,160,1536]{2,1,0:T(8,128)} %get-tuple-element.66) | copy-start | bytes 2949124
  154.9 18.1 %copy-start.21 = (f32[1,160,1536]{2,1,0:T(8,128)S(1)}, f32[1,160,1536]{2,1,0:T(8,128)}, u32[]{:S(2)}) copy-start(f32[1,160,1536]{2,1,0:T(8,128)} %get-tuple-element.74) | copy-start | bytes 2949124
  154.9 18.1 %copy-start.22 = (f32[1,160,1536]{2,1,0:T(8,128)S(1)}, f32[1,160,1536]{2,1,0:T(8,128)}, u32[]{:S(2)}) copy-start(f32[1,160,1536]{2,1,0:T(8,128)} %get-tuple-element.64) | copy-start | bytes 2949124
  154.9 18.1 %copy-start.23 = (f32[1,160,1536]{2,1,0:T(8,128)S(1)}, f32[1,160,1536]{2,1,0:T(8,128)}, u32[]{:S(2)}) copy-start(f32[1,160,1536]{2,1,0:T(8,128)} %get-tuple-element.72) | copy-start | bytes 2949124
  155.0 18.1 %collective-permute-start.23 = (bf16[160,1536]{1,0:T(8,128)(2,1)S(1)}, bf16[160,1536]{1,0:T(8,128)(2,1)S(1)}, u32[]{:S(2)}, u32[]{:S(2)}) collective-permute-start(bf16[160,1536]{1,0:T(8,128)(2,1)S(1)} %copy-done.28), channel_id=1, source_target_pairs={{0,8},{8,16},{1,9},{9,17},{2,10},{10,18},{3,11},{11,19},{4,12},{12... | collective-permute-start | bytes 1474568 | tf_op jit(solution)/shard_map/ppermute | solution.py:233
  159.6 13.4 %collective-permute-start.25 = (bf16[160,1536]{1,0:T(8,128)(2,1)S(1)}, bf16[160,1536]{1,0:T(8,128)(2,1)S(1)}, u32[]{:S(2)}, u32[]{:S(2)}) collective-permute-start(bf16[160,1536]{1,0:T(8,128)(2,1)S(1)} %get-tuple-element.62), channel_id=1, source_target_pairs={{24,16},{16,8},{25,17},{17,9},{26,18},{18,10},{27,19},{19,11},{28,... | collective-permute-start | bytes 1474568 | tf_op jit(solution)/shard_map/ppermute | solution.py:234
  171.1 8.9 %collective-permute-start.22 = (bf16[2,160,192]{2,1,0:T(8,128)(2,1)S(1)}, bf16[2,160,192]{2,1,0:T(8,128)(2,1)S(1)}, u32[]{:S(2)}, u32[]{:S(2)}) collective-permute-start(bf16[2,160,192]{2,1,0:T(8,128)(2,1)S(1)} %get-tuple-element.84), channel_id=1, source_target_pairs={{0,2},{2,0},{1,3},{3,1},{4,6},{6,4},{5,7},{7,5},{8,10},{10,8},{9,1... | collective-permute-start | bytes 368648 | tf_op jit(solution)/shard_map/ppermute | solution.py:251
  171.2 8.8 %collective-permute-start.21 = (bf16[2,160,192]{2,1,0:T(8,128)(2,1)S(1)}, bf16[2,160,192]{2,1,0:T(8,128)(2,1)S(1)}, u32[]{:S(2)}, u32[]{:S(2)}) collective-permute-start(bf16[2,160,192]{2,1,0:T(8,128)(2,1)S(1)} %get-tuple-element.85), channel_id=1, source_target_pairs={{0,4},{4,0},{1,5},{5,1},{2,6},{6,2},{3,7},{7,3},{8,12},{12,8},{9,1... | collective-permute-start | bytes 368648 | tf_op jit(solution)/shard_map/ppermute | solution.py:252
  171.9 9.0 %collective-permute-start.20 = (bf16[2,160,192]{2,1,0:T(8,128)(2,1)S(1)}, bf16[2,160,192]{2,1,0:T(8,128)(2,1)S(1)}, u32[]{:S(2)}, u32[]{:S(2)}) collective-permute-start(bf16[2,160,192]{2,1,0:T(8,128)(2,1)S(1)} %get-tuple-element.83), channel_id=1, source_target_pairs={{0,6},{2,4},{4,2},{6,0},{1,7},{3,5},{5,3},{7,1},{8,14},{10,12},{12... | collective-permute-start | bytes 368648 | tf_op jit(solution)/shard_map/ppermute | solution.py:253
  173.6 16.1 %collective-permute-start.26 = (bf16[160,1536]{1,0:T(8,128)(2,1)S(1)}, bf16[160,1536]{1,0:T(8,128)(2,1)S(1)}, u32[]{:S(2)}, u32[]{:S(2)}) collective-permute-start(bf16[160,1536]{1,0:T(8,128)(2,1)S(1)} %get-tuple-element.76), channel_id=1, source_target_pairs={{8,0},{16,8},{24,16},{9,1},{17,9},{25,17},{10,2},{18,10},{26,18},{... | collective-permute-start | bytes 1474568 | tf_op jit(solution)/shard_map/ppermute | solution.py:245
  174.9 16.0 %collective-permute-start.24 = (bf16[160,1536]{1,0:T(8,128)(2,1)S(1)}, bf16[160,1536]{1,0:T(8,128)(2,1)S(1)}, u32[]{:S(2)}, u32[]{:S(2)}) collective-permute-start(bf16[160,1536]{1,0:T(8,128)(2,1)S(1)} %get-tuple-element.75), channel_id=1, source_target_pairs={{0,8},{8,16},{16,24},{1,9},{9,17},{17,25},{2,10},{10,18},{18,26},{... | collective-permute-start | bytes 1474568 | tf_op jit(solution)/shard_map/ppermute | solution.py:244
  180.9 10.0 %copy-start.27 = (bf16[160,1536]{1,0:T(8,128)(2,1)S(1)}, bf16[160,1536]{1,0:T(8,128)(2,1)}, u32[]{:S(2)}) copy-start(bf16[160,1536]{1,0:T(8,128)(2,1)} %param.7) | copy-start | bytes 1474564

commit v3 on v2

--- a/solution.py
+++ b/solution.py
@@ -8,6 +8,7 @@
 F32 = jnp.float32
 BF16 = jnp.bfloat16
 SWAP = ((0, 1), (1, 0))
+VMEM = 32 << 20
 FREE = pl.CostEstimate(flops=0, bytes_accessed=0, transcendentals=0)
 
 
@@ -51,49 +52,54 @@
     return high, low
 
 
-def combine_kernel(at, gates, mine, sibling, out):
+def combine_kernel(here, gates, columns, mine, sibling, out):
     capacity, tokens = mine.shape[1], gates.shape[2]
-    steps = pl.num_programs(0)
     order = lax.broadcasted_iota(jnp.int32, (tokens, tokens), 0)
     earlier = (order < lax.broadcasted_iota(jnp.int32, (tokens, tokens), 1)).astype(BF16)
     places = lax.broadcasted_iota(jnp.int32, (capacity, tokens), 0)
+    c = here[2]
     total = None
-    for e, table in enumerate((mine, sibling)):
-        gate = gates[0, pl.ds(at[3 * steps + e], 1), :]
-        picked = gate >= 0
+    for e, table in ((c, mine), (1 - c, sibling)):
+        picked = gates[0, pl.ds(e, 1), :] >= 0
         marks = jnp.broadcast_to(jnp.where(picked, F32(1.0), F32(0.0)), (8, tokens)).astype(BF16)
         slot = jnp.dot(marks, earlier, preferred_element_type=F32)[0:1].astype(jnp.int32)
-        place = jnp.where((slot == places) & picked, gate, F32(0.0))
-        high = place.astype(BF16)
-        low = (place - high.astype(F32)).astype(BF16)
-        for part in (high, low):
-            term = lax.dot_general(part, table[0], (((0,), (0,)), ((), ())), preferred_element_type=F32)
-            total = term if total is None else total + term
-    out[0] = total.astype(out.dtype)
-
-
-def combine(at, steps, gates, table, sibling, dtype):
+        place = jnp.where((slot == places) & picked, F32(1.0), F32(0.0)).astype(BF16)
+        term = lax.dot_general(place, table[0], (((0,), (0,)), ((), ())), preferred_element_type=F32)
+        term = jnp.where(e == 0, columns[0, :, 0:1], columns[0, :, 1:2]) * term
+        total = term if total is None else total + term
+    out[...] = total.astype(out.dtype)
+
+
+def combine(here, goal, place, away, gates, columns, table, sibling, dtype):
     _, capacity, features = table.shape
     tokens = gates.shape[2]
+
+    def gate_block(i, here):
+        return goal(here[0]) * 2 + (1 - here[1] if away else here[1]), 0, 0
+
+    def table_block(i, here):
+        return place(here[0]) * 2 + (1 - here[1] if away else here[1]), 0, 0
+
     return pl.pallas_call(
         combine_kernel,
-        out_shape=jax.ShapeDtypeStruct((steps, tokens, features), dtype),
+        out_shape=jax.ShapeDtypeStruct((tokens, features), dtype),
         grid_spec=pltpu.PrefetchScalarGridSpec(
             num_scalar_prefetch=1,
-            grid=(steps,),
+            grid=(1,),
             in_specs=[
-                pl.BlockSpec((1,) + gates.shape[1:], lambda i, at: (at[i], 0, 0)),
-                pl.BlockSpec((1, capacity, features), lambda i, at: (at[steps + i], 0, 0)),
-                pl.BlockSpec((1, capacity, features), lambda i, at: (at[2 * steps + i], 0, 0)),
+                pl.BlockSpec((1,) + gates.shape[1:], gate_block),
+                pl.BlockSpec((1,) + columns.shape[1:], gate_block),
+                pl.BlockSpec((1, capacity, features), table_block),
+                pl.BlockSpec((1, capacity, features), table_block),
             ],
-            out_specs=pl.BlockSpec((1, tokens, features), lambda i, at: (i, 0, 0)),
+            out_specs=pl.BlockSpec((tokens, features), lambda i, here: (0, 0)),
         ),
-        compiler_params=pltpu.CompilerParams(vmem_limit_bytes=32 << 20),
+        compiler_params=pltpu.CompilerParams(vmem_limit_bytes=VMEM),
         cost_estimate=FREE,
-    )(at, gates, table, sibling)
-
-
-def tables_kernel(core, hidden, down, sent, kept):
+    )(here, gates, columns, table, sibling)
+
+
+def tables_kernel(here, hidden, down, sent, kept):
     steps = pl.num_programs(0)
     value = jnp.dot(hidden[0, 0], down[...], preferred_element_type=F32).astype(sent.dtype)
 
@@ -106,7 +112,7 @@
         kept[0] = value
 
 
-def expert_tables(core, hidden, down):
+def expert_tables(here, hidden, down):
     blocks, _, capacity, units = hidden.shape
     features = down.shape[1]
     shape = jax.ShapeDtypeStruct((blocks, capacity, features), hidden.dtype)
@@ -119,42 +125,45 @@
             in_specs=[
                 pl.BlockSpec(
                     (1, 1, capacity, units),
-                    lambda i, core: (lax.rem(i, blocks), jnp.where(i < blocks, 1 - core[0], core[0]), 0, 0),
+                    lambda i, here: (lax.rem(i, blocks), jnp.where(i < blocks, 1 - here[2], here[2]), 0, 0),
                 ),
-                pl.BlockSpec((units, features), lambda i, core: (0, 0)),
+                pl.BlockSpec((units, features), lambda i, here: (0, 0)),
             ],
             out_specs=[
-                pl.BlockSpec((1, capacity, features), lambda i, core: (jnp.minimum(i, blocks - 1), 0, 0)),
-                pl.BlockSpec((1, capacity, features), lambda i, core: (jnp.maximum(i - blocks, 0), 0, 0)),
+                pl.BlockSpec((1, capacity, features), lambda i, here: (jnp.minimum(i, blocks - 1), 0, 0)),
+                pl.BlockSpec((1, capacity, features), lambda i, here: (jnp.maximum(i - blocks, 0), 0, 0)),
             ],
         ),
-        compiler_params=pltpu.CompilerParams(vmem_limit_bytes=32 << 20),
+        compiler_params=pltpu.CompilerParams(vmem_limit_bytes=VMEM),
         cost_estimate=FREE,
-    )(core, hidden, down)
-
-
-def product_kernel(acts_a, acts_b, acts_c, acts_d, first, second, out):
+    )(here, hidden, down)
+
+
+def products_kernel(acts_a, acts_b, acts_c, acts_d, *weights_and_outs):
     start = pl.program_id(0) == 0
-    for w, weights in enumerate((first, second)):
+    count = len(weights_and_outs) // 2
+    for weights, out in zip(weights_and_outs[:count], weights_and_outs[count:]):
         for i, acts in enumerate((acts_a, acts_b, acts_c, acts_d)):
             term = lax.dot_general(acts[...], weights[...], (((1,), (1,)), ((), ())), preferred_element_type=F32)
-            out[w, i] = jnp.where(start, term, out[w, i] + term)
-
-
-def products(acts, first, second):
+            out[i] = jnp.where(start, term, out[i] + term)
+
+
+def products(acts, *weights):
     rows, depth = acts[0].shape
-    columns = first.shape[0]
+    columns = weights[0].shape[0]
     step = depth // 4
-    shape = (2, 4, rows, columns)
+    shape = (4, rows, columns)
+    count = len(weights)
     return pl.pallas_call(
-        product_kernel,
-        out_shape=jax.ShapeDtypeStruct(shape, F32),
+        products_kernel,
+        out_shape=[jax.ShapeDtypeStruct(shape, F32)] * count,
         grid=(depth // step,),
-        in_specs=[pl.BlockSpec((rows, step), lambda i: (0, i))] * 4 + [pl.BlockSpec((columns, step), lambda i: (0, i))] * 2,
-        out_specs=pl.BlockSpec(shape, lambda i: (0, 0, 0, 0)),
-        compiler_params=pltpu.CompilerParams(vmem_limit_bytes=32 << 20),
+        in_specs=[pl.BlockSpec((rows, step), lambda i: (0, i))] * 4
+        + [pl.BlockSpec((columns, step), lambda i: (0, i))] * count,
+        out_specs=[pl.BlockSpec(shape, lambda i: (0, 0, 0))] * count,
+        compiler_params=pltpu.CompilerParams(vmem_limit_bytes=VMEM),
         cost_estimate=FREE,
-    )(*acts, first, second)
+    )(*acts, *weights)
 
 
 def four_by_two(tokens, expert_ids, gate_weights, expert_hidden, expert_down, dense_hidden, dense_down):
@@ -169,82 +178,112 @@
     left = [(1, 0), (2, 1), (3, 2)]
     tie = lax.optimization_barrier
 
-    core = jnp.reshape(c, (1,))
+    here = jnp.stack([x, y, c]).astype(jnp.int32)
 
     def tables(chunk):
-        sent, kept = expert_tables(core, chunk.reshape(-1, 2, capacity, chunk.shape[-1]), down)
-        return kept, lax.ppermute(sent, "c", SWAP)
-
-    def sums(tables, gates, goals, away, dtype):
-        side = 1 - y if away else y
-        at = [goal * 2 + side for goal, _ in goals]
-        at += [place * 2 + side for _, place in goals] * 2
-        at = jnp.stack(at + [c, 1 - c]).astype(jnp.int32)
-        return combine(at, len(goals), gates, *tables, dtype)
+        return expert_tables(here, chunk.reshape(-1, 2, capacity, chunk.shape[-1]), down)
+
+    def over_c(value):
+        return lax.ppermute(value, "c", SWAP)
+
+    def sums(tables, gates, goal, away, dtype):
+        return combine(here, *goal, away, *gates, *tables, dtype)
+
+    def hop(value, *ways):
+        pairs = [(i * 2 + at, j * 2 + at) for at in range(2) for i, j in ways[at]]
+        return lax.ppermute(value.astype(BF16), ("z", "tp"), pairs)
+
+    def over_y(value):
+        return lax.ppermute(value, "y", SWAP)
+
+    own_goals = (lambda x: 3 * x, lambda x: x), (lambda x: 1 + x, lambda x: 1 - x)
+    outer_goal = lambda x: 3 * (1 - x), lambda x: 0
+    inner_goal = lambda x: 2 - x, lambda x: 0
+    far = jnp.where(x == 0, 3, 0)
+    distance = jnp.abs(z - far)
 
     halves = hidden.reshape(2, 4 * capacity, hidden.shape[1])
-    hidden_0 = lax.ppermute(pick(halves, x), "tp", SWAP)
     weights = dense_down.T
+    gates = gate_rows(expert_ids, gate_weights, experts).reshape(8, 2, rows)
+    weights, hidden_0, gates = tie((weights, pick(halves, x), gates))
     weights_r1 = lax.ppermute(weights, "z", right)
     weights_l1 = lax.ppermute(weights, "z", left)
-    acts_y = lax.ppermute(dense_hidden, "y", SWAP)
-    gates = gate_rows(expert_ids, gate_weights, experts).reshape(8, 2, rows)
+    hidden_0 = lax.ppermute(hidden_0, "tp", SWAP)
+    acts_y = over_y(dense_hidden)
+    acts_c = over_c(dense_hidden)
     gates = lax.all_to_all(gates, ("z", "y"), 0, 0, tiled=True)
-    own = tables(hidden)
-    own_goals = ((3 * x, x), (1 + x, 1 - x))
-    given_own = sums(own, gates, own_goals, 1, BF16)
-    given_own, acts_y, acts_c = tie((given_own, acts_y, dense_hidden))
-    acts_c = lax.ppermute(acts_c, "c", SWAP)
-    got_own = lax.ppermute(given_own, "y", SWAP)
-    acts_cy = lax.ppermute(acts_y, "c", SWAP)
-    acts = (dense_hidden, acts_y, acts_c, acts_cy)
-
-    hidden_1, hidden_0, weights_r1, weights_l1 = tie((pick(halves, 1 - x), hidden_0, weights_r1, weights_l1))
+    own_sent, own = tables(hidden)
+    hidden_1 = pick(halves, 1 - x)
+    gates = gates, jnp.swapaxes(gates, 1, 2)
+    hidden_0, acts_y, weights_r1, weights_l1, gates, own, own_sent, hidden_1, acts_c = tie(
+        (hidden_0, acts_y, weights_r1, weights_l1, gates, own, own_sent, hidden_1, acts_c)
+    )
+    own = own, over_c(own_sent)
+
+    weights_r2 = lax.ppermute(weights_r1, "z", right[1:])
+    weights_l2 = lax.ppermute(weights_l1, "z", left[:2])
     hidden_1 = lax.ppermute(hidden_1, "tp", SWAP)
-    weights_r2 = lax.ppermute(weights_r1, "z", right)
-    weights_l2 = lax.ppermute(weights_l1, "z", left)
-    outer = tables(hidden_0)
-    given_outer = sums(outer, gates, ((3 * (1 - x), 0),), 1, BF16)
-    given_outer, got_own = tie((given_outer, got_own))
-    got_outer = lax.ppermute(given_outer, "y", SWAP)
-    sum_own = sums(own, gates, own_goals, 0, F32) + got_own.astype(F32)
-    sheets = [products(acts, weights, weights), products(acts, weights_r1, weights_l1)]
-
-    weights_r2, weights_l2, hidden_1, sheets = tie((weights_r2, weights_l2, hidden_1, sheets))
-    weights_r3 = lax.ppermute(weights_r2, "z", right)
-    weights_l3 = lax.ppermute(weights_l2, "z", left)
-    inner = tables(hidden_1)
-    given_inner = sums(inner, gates, ((2 - x, 0),), 1, BF16)
-    given_inner, got_outer = tie((given_inner, got_outer))
-    got_inner = lax.ppermute(given_inner, "y", SWAP)
-    sum_outer = (sums(outer, gates, ((3 * (1 - x), 0),), 0, F32) + got_outer.astype(F32))[0]
-    goal_0 = jnp.where(x == 0, sum_own[0], sum_outer)
-    goal_3 = jnp.where(x == 0, sum_outer, sum_own[0])
-    up = lax.ppermute(goal_3.astype(BF16), "z", [(0, 1)])
-    low = lax.ppermute(goal_0.astype(BF16), "z", [(3, 2)])
-    sheets = sheets + [products(acts, weights_r2, weights_l2)]
-    sum_inner = (sums(inner, gates, ((2 - x, 0),), 0, F32) + got_inner.astype(F32))[0]
-    goal_1 = jnp.where(x == 0, sum_own[1], sum_inner)
-    goal_2 = jnp.where(x == 0, sum_inner, sum_own[1])
-
-    up = jnp.where(z == 0, goal_2, goal_3 + up.astype(F32)).astype(BF16)
-    low = jnp.where(z == 3, goal_1, goal_0 + low.astype(F32)).astype(BF16)
-    up, low, weights_r3, weights_l3, sheets = tie((up, low, weights_r3, weights_l3, sheets))
-    up = lax.ppermute(up, "z", [(0, 1), (1, 2)])
-    low = lax.ppermute(low, "z", [(3, 2), (2, 1)])
-    sheets = sheets + [products(acts, weights_r3, weights_l3)]
-    sheet = [sheets[i][0] for i in (3, 2, 1, 0)] + [sheets[i][1] for i in (1, 2, 3)]
-    sheet = jnp.stack(sheet)
-    theirs = lax.dynamic_slice_in_dim(sheet, 3 - z + 2 * (1 - x), 2).astype(BF16)
-    dense = lax.dynamic_slice_in_dim(sheet, 3 - z + 2 * x, 2)
-    dense = dense + lax.ppermute(theirs, "tp", SWAP).astype(F32)
-
-    up = jnp.where(z == 0, goal_1, jnp.where(z == 1, goal_2, goal_3) + up.astype(F32)).astype(BF16)
-    low = jnp.where(z == 3, goal_2, jnp.where(z == 2, goal_1, goal_0) + low.astype(F32)).astype(BF16)
-    up = lax.ppermute(up, "z", right)
-    low = lax.ppermute(low, "z", left)
-    routed = jnp.where(z == 0, goal_0, jnp.where(z == 1, goal_1, jnp.where(z == 2, goal_2, goal_3)))
-    routed = routed + (up.astype(F32) + low.astype(F32))
+    got_own_0 = over_y(sums(own, gates, own_goals[0], 1, BF16))
+    sum_own_0 = sums(own, gates, own_goals[0], 0, F32)
+    outer_sent, outer = tables(hidden_0)
+    outer = outer, over_c(outer_sent)
+    got_own_0, given_outer, sum_own_0 = tie((got_own_0, sums(outer, gates, outer_goal, 1, BF16), sum_own_0))
+
+    got_outer = over_y(given_outer)
+    own_0 = sum_own_0 + got_own_0.astype(F32)
+    own_a = hop(own_0, [(3, 2)], [(0, 1)])
+    sum_outer = sums(outer, gates, outer_goal, 0, F32)
+    given_own_1 = sums(own, gates, own_goals[1], 1, BF16)
+    got_outer, own_a, weights_r2, weights_l2, hidden_1, given_own_1, sum_outer, own_0, acts_y = tie(
+        (got_outer, own_a, weights_r2, weights_l2, hidden_1, given_own_1, sum_outer, own_0, acts_y)
+    )
+
+    weights_r3 = lax.ppermute(weights_r2, "z", right[2:])
+    weights_l3 = lax.ppermute(weights_l2, "z", left[:1])
+    got_own_1 = over_y(given_own_1)
+    outer_0 = sum_outer + got_outer.astype(F32)
+    other_a = hop(outer_0, [(0, 1)], [(3, 2)])
+    inner_sent, inner = tables(hidden_1)
+    inner = inner, over_c(inner_sent)
+    sum_own_1 = sums(own, gates, own_goals[1], 0, F32)
+    got_own_1, given_inner, acts_y, sum_own_1 = tie((got_own_1, sums(inner, gates, inner_goal, 1, BF16), acts_y, sum_own_1))
+
+    got_inner = over_y(given_inner)
+    acts = (dense_hidden, acts_y, acts_c, over_c(acts_y))
+    sum_inner = sums(inner, gates, inner_goal, 0, F32)
+    second = jnp.where(z == 0, weights_l1, weights_r1)
+    third = jnp.where(z == 0, weights_l2, jnp.where(z == 3, weights_r2, weights_l1))
+    fourth = jnp.where(z == 1, weights_l2, weights_r2)
+    sheet = tuple(products(acts, weights, second, third))
+    weights_r3, weights_l3, other_a, got_own_1, got_inner, sum_inner, sheet, fourth, own_0, outer_0 = tie(
+        (weights_r3, weights_l3, other_a, got_own_1, got_inner, sum_inner, sheet, fourth, own_0, outer_0)
+    )
+
+    own_1 = sum_own_1 + got_own_1.astype(F32)
+    inner_0 = sum_inner + got_inner.astype(F32)
+    (last,) = products(acts, jnp.where(z == 0, weights_l3, jnp.where(z == 3, weights_r3, fourth)))
+    s_0, s_1, s_2 = sheet
+    of_z = [
+        jnp.where(z == 0, s_0, jnp.where(z == 1, s_1, last)),
+        jnp.where(z == 1, s_0, jnp.where(z == 3, s_2, s_1)),
+        jnp.where(z == 2, s_0, jnp.where(z == 3, s_1, s_2)),
+        jnp.where(z == 3, s_0, jnp.where(z == 2, s_2, last)),
+    ]
+    theirs = jnp.stack([jnp.where(x == 0, of_z[2], of_z[0]), jnp.where(x == 0, of_z[3], of_z[1])]).astype(BF16)
+    dense = jnp.stack([jnp.where(x == 0, of_z[0], of_z[2]), jnp.where(x == 0, of_z[1], of_z[3])])
+    theirs = lax.ppermute(theirs, "tp", SWAP)
+    own_b = hop(jnp.where(z == far, own_1, own_0 + own_a.astype(F32)), [(3, 2), (2, 1)], [(0, 1), (1, 2)])
+    other_b = jnp.where(z == 3 - far, inner_0, outer_0 + other_a.astype(F32))
+    other_b = hop(other_b, [(0, 1), (1, 2)], [(3, 2), (2, 1)])
+    own_b, other_b, theirs, dense, own_1, inner_0 = tie((own_b, other_b, theirs, dense, own_1, inner_0))
+    dense = dense + theirs.astype(F32)
+
+    own_c = jnp.where(z == far, inner_0, own_b.astype(F32) + jnp.where(distance == 1, own_1, own_0))
+    own_c = hop(own_c, left, right)
+    other_c = jnp.where(z == 3 - far, own_1, other_b.astype(F32) + jnp.where(distance == 2, inner_0, outer_0))
+    other_c = hop(other_c, right, left)
+    routed = jnp.where(distance == 3, own_0, jnp.where(distance == 2, own_1, jnp.where(distance == 1, inner_0, outer_0)))
+    routed = routed + own_c.astype(F32) + other_c.astype(F32)
 
     dense = dense.reshape(2, 2, 2, rows, columns)
     near = dense[:, 0, 0]

time: 193 us -> 170 us (0.88)
  Pallas kernels: 53.3 us -> 37.8 us
  starting transfers between devices: 50.2 us -> 43.8 us
  local copies, waits for them, and re-layouts: 18.3 us -> 12.1 us
  other arithmetic: 10.1 us -> 13.5 us
    pallas_call x10, Pallas kernels: 39.4 us -> 24 us  [the longest x8 13.4 us: combine(): pl.pallas_call(combine_kernel, out_shape=jax.ShapeDtypeStruct((tokens, fe...]
    all_to_all x1, waiting for transfers between devices: 18.7 us -> 9.77 us  [four_by_two(): gates = lax.all_to_all(gates, ('z', 'y'), 0, 0, tiled=True)]
    ppermute x21 -> x22, waiting for transfers between devices: 37.8 us -> 44.7 us  [the longest x5 11.8 us: over_y(): return lax.ppermute(value, 'y', SWAP)]
    ppermute x21 -> x22, starting transfers between devices: 35 us -> 28.1 us  [the longest x6 13.8 us: hop(): return lax.ppermute(value.astype(BF16), ('z', 'tp'), pairs)]
    unnamed x68 -> x58, local copies, waits for them, and re-layouts: 14 us -> 8.01 us
    ppermute x1, waiting for transfers between devices: 2.56 us -> 7.13 us  [four_by_two(): hidden_1 = lax.ppermute(hidden_1, 'tp', SWAP)]
    ppermute x1, starting transfers between devices: 4.52 us -> 6.6 us  [four_by_two(): weights_r1 = lax.ppermute(weights, 'z', right)]
    convert_element_type x3 -> x5, other arithmetic: 5.48 us -> 6.32 us  [hop(): return lax.ppermute(value.astype(BF16), ('z', 'tp'), pairs)]
  transfers between devices with their start and end apart: 28 -> 29, of which waited for: 10 -> 9; matrix products, arithmetic and copies ran while one was open for 7% -> 5% of each run, Pallas kernels for 22% -> 20%
where the time goes in v3:
time: 170 us; the launch traced here: 169 us
  waiting for transfers between devices  61.6 us (36%)
  starting transfers between devices  43.8 us (26%)
  Pallas kernels  37.8 us (22%)
  other arithmetic  13.5 us (8%)
  local copies, waits for them, and re-layouts  12.1 us (7%)
    ppermute x6, starting transfers between devices, hop(): return lax.ppermute(value.astype(BF16), ('z', 'tp'), pairs)  13.8 us
    pallas_call x3, Pallas kernels, expert_tables(): pl.pallas_call(tables_kernel, out_shape=(shape, shape), grid_spec=pltpu.P...  13.8 us
    pallas_call x8, Pallas kernels, combine(): pl.pallas_call(combine_kernel, out_shape=jax.ShapeDtypeStruct((tokens, fe...  13.4 us
    ppermute x5, waiting for transfers between devices, over_y(): return lax.ppermute(value, 'y', SWAP)  11.8 us
    ppermute x1, waiting for transfers between devices, four_by_two(): theirs = lax.ppermute(theirs, 'tp', SWAP)  10.9 us
    pallas_call x2, Pallas kernels, products(): pl.pallas_call(products_kernel, out_shape=[jax.ShapeDtypeStruct(shape, F3...  10.6 us
    all_to_all x1, waiting for transfers between devices, four_by_two(): gates = lax.all_to_all(gates, ('z', 'y'), 0, 0, tiled=True)  9.77 us
    ppermute x6, waiting for transfers between devices, hop(): return lax.ppermute(value.astype(BF16), ('z', 'tp'), pairs)  9.55 us
  transfers between devices with their start and end apart: 29, of which 9 were waited for; matrix products, arithmetic and copies ran while one was open for 5% of the time, Pallas kernels for 20%

profile of v3, /device:TPU:0, one launch (start us, length us, event | category | flops | bytes accessed | tf_op | source)
XLA Modules:
  0.0 169.4 jit_solution(6274526311009386295)
XLA Ops:
  0.0 0.8 select_reduce_fusion
  0.8 0.6 reshape.18
  1.4 3.1 %dynamic-slice_bitcast_fusion = (bf16[480,1024]{1,0:T(8,128)(2,1)}, bf16[480,1024]{1,0:T(8,128)(2,1)}) fusion(bf16[2,480,1024]{2,1,0:T(8,128)(2,1)} %bitcast.56, s32[]{:T(128)S(6)} %select_n.197, s32[]{:T(128)S(6)} %select_n.195), kind=kLoop, calls=%fused_computation.17 | loop fusion | bytes 3932168 | tf_op jit(solution)/shard_map/jit(dynamic_index_in_dim)/squeeze | solution.py:16
  4.5 1.3 collective-permute-start.3
  5.8 6.6 %collective-permute-start.2 = (bf16[192,3072]{1,0:T(8,128)(2,1)}, bf16[192,3072]{1,0:T(8,128)(2,1)}, u32[]{:S(2)}, u32[]{:S(2)}) collective-permute-start(bf16[192,3072]{1,0:T(8,128)(2,1)} %bitcast.59), channel_id=1, source_target_pairs={{0,8},{8,16},{16,24},{1,9},{9,17},{17,25},{2,10},{10,18},{18,26},{... | collective-permute-start | bytes 3538952 | tf_op jit(solution)/shard_map/ppermute | solution.py:209
  12.4 2.0 %collective-permute-start.1 = (bf16[160,3072]{1,0:T(8,128)(2,1)}, bf16[160,3072]{1,0:T(8,128)(2,1)}, u32[]{:S(2)}, u32[]{:S(2)}) collective-permute-start(bf16[160,3072]{1,0:T(8,128)(2,1)} %acts_a.3), channel_id=1, source_target_pairs={{0,4},{4,0},{1,5},{5,1},{2,6},{6,2},{3,7},{7,3},{8,12},{12,8},{9,1... | collective-permute-start | bytes 2949128 | tf_op jit(solution)/shard_map/ppermute | solution.py:197
  14.4 1.5 collective-permute-start
  15.8 4.0 %all-to-all-start = ((f32[8,2,160]{2,1,0:T(2,128)}), f32[8,2,160]{2,1,0:T(2,128)S(1)}, u32[]{:S(2)}, u32[]{:S(2)}) async-start(f32[8,2,160]{2,1,0:T(2,128)} %reshape.18), calls=%async_computation | async-start | bytes 32768 | tf_op jit(solution)/shard_map/all_to_all | solution.py:214
  19.9 1.5 copy-done.7
  21.5 5.5 %shard_map.73 = (bf16[4,120,1536]{2,1,0:T(8,128)(2,1)S(1)}, bf16[4,120,1536]{2,1,0:T(8,128)(2,1)S(1)}) custom-call(s32[3]{0:T(128)S(1)} %pad_add_fusion.here, bf16[4,2,120,1024]{3,2,1,0:T(8,128)(2,1)S(1)} %bitcast.57, bf16[1024,1536]{1,0:T(8,128)(2,1)S(1)} %bitcast.53), custom_call_target="tpu_custom_call" | custom-call | tf_op jit(solution)/shard_map/pallas_call | solution.py:119
  27.0 1.1 copy-done.3
  28.1 1.1 copy-done.12
  29.2 9.8 %all-to-all-done.gates = f32[8,2,160]{2,1,0:T(2,128)S(1)} async-done(((f32[8,2,160]{2,1,0:T(2,128)}), f32[8,2,160]{2,1,0:T(2,128)S(1)}, u32[]{:S(2)}, u32[]{:S(2)}) %all-to-all-start) | async-done | bytes 10272 | tf_op jit(solution)/shard_map/all_to_all | solution.py:214
  39.4 1.9 %copy-done.1 = bf16[1,1024,1536]{2,1,0:T(8,128)(2,1)S(1)} copy-done((bf16[1,1024,1536]{2,1,0:T(8,128)(2,1)S(1)}, bf16[1,1024,1536]{2,1,0:T(8,128)(2,1)}, u32[]{:S(2)}) %copy-start.1) | copy-done | bytes 3145752
  41.3 4.4 %shard_map.75 = (bf16[2,120,1536]{2,1,0:T(8,128)(2,1)S(1)}, bf16[2,120,1536]{2,1,0:T(8,128)(2,1)S(1)}) custom-call(s32[3]{0:T(128)S(1)} %pad_add_fusion.here, bf16[2,2,120,1024]{3,2,1,0:T(8,128)(2,1)} %bitcast.12.hidden, bf16[1024,1536]{1,0:T(8,128)(2,1)S(1)} %bitcast.54), custom_call_target="tpu_custom_call" | custom-call | tf_op jit(solution)/shard_map/pallas_call | solution.py:119
  45.7 0.5 collective-permute-start.7
  46.3 1.3 shard_map.74
  47.6 0.6 collective-permute-start.6
  48.2 0.7 collective-permute-start.10
  48.9 1.3 collective-permute-start.11
  50.2 1.6 collective-permute-start.12
  51.8 1.3 shard_map.76
  53.1 1.3 shard_map.77
  54.5 6.4 %collective-permute-done.6 = bf16[160,1536]{1,0:T(8,128)(2,1)S(1)} collective-permute-done((bf16[160,1536]{1,0:T(8,128)(2,1)S(1)}, bf16[160,1536]{1,0:T(8,128)(2,1)S(1)}, u32[]{:S(2)}, u32[]{:S(2)}) %collective-permute-start.6) | collective-permute-done | bytes 491552 | tf_op jit(solution)/shard_map/ppermute | solution.py:197
  60.8 0.5 collective-permute-start.8
  61.4 1.1 fusion.7
  62.4 0.7 collective-permute-start.9
  63.1 1.3 shard_map.79
  64.5 2.1 %shard_map.78 = bf16[160,1536]{1,0:T(8,128)(2,1)} custom-call(s32[3]{0:T(128)S(1)} %pad_add_fusion.here, f32[8,2,160]{2,1,0:T(2,128)S(1)} %all-to-all-done.gates, f32[8,160,2]{2,1,0:T(8,128)S(1)} %bitcast.49, bf16[4,120,1536]{2,1,0:T(8,128)(2,1)S(1)} %copy-done.4, bf16[4,120,1536]{2,1,0:T(8,128)(2,1)S(1)} %collective-permute-done.5.sibling), custom_call_target="tpu_custom_call" | custom-call | tf_op jit(solution)/shard_map/pallas_call | solution.py:83
  66.6 7.1 %collective-permute-done.12 = bf16[480,1024]{1,0:T(8,128)(2,1)S(1)} collective-permute-done((bf16[480,1024]{1,0:T(8,128)(2,1)S(1)}, bf16[480,1024]{1,0:T(8,128)(2,1)S(1)}, u32[]{:S(2)}, u32[]{:S(2)}) %collective-permute-start.12) | collective-permute-done | bytes 983072 | tf_op jit(solution)/shard_map/ppermute | solution.py:225
  73.7 7.6 %collective-permute-done.11 = bf16[192,3072]{1,0:T(8,128)(2,1)S(1)} collective-permute-done((bf16[192,3072]{1,0:T(8,128)(2,1)}, bf16[192,3072]{1,0:T(8,128)(2,1)S(1)}, u32[]{:S(2)}, u32[]{:S(2)}) %collective-permute-start.11) | collective-permute-done | bytes 1179680 | tf_op jit(solution)/shard_map/ppermute | solution.py:224
  81.4 3.9 %shard_map.80 = (bf16[2,120,1536]{2,1,0:T(8,128)(2,1)}, bf16[2,120,1536]{2,1,0:T(8,128)(2,1)S(1)}) custom-call(s32[3]{0:T(128)S(1)} %pad_add_fusion.here, bf16[2,2,120,1024]{3,2,1,0:T(8,128)(2,1)S(1)} %bitcast.61, bf16[1024,1536]{1,0:T(8,128)(2,1)S(1)} %bitcast.55), custom_call_target="tpu_custom_call" | custom-call | tf_op jit(solution)/shard_map/pallas_call | solution.py:119
  85.3 0.9 copy-done.9
  86.2 1.4 collective-permute-start.13
  87.5 1.4 copy-done.6
  88.9 1.3 shard_map.82
  90.2 0.7 collective-permute-start.15
  91.0 1.3 collective-permute-start.16
  92.3 2.3 %shard_map.81 = bf16[160,1536]{1,0:T(8,128)(2,1)S(1)} custom-call(s32[3]{0:T(128)S(1)} %pad_add_fusion.here, f32[8,2,160]{2,1,0:T(2,128)S(1)} %all-to-all-done.gates, f32[8,160,2]{2,1,0:T(8,128)S(1)} %bitcast.51, bf16[2,120,1536]{2,1,0:T(8,128)(2,1)S(1)} %copy-done.10, bf16[2,120,1536]{2,1,0:T(8,128)(2,1)} %collective-permute-done.14.sibling), custom_call_target="tpu_custom_call" | custom-call | tf_op jit(solution)/shard_map/pallas_call | solution.py:83
  94.7 5.5 %collective-permute-done.13 = bf16[160,1536]{1,0:T(8,128)(2,1)} collective-permute-done((bf16[160,1536]{1,0:T(8,128)(2,1)}, bf16[160,1536]{1,0:T(8,128)(2,1)}, u32[]{:S(2)}, u32[]{:S(2)}) %collective-permute-start.13) | collective-permute-done | bytes 491552 | tf_op jit(solution)/shard_map/ppermute | solution.py:197
  100.3 3.7 %collective-permute-start.17 = (bf16[160,1536]{1,0:T(8,128)(2,1)S(1)}, bf16[160,1536]{1,0:T(8,128)(2,1)S(1)}, u32[]{:S(2)}, u32[]{:S(2)}) collective-permute-start(bf16[160,1536]{1,0:T(8,128)(2,1)S(1)} %get-tuple-element.127), channel_id=1, source_target_pairs={{0,8},{25,17},{2,10},{27,19},{4,12},{29,21},{6,14},{31,23}} | collective-permute-start | bytes 1474568 | tf_op jit(solution)/shard_map/ppermute | solution.py:194
  104.0 1.4 collective-permute-start.18
  105.5 1.5 broadcast_select_fusion
  107.0 2.4 %shard_map.83 = f32[160,1536]{1,0:T(8,128)S(1)} custom-call(s32[3]{0:T(128)S(1)} %pad_add_fusion.here, f32[8,2,160]{2,1,0:T(2,128)S(1)} %all-to-all-done.gates, f32[8,160,2]{2,1,0:T(8,128)S(1)} %bitcast.52, bf16[2,120,1536]{2,1,0:T(8,128)(2,1)S(1)} %copy-done.10, bf16[2,120,1536]{2,1,0:T(8,128)(2,1)} %collective-permute-done.14.sibling), custom_call_target="tpu_custom_call" | custom-call | tf_op jit(solution)/shard_map/pallas_call | solution.py:83
  109.5 6.7 %shard_map.84 = (f32[4,160,192]{2,1,0:T(8,128)S(1)}, f32[4,160,192]{2,1,0:T(8,128)S(1)}, f32[4,160,192]{2,1,0:T(8,128)S(1)}) custom-call(bf16[160,3072]{1,0:T(8,128)(2,1)S(1)} %copy-done.8, bf16[160,3072]{1,0:T(8,128)(2,1)} %collective-permute-done.1.acts_b, bf16[160,3072]{1,0:T(8,128)(2,1)} %collective-permute-done.4.acts_c, ...), custom_call_target="tpu_custom_call" | custom-call | tf_op jit(solution)/shard_map/pallas_call | solution.py:157
  116.2 4.8 %collective-permute-done.16 = bf16[192,3072]{1,0:T(8,128)(2,1)S(1)} collective-permute-done((bf16[192,3072]{1,0:T(8,128)(2,1)S(1)}, bf16[192,3072]{1,0:T(8,128)(2,1)S(1)}, u32[]{:S(2)}, u32[]{:S(2)}) %collective-permute-start.16) | collective-permute-done | bytes 1179680 | tf_op jit(solution)/shard_map/ppermute | solution.py:242
  121.0 2.1 %select_convert_fusion.3 = (bf16[160,1536]{1,0:T(8,128)(2,1)}, f32[160,1536]{1,0:T(8,128)S(1)}) fusion(f32[160,1536]{1,0:T(8,128)S(1)} %copy-done.13, bf16[160,1536]{1,0:T(8,128)(2,1)S(1)} %copy-done.24, pred[]{:T(512)S(6)} %eq.33, f32[160,1536]{1,0:T(8,128)S(1)} %shard_map.82, bf16[160,1536]{1,0:T(8,128)(2,1)} %collective-permute-done.13), kind=kLoop, calls=%fused_computation.13 | loop fusion | flops 1228800 | bytes 4423681 | tf_op jit(solution)/shard_map/convert_element_type | solution.py:194
  123.1 1.4 collective-permute-start.20
  124.7 3.9 %shard_map.85 = f32[4,160,192]{2,1,0:T(8,128)S(1)} custom-call(bf16[160,3072]{1,0:T(8,128)(2,1)S(1)} %copy-done.8, bf16[160,3072]{1,0:T(8,128)(2,1)} %collective-permute-done.1.acts_b, bf16[160,3072]{1,0:T(8,128)(2,1)} %collective-permute-done.4.acts_c, bf16[160,3072]{1,0:T(8,128)(2,1)S(1)} %collective-permute-done.19.acts_d, ...), custom_call_target="tpu_custom_call" | custom-call | tf_op jit(solution)/shard_map/pallas_call | solution.py:157
  128.6 0.4 select_bitcast_fusion.1
  129.1 1.0 pad_maximum_fusion.1
  130.0 2.3 %collective-permute-start.22 = (bf16[2,4,160,192]{3,2,1,0:T(8,128)(2,1)}, bf16[2,4,160,192]{3,2,1,0:T(8,128)(2,1)}, u32[]{:S(2)}, u32[]{:S(2)}) collective-permute-start(bf16[2,4,160,192]{3,2,1,0:T(8,128)(2,1)} %pad_maximum_fusion.1), channel_id=1, source_target_pairs={{0,1},{1,0},{2,3},{3,2},{4,5},{5,4},{6,7},{7,6},{8,9},{9,8},{10,11... | collective-permute-start | bytes 1474568 | tf_op jit(solution)/shard_map/ppermute | solution.py:274
  132.3 1.3 select_convert_fusion.2
  133.7 2.1 %collective-permute-start.21 = (bf16[160,1536]{1,0:T(8,128)(2,1)}, bf16[160,1536]{1,0:T(8,128)(2,1)}, u32[]{:S(2)}, u32[]{:S(2)}) collective-permute-start(bf16[160,1536]{1,0:T(8,128)(2,1)} %get-tuple-element.123), channel_id=1, source_target_pairs={{0,8},{8,16},{25,17},{17,9},{2,10},{10,18},{27,19},{19,11},{4,12},... | collective-permute-start | bytes 1474568 | tf_op jit(solution)/shard_map/ppermute | solution.py:194
  135.9 10.9 %collective-permute-done.22 = bf16[2,4,160,192]{3,2,1,0:T(8,128)(2,1)} collective-permute-done((bf16[2,4,160,192]{3,2,1,0:T(8,128)(2,1)}, bf16[2,4,160,192]{3,2,1,0:T(8,128)(2,1)}, u32[]{:S(2)}, u32[]{:S(2)}) %collective-permute-start.22) | collective-permute-done | bytes 491552 | tf_op jit(solution)/shard_map/ppermute | solution.py:274
  146.8 1.3 convert_add_fusion
  148.3 0.7 collective-permute-start.25
  149.0 1.4 collective-permute-start.24
  150.4 1.7 select_convert_fusion.1
  152.1 1.3 collective-permute-start.26
  153.4 4.6 %collective-permute-start.27 = (bf16[160,1536]{1,0:T(8,128)(2,1)S(1)}, bf16[160,1536]{1,0:T(8,128)(2,1)S(1)}, u32[]{:S(2)}, u32[]{:S(2)}) collective-permute-start(bf16[160,1536]{1,0:T(8,128)(2,1)S(1)} %get-tuple-element.137), channel_id=1, source_target_pairs={{0,8},{8,16},{16,24},{9,1},{17,9},{25,17},{2,10},{10,18},{18,26},{... | collective-permute-start | bytes 1474568 | tf_op jit(solution)/shard_map/ppermute | solution.py:194
  158.5 8.4 %collective-permute-done.26 = bf16[160,1536]{1,0:T(8,128)(2,1)S(1)} collective-permute-done((bf16[160,1536]{1,0:T(8,128)(2,1)S(1)}, bf16[160,1536]{1,0:T(8,128)(2,1)S(1)}, u32[]{:S(2)}, u32[]{:S(2)}) %collective-permute-start.26) | collective-permute-done | bytes 491552 | tf_op jit(solution)/shard_map/ppermute | solution.py:194
  166.9 1.2 collective-permute-done.27
  168.0 1.4 fusion.1
  (90 shorter events, 1.6 us)
Async XLA Ops:
  1.4 18.5 %copy-start = (bf16[1,1024,1536]{2,1,0:T(8,128)(2,1)S(1)}, bf16[1,1024,1536]{2,1,0:T(8,128)(2,1)}, u32[]{:S(2)}) copy-start(bf16[1,1024,1536]{2,1,0:T(8,128)(2,1)} %param.11) | copy-start | bytes 9437188
  4.5 34.8 %collective-permute-start.3 = (bf16[192,3072]{1,0:T(8,128)(2,1)}, bf16[192,3072]{1,0:T(8,128)(2,1)}, u32[]{:S(2)}, u32[]{:S(2)}) collective-permute-start(bf16[192,3072]{1,0:T(8,128)(2,1)} %bitcast.58), channel_id=1, source_target_pairs={{8,0},{16,8},{24,16},{9,1},{17,9},{25,17},{10,2},{18,10},{26,18},{... | collective-permute-start | bytes 3538952 | tf_op jit(solution)/shard_map/ppermute | solution.py:210
  5.8 33.5 %collective-permute-start.2 = (bf16[192,3072]{1,0:T(8,128)(2,1)}, bf16[192,3072]{1,0:T(8,128)(2,1)}, u32[]{:S(2)}, u32[]{:S(2)}) collective-permute-start(bf16[192,3072]{1,0:T(8,128)(2,1)} %bitcast.59), channel_id=1, source_target_pairs={{0,8},{8,16},{16,24},{1,9},{9,17},{17,25},{2,10},{10,18},{18,26},{... | collective-permute-start | bytes 3538952 | tf_op jit(solution)/shard_map/ppermute | solution.py:209
  12.4 26.9 %collective-permute-start.4 = (bf16[160,3072]{1,0:T(8,128)(2,1)}, bf16[160,3072]{1,0:T(8,128)(2,1)}, u32[]{:S(2)}, u32[]{:S(2)}) collective-permute-start(bf16[160,3072]{1,0:T(8,128)(2,1)} %acts_a.3), channel_id=1, source_target_pairs={{0,2},{2,0},{1,3},{3,1},{4,6},{6,4},{5,7},{7,5},{8,10},{10,8},{9,1... | collective-permute-start | bytes 2949128 | tf_op jit(solution)/shard_map/ppermute | solution.py:187
  12.4 26.9 %collective-permute-start.1 = (bf16[160,3072]{1,0:T(8,128)(2,1)}, bf16[160,3072]{1,0:T(8,128)(2,1)}, u32[]{:S(2)}, u32[]{:S(2)}) collective-permute-start(bf16[160,3072]{1,0:T(8,128)(2,1)} %acts_a.3), channel_id=1, source_target_pairs={{0,4},{4,0},{1,5},{5,1},{2,6},{6,2},{3,7},{7,3},{8,12},{12,8},{9,1... | collective-permute-start | bytes 2949128 | tf_op jit(solution)/shard_map/ppermute | solution.py:197
  14.4 24.9 %collective-permute-start = (bf16[480,1024]{1,0:T(8,128)(2,1)}, bf16[480,1024]{1,0:T(8,128)(2,1)}, u32[]{:S(2)}, u32[]{:S(2)}) collective-permute-start(bf16[480,1024]{1,0:T(8,128)(2,1)} %get-tuple-element.61), channel_id=1, source_target_pairs={{0,1},{1,0},{2,3},{3,2},{4,5},{5,4},{6,7},{7,6},{8,9},{9,8},{10,11... | collective-permute-start | bytes 2949128 | tf_op jit(solution)/shard_map/ppermute | solution.py:211
  15.8 23.1 %all-to-all-start = ((f32[8,2,160]{2,1,0:T(2,128)}), f32[8,2,160]{2,1,0:T(2,128)S(1)}, u32[]{:S(2)}, u32[]{:S(2)}) async-start(f32[8,2,160]{2,1,0:T(2,128)} %reshape.18), calls=%async_computation | async-start | bytes 32768 | tf_op jit(solution)/shard_map/all_to_all | solution.py:214
  19.9 1.5 copy-start.7
  27.0 1.2 copy-start.3
  28.1 1.1 copy-start.12
  39.3 7.0 %collective-permute-start.5 = (bf16[4,120,1536]{2,1,0:T(8,128)(2,1)}, bf16[4,120,1536]{2,1,0:T(8,128)(2,1)S(1)}, u32[]{:S(2)}, u32[]{:S(2)}) collective-permute-start(bf16[4,120,1536]{2,1,0:T(8,128)(2,1)} %copy-done.12), channel_id=1, source_target_pairs={{0,2},{2,0},{1,3},{3,1},{4,6},{6,4},{5,7},{7,5},{8,10},{10,8},{9,1... | collective-permute-start | bytes 4423688 | tf_op jit(solution)/shard_map/ppermute | solution.py:187
  39.4 1.9 %copy-start.1 = (bf16[1,1024,1536]{2,1,0:T(8,128)(2,1)S(1)}, bf16[1,1024,1536]{2,1,0:T(8,128)(2,1)}, u32[]{:S(2)}) copy-start(bf16[1,1024,1536]{2,1,0:T(8,128)(2,1)} %param.11) | copy-start | bytes 9437188
  41.3 5.0 %copy-start.4 = (bf16[4,120,1536]{2,1,0:T(8,128)(2,1)S(1)}, bf16[4,120,1536]{2,1,0:T(8,128)(2,1)}, u32[]{:S(2)}) copy-start(bf16[4,120,1536]{2,1,0:T(8,128)(2,1)} %copy-done.3) | copy-start | bytes 4423684
  45.7 4.5 %copy-start.21 = (bf16[480,1024]{1,0:T(8,128)(2,1)S(1)}, bf16[480,1024]{1,0:T(8,128)(2,1)}, u32[]{:S(2)}) copy-start(bf16[480,1024]{1,0:T(8,128)(2,1)} %get-tuple-element.78) | copy-start | bytes 2949124
  45.7 6.1 %collective-permute-start.7 = (bf16[2,120,1536]{2,1,0:T(8,128)(2,1)S(1)}, bf16[2,120,1536]{2,1,0:T(8,128)(2,1)S(1)}, u32[]{:S(2)}, u32[]{:S(2)}) collective-permute-start(bf16[2,120,1536]{2,1,0:T(8,128)(2,1)S(1)} %get-tuple-element.72), channel_id=1, source_target_pairs={{0,2},{2,0},{1,3},{3,1},{4,6},{6,4},{5,7},{7,5},{8,10},{10,8},{9,1... | collective-permute-start | bytes 2211848 | tf_op jit(solution)/shard_map/ppermute | solution.py:187
  46.3 18.2 %copy-start.5 = (bf16[4,120,1536]{2,1,0:T(8,128)(2,1)}, bf16[4,120,1536]{2,1,0:T(8,128)(2,1)S(1)}, u32[]{:S(2)}) copy-start(bf16[4,120,1536]{2,1,0:T(8,128)(2,1)S(1)} %collective-permute-done.5.sibling) | copy-start | bytes 4423684
  47.6 13.2 %collective-permute-start.6 = (bf16[160,1536]{1,0:T(8,128)(2,1)S(1)}, bf16[160,1536]{1,0:T(8,128)(2,1)S(1)}, u32[]{:S(2)}, u32[]{:S(2)}) collective-permute-start(bf16[160,1536]{1,0:T(8,128)(2,1)S(1)} %shard_map.74), channel_id=1, source_target_pairs={{0,4},{4,0},{1,5},{5,1},{2,6},{6,2},{3,7},{7,3},{8,12},{12,8},{9,1... | collective-permute-start | bytes 1474568 | tf_op jit(solution)/shard_map/ppermute | solution.py:197
  48.2 25.5 %collective-permute-start.10 = (bf16[192,3072]{1,0:T(8,128)(2,1)}, bf16[192,3072]{1,0:T(8,128)(2,1)S(1)}, u32[]{:S(2)}, u32[]{:S(2)}) collective-permute-start(bf16[192,3072]{1,0:T(8,128)(2,1)} %collective-permute-done.2), channel_id=1, source_target_pairs={{8,16},{16,24},{9,17},{17,25},{10,18},{18,26},{11,19},{19,27},{12,... | collective-permute-start | bytes 3538952 | tf_op jit(solution)/shard_map/ppermute | solution.py:223
  48.9 32.4 %collective-permute-start.11 = (bf16[192,3072]{1,0:T(8,128)(2,1)}, bf16[192,3072]{1,0:T(8,128)(2,1)S(1)}, u32[]{:S(2)}, u32[]{:S(2)}) collective-permute-start(bf16[192,3072]{1,0:T(8,128)(2,1)} %collective-permute-done.3), channel_id=1, source_target_pairs={{8,0},{16,8},{9,1},{17,9},{10,2},{18,10},{11,3},{19,11},{12,4},{20... | collective-permute-start | bytes 3538952 | tf_op jit(solution)/shard_map/ppermute | solution.py:224
  50.2 23.5 %collective-permute-start.12 = (bf16[480,1024]{1,0:T(8,128)(2,1)S(1)}, bf16[480,1024]{1,0:T(8,128)(2,1)S(1)}, u32[]{:S(2)}, u32[]{:S(2)}) collective-permute-start(bf16[480,1024]{1,0:T(8,128)(2,1)S(1)} %copy-done.21), channel_id=1, source_target_pairs={{0,1},{1,0},{2,3},{3,2},{4,5},{5,4},{6,7},{7,6},{8,9},{9,8},{10,11... | collective-permute-start | bytes 2949128 | tf_op jit(solution)/shard_map/ppermute | solution.py:225
  60.8 20.5 %collective-permute-start.8 = (bf16[160,1536]{1,0:T(8,128)(2,1)S(1)}, bf16[160,1536]{1,0:T(8,128)(2,1)S(1)}, u32[]{:S(2)}, u32[]{:S(2)}) collective-permute-start(bf16[160,1536]{1,0:T(8,128)(2,1)S(1)} %shard_map.76), channel_id=1, source_target_pairs={{0,4},{4,0},{1,5},{5,1},{2,6},{6,2},{3,7},{7,3},{8,12},{12,8},{9,1... | collective-permute-start | bytes 1474568 | tf_op jit(solution)/shard_map/ppermute | solution.py:197
  62.4 18.9 %collective-permute-start.9 = (bf16[160,1536]{1,0:T(8,128)(2,1)S(1)}, bf16[160,1536]{1,0:T(8,128)(2,1)S(1)}, u32[]{:S(2)}, u32[]{:S(2)}) collective-permute-start(bf16[160,1536]{1,0:T(8,128)(2,1)S(1)} %get-tuple-element.129), channel_id=1, source_target_pairs={{24,16},{1,9},{26,18},{3,11},{28,20},{5,13},{30,22},{7,15}} | collective-permute-start | bytes 1474568 | tf_op jit(solution)/shard_map/ppermute | solution.py:194
  64.5 16.9 %copy-start.2 = (bf16[1,1024,1536]{2,1,0:T(8,128)(2,1)S(1)}, bf16[1,1024,1536]{2,1,0:T(8,128)(2,1)}, u32[]{:S(2)}) copy-start(bf16[1,1024,1536]{2,1,0:T(8,128)(2,1)} %param.11) | copy-start | bytes 9437188
  73.7 11.6 %copy-start.17 = (bf16[192,3072]{1,0:T(8,128)(2,1)}, bf16[192,3072]{1,0:T(8,128)(2,1)S(1)}, u32[]{:S(2)}) copy-start(bf16[192,3072]{1,0:T(8,128)(2,1)S(1)} %collective-permute-done.10) | copy-start | bytes 3538948
  81.3 3.9 %copy-start.19 = (bf16[192,3072]{1,0:T(8,128)(2,1)}, bf16[192,3072]{1,0:T(8,128)(2,1)S(1)}, u32[]{:S(2)}) copy-start(bf16[192,3072]{1,0:T(8,128)(2,1)S(1)} %collective-permute-done.11) | copy-start | bytes 3538948
  81.3 3.9 %copy-start.25 = (bf16[160,1536]{1,0:T(8,128)(2,1)}, bf16[160,1536]{1,0:T(8,128)(2,1)S(1)}, u32[]{:S(2)}) copy-start(bf16[160,1536]{1,0:T(8,128)(2,1)S(1)} %collective-permute-done.8) | copy-start | bytes 1474564
  81.4 3.9 %copy-start.23 = (bf16[160,1536]{1,0:T(8,128)(2,1)}, bf16[160,1536]{1,0:T(8,128)(2,1)S(1)}, u32[]{:S(2)}) copy-start(bf16[160,1536]{1,0:T(8,128)(2,1)S(1)} %collective-permute-done.9) | copy-start | bytes 1474564
  85.3 0.9 copy-start.9
  86.2 6.1 %collective-permute-start.14 = (bf16[2,120,1536]{2,1,0:T(8,128)(2,1)}, bf16[2,120,1536]{2,1,0:T(8,128)(2,1)}, u32[]{:S(2)}, u32[]{:S(2)}) collective-permute-start(bf16[2,120,1536]{2,1,0:T(8,128)(2,1)} %get-tuple-element.83), channel_id=1, source_target_pairs={{0,2},{2,0},{1,3},{3,1},{4,6},{6,4},{5,7},{7,5},{8,10},{10,8},{9,1... | collective-permute-start | bytes 2211848 | tf_op jit(solution)/shard_map/ppermute | solution.py:187
  86.2 13.9 %collective-permute-start.13 = (bf16[160,1536]{1,0:T(8,128)(2,1)}, bf16[160,1536]{1,0:T(8,128)(2,1)}, u32[]{:S(2)}, u32[]{:S(2)}) collective-permute-start(bf16[160,1536]{1,0:T(8,128)(2,1)} %shard_map.78), channel_id=1, source_target_pairs={{0,4},{4,0},{1,5},{5,1},{2,6},{6,2},{3,7},{7,3},{8,12},{12,8},{9,1... | collective-permute-start | bytes 1474568 | tf_op jit(solution)/shard_map/ppermute | solution.py:197
  87.5 1.4 copy-start.6
  88.9 1.3 copy-start.18
  88.9 2.1 %copy-start.20 = (bf16[192,3072]{1,0:T(8,128)(2,1)S(1)}, bf16[192,3072]{1,0:T(8,128)(2,1)}, u32[]{:S(2)}) copy-start(bf16[192,3072]{1,0:T(8,128)(2,1)} %copy-done.19) | copy-start | bytes 3538948
  88.9 3.4 %copy-start.10 = (bf16[2,120,1536]{2,1,0:T(8,128)(2,1)S(1)}, bf16[2,120,1536]{2,1,0:T(8,128)(2,1)}, u32[]{:S(2)}) copy-start(bf16[2,120,1536]{2,1,0:T(8,128)(2,1)} %copy-done.9) | copy-start | bytes 2211844
  90.2 25.9 %collective-permute-start.15 = (bf16[192,3072]{1,0:T(8,128)(2,1)S(1)}, bf16[192,3072]{1,0:T(8,128)(2,1)S(1)}, u32[]{:S(2)}, u32[]{:S(2)}) collective-permute-start(bf16[192,3072]{1,0:T(8,128)(2,1)S(1)} %copy-done.18), channel_id=1, source_target_pairs={{16,24},{17,25},{18,26},{19,27},{20,28},{21,29},{22,30},{23,31}} | collective-permute-start | bytes 3538952 | tf_op jit(solution)/shard_map/ppermute | solution.py:241
  91.0 30.0 %collective-permute-start.16 = (bf16[192,3072]{1,0:T(8,128)(2,1)S(1)}, bf16[192,3072]{1,0:T(8,128)(2,1)S(1)}, u32[]{:S(2)}, u32[]{:S(2)}) collective-permute-start(bf16[192,3072]{1,0:T(8,128)(2,1)S(1)} %copy-done.20), channel_id=1, source_target_pairs={{8,0},{9,1},{10,2},{11,3},{12,4},{13,5},{14,6},{15,7}} | collective-permute-start | bytes 3538952 | tf_op jit(solution)/shard_map/ppermute | solution.py:242
  92.3 7.8 %copy-start.26 = (bf16[160,1536]{1,0:T(8,128)(2,1)S(1)}, bf16[160,1536]{1,0:T(8,128)(2,1)}, u32[]{:S(2)}) copy-start(bf16[160,1536]{1,0:T(8,128)(2,1)} %copy-done.25) | copy-start | bytes 1474564
  100.1 9.3 %collective-permute-start.19 = (bf16[160,3072]{1,0:T(8,128)(2,1)}, bf16[160,3072]{1,0:T(8,128)(2,1)S(1)}, u32[]{:S(2)}, u32[]{:S(2)}) collective-permute-start(bf16[160,3072]{1,0:T(8,128)(2,1)} %collective-permute-done.1.acts_b), channel_id=1, source_target_pairs={{0,2},{2,0},{1,3},{3,1},{4,6},{6,4},{5,7},{7,5},{8,10},{10,8},{9,1... | collective-permute-start | bytes 2949128 | tf_op jit(solution)/shard_map/ppermute | solution.py:187
  100.3 32.1 %copy-start.14 = (f32[160,1536]{1,0:T(8,128)}, f32[160,1536]{1,0:T(8,128)S(1)}, u32[]{:S(2)}) copy-start(f32[160,1536]{1,0:T(8,128)S(1)} %get-tuple-element.103) | copy-start | bytes 2949124
  100.3 15.9 %collective-permute-start.17 = (bf16[160,1536]{1,0:T(8,128)(2,1)S(1)}, bf16[160,1536]{1,0:T(8,128)(2,1)S(1)}, u32[]{:S(2)}, u32[]{:S(2)}) collective-permute-start(bf16[160,1536]{1,0:T(8,128)(2,1)S(1)} %get-tuple-element.127), channel_id=1, source_target_pairs={{0,8},{25,17},{2,10},{27,19},{4,12},{29,21},{6,14},{31,23}} | collective-permute-start | bytes 1474568 | tf_op jit(solution)/shard_map/ppermute | solution.py:194
  104.0 17.0 %collective-permute-start.18 = (bf16[160,1536]{1,0:T(8,128)(2,1)S(1)}, bf16[160,1536]{1,0:T(8,128)(2,1)S(1)}, u32[]{:S(2)}, u32[]{:S(2)}) collective-permute-start(bf16[160,1536]{1,0:T(8,128)(2,1)S(1)} %shard_map.81), channel_id=1, source_target_pairs={{0,4},{4,0},{1,5},{5,1},{2,6},{6,2},{3,7},{7,3},{8,12},{12,8},{9,1... | collective-permute-start | bytes 1474568 | tf_op jit(solution)/shard_map/ppermute | solution.py:197
  107.0 2.4 %copy-start.8 = (bf16[160,3072]{1,0:T(8,128)(2,1)S(1)}, bf16[160,3072]{1,0:T(8,128)(2,1)}, u32[]{:S(2)}) copy-start(bf16[160,3072]{1,0:T(8,128)(2,1)} %acts_a.3) | copy-start | bytes 2949124
  107.0 2.4 %copy-start.11 = (bf16[3072,192]{0,1:T(8,128)(2,1)S(1)}, bf16[3072,192]{0,1:T(8,128)(2,1)}, u32[]{:S(2)}) copy-start(bf16[3072,192]{0,1:T(8,128)(2,1)} %param.13) | copy-start | bytes 3538948
  109.5 11.5 %copy-start.13 = (f32[160,1536]{1,0:T(8,128)S(1)}, f32[160,1536]{1,0:T(8,128)}, u32[]{:S(2)}) copy-start(f32[160,1536]{1,0:T(8,128)} %get-tuple-element.99) | copy-start | bytes 2949124
  109.5 11.5 %copy-start.24 = (bf16[160,1536]{1,0:T(8,128)(2,1)S(1)}, bf16[160,1536]{1,0:T(8,128)(2,1)}, u32[]{:S(2)}) copy-start(bf16[160,1536]{1,0:T(8,128)(2,1)} %copy-done.23) | copy-start | bytes 1474564
  123.1 12.8 %collective-permute-start.20 = (bf16[160,1536]{1,0:T(8,128)(2,1)}, bf16[160,1536]{1,0:T(8,128)(2,1)}, u32[]{:S(2)}, u32[]{:S(2)}) collective-permute-start(bf16[160,1536]{1,0:T(8,128)(2,1)} %get-tuple-element.125), channel_id=1, source_target_pairs={{24,16},{16,8},{1,9},{9,17},{26,18},{18,10},{3,11},{11,19},{28,20}... | collective-permute-start | bytes 1474568 | tf_op jit(solution)/shard_map/ppermute | solution.py:194
  130.0 5.7 %copy-start.27 = (f32[160,12]{0,1:T(8,128)S(1)}, f32[160,12]{0,1:T(8,128)}, u32[]{:S(2)}) copy-start(f32[160,12]{0,1:T(8,128)} %param.9) | copy-start | bytes 23044
  130.0 5.7 %copy-start.28 = (s32[160,12]{0,1:T(8,128)S(1)}, s32[160,12]{0,1:T(8,128)}, u32[]{:S(2)}) copy-start(s32[160,12]{0,1:T(8,128)} %param.8) | copy-start | bytes 23044
  130.0 16.8 %collective-permute-start.22 = (bf16[2,4,160,192]{3,2,1,0:T(8,128)(2,1)}, bf16[2,4,160,192]{3,2,1,0:T(8,128)(2,1)}, u32[]{:S(2)}, u32[]{:S(2)}) collective-permute-start(bf16[2,4,160,192]{3,2,1,0:T(8,128)(2,1)} %pad_maximum_fusion.1), channel_id=1, source_target_pairs={{0,1},{1,0},{2,3},{3,2},{4,5},{5,4},{6,7},{7,6},{8,9},{9,8},{10,11... | collective-permute-start | bytes 1474568 | tf_op jit(solution)/shard_map/ppermute | solution.py:274
  133.7 13.1 %collective-permute-start.21 = (bf16[160,1536]{1,0:T(8,128)(2,1)}, bf16[160,1536]{1,0:T(8,128)(2,1)}, u32[]{:S(2)}, u32[]{:S(2)}) collective-permute-start(bf16[160,1536]{1,0:T(8,128)(2,1)} %get-tuple-element.123), channel_id=1, source_target_pairs={{0,8},{8,16},{25,17},{17,9},{2,10},{10,18},{27,19},{19,11},{4,12},... | collective-permute-start | bytes 1474568 | tf_op jit(solution)/shard_map/ppermute | solution.py:194
  146.8 3.6 %copy-start.16 = (f32[160,1536]{1,0:T(8,128)S(1)}, f32[160,1536]{1,0:T(8,128)}, u32[]{:S(2)}) copy-start(f32[160,1536]{1,0:T(8,128)} %get-tuple-element.114) | copy-start | bytes 2949124
  148.1 2.3 %copy-start.15 = (f32[160,1536]{1,0:T(8,128)S(1)}, f32[160,1536]{1,0:T(8,128)}, u32[]{:S(2)}) copy-start(f32[160,1536]{1,0:T(8,128)} %copy-done.14) | copy-start | bytes 2949124
  148.2 9.9 %collective-permute-start.23 = (bf16[2,160,192]{2,1,0:T(8,128)(2,1)S(1)}, bf16[2,160,192]{2,1,0:T(8,128)(2,1)S(1)}, u32[]{:S(2)}, u32[]{:S(2)}) collective-permute-start(bf16[2,160,192]{2,1,0:T(8,128)(2,1)S(1)} %get-tuple-element.145), channel_id=1, source_target_pairs={{0,6},{2,4},{4,2},{6,0},{1,7},{3,5},{5,3},{7,1},{8,14},{10,12},{12... | collective-permute-start | bytes 368648 | tf_op jit(solution)/shard_map/ppermute | solution.py:292
  148.3 9.7 %collective-permute-start.25 = (bf16[2,160,192]{2,1,0:T(8,128)(2,1)S(1)}, bf16[2,160,192]{2,1,0:T(8,128)(2,1)S(1)}, u32[]{:S(2)}, u32[]{:S(2)}) collective-permute-start(bf16[2,160,192]{2,1,0:T(8,128)(2,1)S(1)} %get-tuple-element.146), channel_id=1, source_target_pairs={{0,2},{2,0},{1,3},{3,1},{4,6},{6,4},{5,7},{7,5},{8,10},{10,8},{9,1... | collective-permute-start | bytes 368648 | tf_op jit(solution)/shard_map/ppermute | solution.py:290
  149.0 9.0 %collective-permute-start.24 = (bf16[2,160,192]{2,1,0:T(8,128)(2,1)S(1)}, bf16[2,160,192]{2,1,0:T(8,128)(2,1)S(1)}, u32[]{:S(2)}, u32[]{:S(2)}) collective-permute-start(bf16[2,160,192]{2,1,0:T(8,128)(2,1)S(1)} %get-tuple-element.147), channel_id=1, source_target_pairs={{0,4},{4,0},{1,5},{5,1},{2,6},{6,2},{3,7},{7,3},{8,12},{12,8},{9,1... | collective-permute-start | bytes 368648 | tf_op jit(solution)/shard_map/ppermute | solution.py:291
  152.1 14.7 %collective-permute-start.26 = (bf16[160,1536]{1,0:T(8,128)(2,1)S(1)}, bf16[160,1536]{1,0:T(8,128)(2,1)S(1)}, u32[]{:S(2)}, u32[]{:S(2)}) collective-permute-start(bf16[160,1536]{1,0:T(8,128)(2,1)S(1)} %get-tuple-element.136), channel_id=1, source_target_pairs={{8,0},{16,8},{24,16},{1,9},{9,17},{17,25},{10,2},{18,10},{26,18},{... | collective-permute-start | bytes 1474568 | tf_op jit(solution)/shard_map/ppermute | solution.py:194
  153.4 14.6 %collective-permute-start.27 = (bf16[160,1536]{1,0:T(8,128)(2,1)S(1)}, bf16[160,1536]{1,0:T(8,128)(2,1)S(1)}, u32[]{:S(2)}, u32[]{:S(2)}) collective-permute-start(bf16[160,1536]{1,0:T(8,128)(2,1)S(1)} %get-tuple-element.137), channel_id=1, source_target_pairs={{0,8},{8,16},{16,24},{9,1},{17,9},{25,17},{2,10},{10,18},{18,26},{... | collective-permute-start | bytes 1474568 | tf_op jit(solution)/shard_map/ppermute | solution.py:194
  158.4 9.6 %copy-start.22 = (bf16[160,1536]{1,0:T(8,128)(2,1)S(1)}, bf16[160,1536]{1,0:T(8,128)(2,1)}, u32[]{:S(2)}) copy-start(bf16[160,1536]{1,0:T(8,128)(2,1)} %param.7) | copy-start | bytes 1474564

commit v4 on v3

--- a/solution.py
+++ b/solution.py
@@ -151,7 +151,7 @@
 def products(acts, *weights):
     rows, depth = acts[0].shape
     columns = weights[0].shape[0]
-    step = depth // 4
+    step = depth
     shape = (4, rows, columns)
     count = len(weights)
     return pl.pallas_call(
@@ -272,10 +272,12 @@
     theirs = jnp.stack([jnp.where(x == 0, of_z[2], of_z[0]), jnp.where(x == 0, of_z[3], of_z[1])]).astype(BF16)
     dense = jnp.stack([jnp.where(x == 0, of_z[0], of_z[2]), jnp.where(x == 0, of_z[1], of_z[3])])
     theirs = lax.ppermute(theirs, "tp", SWAP)
-    own_b = hop(jnp.where(z == far, own_1, own_0 + own_a.astype(F32)), [(3, 2), (2, 1)], [(0, 1), (1, 2)])
-    other_b = jnp.where(z == 3 - far, inner_0, outer_0 + other_a.astype(F32))
+    own_b = jnp.where(z == far, own_1, own_0 + own_a.astype(F32)).astype(BF16)
+    other_b = jnp.where(z == 3 - far, inner_0, outer_0 + other_a.astype(F32)).astype(BF16)
+    own_b, other_b = tie((own_b, other_b))
+    own_b = hop(own_b, [(3, 2), (2, 1)], [(0, 1), (1, 2)])
     other_b = hop(other_b, [(0, 1), (1, 2)], [(3, 2), (2, 1)])
-    own_b, other_b, theirs, dense, own_1, inner_0 = tie((own_b, other_b, theirs, dense, own_1, inner_0))
+    own_b, other_b, own_1, inner_0 = tie((own_b, other_b, own_1, inner_0))
     dense = dense + theirs.astype(F32)
 
     own_c = jnp.where(z == far, inner_0, own_b.astype(F32) + jnp.where(distance == 1, own_1, own_0))

time: 170 us -> 162 us (0.953)
  other arithmetic: 13.5 us -> 8.48 us
    convert_element_type x5 -> x3, other arithmetic: 6.32 us -> 1.76 us  [hop(): return lax.ppermute(value.astype(BF16), ('z', 'tp'), pairs)]
    unnamed x58 -> x52, local copies, waits for them, and re-layouts: 8.01 us -> 8.07 us
  transfers between devices with their start and end apart: 29 -> 29, of which waited for: 9 -> 9; matrix products, arithmetic and copies ran while one was open for 5% -> 4% of each run, Pallas kernels for 20% -> 18%
where the time goes in v4:
time: 162 us; the launch traced here: 161 us
  waiting for transfers between devices  61.2 us (38%)
  starting transfers between devices  42.5 us (26%)
  Pallas kernels  36.2 us (22%)
  local copies, waits for them, and re-layouts  12.2 us (8%)
  other arithmetic  8.48 us (5%)
    pallas_call x3, Pallas kernels, expert_tables(): pl.pallas_call(tables_kernel, out_shape=(shape, shape), grid_spec=pltpu.P...  13.8 us
    pallas_call x8, Pallas kernels, combine(): pl.pallas_call(combine_kernel, out_shape=jax.ShapeDtypeStruct((tokens, fe...  13.4 us
    ppermute x6, starting transfers between devices, hop(): return lax.ppermute(value.astype(BF16), ('z', 'tp'), pairs)  13.2 us
    ppermute x5, waiting for transfers between devices, over_y(): return lax.ppermute(value, 'y', SWAP)  11.8 us
    ppermute x1, waiting for transfers between devices, four_by_two(): theirs = lax.ppermute(theirs, 'tp', SWAP)  9.98 us
    all_to_all x1, waiting for transfers between devices, four_by_two(): gates = lax.all_to_all(gates, ('z', 'y'), 0, 0, tiled=True)  9.72 us
    ppermute x6, waiting for transfers between devices, hop(): return lax.ppermute(value.astype(BF16), ('z', 'tp'), pairs)  9.56 us
    pallas_call x2, Pallas kernels, products(): pl.pallas_call(products_kernel, out_shape=[jax.ShapeDtypeStruct(shape, F3...  9.02 us
  transfers between devices with their start and end apart: 29, of which 9 were waited for; matrix products, arithmetic and copies ran while one was open for 4% of the time, Pallas kernels for 18%

profile of v4, /device:TPU:0, one launch (start us, length us, event | category | flops | bytes accessed | tf_op | source)
XLA Modules:
  0.0 161.3 jit_solution(14426646795482179345)
XLA Ops:
  0.0 0.8 select_reduce_fusion
  0.8 0.6 reshape.18
  1.4 3.1 %dynamic-slice_bitcast_fusion = (bf16[480,1024]{1,0:T(8,128)(2,1)}, bf16[480,1024]{1,0:T(8,128)(2,1)}) fusion(bf16[2,480,1024]{2,1,0:T(8,128)(2,1)} %bitcast.56, s32[]{:T(128)S(6)} %select_n.197, s32[]{:T(128)S(6)} %select_n.195), kind=kLoop, calls=%fused_computation.16 | loop fusion | bytes 3932168 | tf_op jit(solution)/shard_map/jit(dynamic_index_in_dim)/squeeze | solution.py:16
  4.5 1.3 collective-permute-start.3
  5.8 6.6 %collective-permute-start.2 = (bf16[192,3072]{1,0:T(8,128)(2,1)}, bf16[192,3072]{1,0:T(8,128)(2,1)}, u32[]{:S(2)}, u32[]{:S(2)}) collective-permute-start(bf16[192,3072]{1,0:T(8,128)(2,1)} %bitcast.59), channel_id=1, source_target_pairs={{0,8},{8,16},{16,24},{1,9},{9,17},{17,25},{2,10},{10,18},{18,26},{... | collective-permute-start | bytes 3538952 | tf_op jit(solution)/shard_map/ppermute | solution.py:209
  12.4 2.0 %collective-permute-start.1 = (bf16[160,3072]{1,0:T(8,128)(2,1)}, bf16[160,3072]{1,0:T(8,128)(2,1)}, u32[]{:S(2)}, u32[]{:S(2)}) collective-permute-start(bf16[160,3072]{1,0:T(8,128)(2,1)} %acts_a.3), channel_id=1, source_target_pairs={{0,4},{4,0},{1,5},{5,1},{2,6},{6,2},{3,7},{7,3},{8,12},{12,8},{9,1... | collective-permute-start | bytes 2949128 | tf_op jit(solution)/shard_map/ppermute | solution.py:197
  14.3 1.5 collective-permute-start
  15.8 4.0 %all-to-all-start = ((f32[8,2,160]{2,1,0:T(2,128)}), f32[8,2,160]{2,1,0:T(2,128)S(1)}, u32[]{:S(2)}, u32[]{:S(2)}) async-start(f32[8,2,160]{2,1,0:T(2,128)} %reshape.18), calls=%async_computation | async-start | bytes 32768 | tf_op jit(solution)/shard_map/all_to_all | solution.py:214
  19.9 1.5 copy-done.7
  21.5 5.5 %shard_map.73 = (bf16[4,120,1536]{2,1,0:T(8,128)(2,1)S(1)}, bf16[4,120,1536]{2,1,0:T(8,128)(2,1)S(1)}) custom-call(s32[3]{0:T(128)S(1)} %pad_add_fusion.here, bf16[4,2,120,1024]{3,2,1,0:T(8,128)(2,1)S(1)} %bitcast.57, bf16[1024,1536]{1,0:T(8,128)(2,1)S(1)} %bitcast.53), custom_call_target="tpu_custom_call" | custom-call | tf_op jit(solution)/shard_map/pallas_call | solution.py:119
  27.0 1.2 copy-done.3
  28.2 1.1 copy-done.12
  29.3 9.7 %all-to-all-done.gates = f32[8,2,160]{2,1,0:T(2,128)S(1)} async-done(((f32[8,2,160]{2,1,0:T(2,128)}), f32[8,2,160]{2,1,0:T(2,128)S(1)}, u32[]{:S(2)}, u32[]{:S(2)}) %all-to-all-start) | async-done | bytes 10272 | tf_op jit(solution)/shard_map/all_to_all | solution.py:214
  39.0 0.3 copy.32
  39.4 1.9 %copy-done.1 = bf16[1,1024,1536]{2,1,0:T(8,128)(2,1)S(1)} copy-done((bf16[1,1024,1536]{2,1,0:T(8,128)(2,1)S(1)}, bf16[1,1024,1536]{2,1,0:T(8,128)(2,1)}, u32[]{:S(2)}) %copy-start.1) | copy-done | bytes 3145752
  41.3 4.4 %shard_map.75 = (bf16[2,120,1536]{2,1,0:T(8,128)(2,1)S(1)}, bf16[2,120,1536]{2,1,0:T(8,128)(2,1)S(1)}) custom-call(s32[3]{0:T(128)S(1)} %pad_add_fusion.here, bf16[2,2,120,1024]{3,2,1,0:T(8,128)(2,1)} %bitcast.12.hidden, bf16[1024,1536]{1,0:T(8,128)(2,1)S(1)} %bitcast.54), custom_call_target="tpu_custom_call" | custom-call | tf_op jit(solution)/shard_map/pallas_call | solution.py:119
  45.7 0.6 collective-permute-start.7
  46.3 1.3 shard_map.74
  47.6 0.6 collective-permute-start.6
  48.2 0.7 collective-permute-start.10
  48.9 1.3 collective-permute-start.11
  50.3 1.6 collective-permute-start.12
  51.8 1.3 shard_map.76
  53.1 1.3 shard_map.77
  54.5 6.4 %collective-permute-done.6 = bf16[160,1536]{1,0:T(8,128)(2,1)S(1)} collective-permute-done((bf16[160,1536]{1,0:T(8,128)(2,1)S(1)}, bf16[160,1536]{1,0:T(8,128)(2,1)S(1)}, u32[]{:S(2)}, u32[]{:S(2)}) %collective-permute-start.6) | collective-permute-done | bytes 491552 | tf_op jit(solution)/shard_map/ppermute | solution.py:197
  60.9 0.5 collective-permute-start.8
  61.4 1.1 fusion.7
  62.5 0.7 collective-permute-start.9
  63.2 1.3 shard_map.79
  64.5 2.1 %shard_map.78 = bf16[160,1536]{1,0:T(8,128)(2,1)} custom-call(s32[3]{0:T(128)S(1)} %pad_add_fusion.here, f32[8,2,160]{2,1,0:T(2,128)S(1)} %all-to-all-done.gates, f32[8,160,2]{2,1,0:T(8,128)S(1)} %bitcast.49, bf16[4,120,1536]{2,1,0:T(8,128)(2,1)S(1)} %copy-done.4, bf16[4,120,1536]{2,1,0:T(8,128)(2,1)S(1)} %collective-permute-done.5.sibling), custom_call_target="tpu_custom_call" | custom-call | tf_op jit(solution)/shard_map/pallas_call | solution.py:83
  66.6 7.1 %collective-permute-done.12 = bf16[480,1024]{1,0:T(8,128)(2,1)S(1)} collective-permute-done((bf16[480,1024]{1,0:T(8,128)(2,1)S(1)}, bf16[480,1024]{1,0:T(8,128)(2,1)S(1)}, u32[]{:S(2)}, u32[]{:S(2)}) %collective-permute-start.12) | collective-permute-done | bytes 983072 | tf_op jit(solution)/shard_map/ppermute | solution.py:225
  73.7 7.6 %collective-permute-done.11 = bf16[192,3072]{1,0:T(8,128)(2,1)S(1)} collective-permute-done((bf16[192,3072]{1,0:T(8,128)(2,1)}, bf16[192,3072]{1,0:T(8,128)(2,1)S(1)}, u32[]{:S(2)}, u32[]{:S(2)}) %collective-permute-start.11) | collective-permute-done | bytes 1179680 | tf_op jit(solution)/shard_map/ppermute | solution.py:224
  81.4 3.9 %shard_map.80 = (bf16[2,120,1536]{2,1,0:T(8,128)(2,1)}, bf16[2,120,1536]{2,1,0:T(8,128)(2,1)S(1)}) custom-call(s32[3]{0:T(128)S(1)} %pad_add_fusion.here, bf16[2,2,120,1024]{3,2,1,0:T(8,128)(2,1)S(1)} %bitcast.61, bf16[1024,1536]{1,0:T(8,128)(2,1)S(1)} %bitcast.55), custom_call_target="tpu_custom_call" | custom-call | tf_op jit(solution)/shard_map/pallas_call | solution.py:119
  85.4 0.9 copy-done.9
  86.3 1.4 collective-permute-start.16
  87.7 1.4 copy-done.6
  89.0 1.3 shard_map.82
  90.4 0.7 collective-permute-start.13
  91.1 1.3 collective-permute-start.14
  92.5 2.3 %shard_map.81 = bf16[160,1536]{1,0:T(8,128)(2,1)S(1)} custom-call(s32[3]{0:T(128)S(1)} %pad_add_fusion.here, f32[8,2,160]{2,1,0:T(2,128)S(1)} %all-to-all-done.gates, f32[8,160,2]{2,1,0:T(8,128)S(1)} %bitcast.51, bf16[2,120,1536]{2,1,0:T(8,128)(2,1)S(1)} %copy-done.10, bf16[2,120,1536]{2,1,0:T(8,128)(2,1)} %collective-permute-done.17.sibling), custom_call_target="tpu_custom_call" | custom-call | tf_op jit(solution)/shard_map/pallas_call | solution.py:83
  94.8 5.4 %collective-permute-done.16 = bf16[160,1536]{1,0:T(8,128)(2,1)} collective-permute-done((bf16[160,1536]{1,0:T(8,128)(2,1)}, bf16[160,1536]{1,0:T(8,128)(2,1)}, u32[]{:S(2)}, u32[]{:S(2)}) %collective-permute-start.16) | collective-permute-done | bytes 491552 | tf_op jit(solution)/shard_map/ppermute | solution.py:197
  100.4 3.9 %collective-permute-start.15 = (bf16[160,1536]{1,0:T(8,128)(2,1)S(1)}, bf16[160,1536]{1,0:T(8,128)(2,1)S(1)}, u32[]{:S(2)}, u32[]{:S(2)}) collective-permute-start(bf16[160,1536]{1,0:T(8,128)(2,1)S(1)} %get-tuple-element.127), channel_id=1, source_target_pairs={{0,8},{25,17},{2,10},{27,19},{4,12},{29,21},{6,14},{31,23}} | collective-permute-start | bytes 1474568 | tf_op jit(solution)/shard_map/ppermute | solution.py:194
  104.3 1.5 collective-permute-start.18
  105.8 1.5 broadcast_select_fusion
  107.3 2.4 %shard_map.83 = f32[160,1536]{1,0:T(8,128)S(1)} custom-call(s32[3]{0:T(128)S(1)} %pad_add_fusion.here, f32[8,2,160]{2,1,0:T(2,128)S(1)} %all-to-all-done.gates, f32[8,160,2]{2,1,0:T(8,128)S(1)} %bitcast.52, bf16[2,120,1536]{2,1,0:T(8,128)(2,1)S(1)} %copy-done.10, bf16[2,120,1536]{2,1,0:T(8,128)(2,1)} %collective-permute-done.17.sibling), custom_call_target="tpu_custom_call" | custom-call | tf_op jit(solution)/shard_map/pallas_call | solution.py:83
  109.8 5.9 %shard_map.84 = (f32[4,160,192]{2,1,0:T(8,128)S(1)}, f32[4,160,192]{2,1,0:T(8,128)S(1)}, f32[4,160,192]{2,1,0:T(8,128)S(1)}) custom-call(bf16[160,3072]{1,0:T(8,128)(2,1)S(1)} %copy-done.8, bf16[160,3072]{1,0:T(8,128)(2,1)} %collective-permute-done.1.acts_b, bf16[160,3072]{1,0:T(8,128)(2,1)} %collective-permute-done.4.acts_c, ...), custom_call_target="tpu_custom_call" | custom-call | tf_op jit(solution)/shard_map/pallas_call | solution.py:157
  115.7 5.4 %collective-permute-done.14 = bf16[192,3072]{1,0:T(8,128)(2,1)S(1)} collective-permute-done((bf16[192,3072]{1,0:T(8,128)(2,1)S(1)}, bf16[192,3072]{1,0:T(8,128)(2,1)S(1)}, u32[]{:S(2)}, u32[]{:S(2)}) %collective-permute-start.14) | collective-permute-done | bytes 1179680 | tf_op jit(solution)/shard_map/ppermute | solution.py:242
  121.3 3.1 %shard_map.85 = f32[4,160,192]{2,1,0:T(8,128)S(1)} custom-call(bf16[160,3072]{1,0:T(8,128)(2,1)S(1)} %copy-done.8, bf16[160,3072]{1,0:T(8,128)(2,1)} %collective-permute-done.1.acts_b, bf16[160,3072]{1,0:T(8,128)(2,1)} %collective-permute-done.4.acts_c, bf16[160,3072]{1,0:T(8,128)(2,1)S(1)} %collective-permute-done.19.acts_d, ...), custom_call_target="tpu_custom_call" | custom-call | tf_op jit(solution)/shard_map/pallas_call | solution.py:157
  124.4 0.4 fusion.2
  124.9 1.6 collective-permute-start.20
  126.5 1.6 select_convert_fusion.2
  128.1 0.7 collective-permute-start.24
  128.8 2.1 %collective-permute-start.25 = (bf16[160,1536]{1,0:T(8,128)(2,1)S(1)}, bf16[160,1536]{1,0:T(8,128)(2,1)S(1)}, u32[]{:S(2)}, u32[]{:S(2)}) collective-permute-start(bf16[160,1536]{1,0:T(8,128)(2,1)S(1)} %get-tuple-element.112), channel_id=1, source_target_pairs={{0,8},{8,16},{25,17},{17,9},{2,10},{10,18},{27,19},{19,11},{4,12},... | collective-permute-start | bytes 1474568 | tf_op jit(solution)/shard_map/ppermute | solution.py:194
  130.9 0.2 select_bitcast_fusion
  131.1 10.0 %collective-permute-done.20 = bf16[2,4,160,192]{3,2,1,0:T(8,128)(2,1)S(1)} collective-permute-done((bf16[2,4,160,192]{3,2,1,0:T(8,128)(2,1)S(1)}, bf16[2,4,160,192]{3,2,1,0:T(8,128)(2,1)S(1)}, u32[]{:S(2)}, u32[]{:S(2)}) %collective-permute-start.20) | collective-permute-done | bytes 491552 | tf_op jit(solution)/shard_map/ppermute | solution.py:274
  141.3 0.8 collective-permute-start.23
  142.1 1.3 collective-permute-start.22
  143.5 0.5 select_convert_fusion.1
  144.0 1.3 collective-permute-start.26
  145.3 4.6 %collective-permute-start.27 = (bf16[160,1536]{1,0:T(8,128)(2,1)S(1)}, bf16[160,1536]{1,0:T(8,128)(2,1)S(1)}, u32[]{:S(2)}, u32[]{:S(2)}) collective-permute-start(bf16[160,1536]{1,0:T(8,128)(2,1)S(1)} %get-tuple-element.137), channel_id=1, source_target_pairs={{0,8},{8,16},{16,24},{9,1},{17,9},{25,17},{2,10},{10,18},{18,26},{... | collective-permute-start | bytes 1474568 | tf_op jit(solution)/shard_map/ppermute | solution.py:194
  150.0 0.2 fusion.5
  150.3 8.4 %collective-permute-done.26 = bf16[160,1536]{1,0:T(8,128)(2,1)S(1)} collective-permute-done((bf16[160,1536]{1,0:T(8,128)(2,1)S(1)}, bf16[160,1536]{1,0:T(8,128)(2,1)S(1)}, u32[]{:S(2)}, u32[]{:S(2)}) %collective-permute-start.26) | collective-permute-done | bytes 491552 | tf_op jit(solution)/shard_map/ppermute | solution.py:194
  158.7 1.2 collective-permute-done.27
  159.9 1.4 fusion.1
  (82 shorter events, 1.2 us)
Async XLA Ops:
  1.4 18.5 %copy-start = (bf16[1,1024,1536]{2,1,0:T(8,128)(2,1)S(1)}, bf16[1,1024,1536]{2,1,0:T(8,128)(2,1)}, u32[]{:S(2)}) copy-start(bf16[1,1024,1536]{2,1,0:T(8,128)(2,1)} %param.11) | copy-start | bytes 9437188
  4.5 34.8 %collective-permute-start.3 = (bf16[192,3072]{1,0:T(8,128)(2,1)}, bf16[192,3072]{1,0:T(8,128)(2,1)}, u32[]{:S(2)}, u32[]{:S(2)}) collective-permute-start(bf16[192,3072]{1,0:T(8,128)(2,1)} %bitcast.58), channel_id=1, source_target_pairs={{8,0},{16,8},{24,16},{9,1},{17,9},{25,17},{10,2},{18,10},{26,18},{... | collective-permute-start | bytes 3538952 | tf_op jit(solution)/shard_map/ppermute | solution.py:210
  5.8 33.5 %collective-permute-start.2 = (bf16[192,3072]{1,0:T(8,128)(2,1)}, bf16[192,3072]{1,0:T(8,128)(2,1)}, u32[]{:S(2)}, u32[]{:S(2)}) collective-permute-start(bf16[192,3072]{1,0:T(8,128)(2,1)} %bitcast.59), channel_id=1, source_target_pairs={{0,8},{8,16},{16,24},{1,9},{9,17},{17,25},{2,10},{10,18},{18,26},{... | collective-permute-start | bytes 3538952 | tf_op jit(solution)/shard_map/ppermute | solution.py:209
  12.4 26.9 %collective-permute-start.4 = (bf16[160,3072]{1,0:T(8,128)(2,1)}, bf16[160,3072]{1,0:T(8,128)(2,1)}, u32[]{:S(2)}, u32[]{:S(2)}) collective-permute-start(bf16[160,3072]{1,0:T(8,128)(2,1)} %acts_a.3), channel_id=1, source_target_pairs={{0,2},{2,0},{1,3},{3,1},{4,6},{6,4},{5,7},{7,5},{8,10},{10,8},{9,1... | collective-permute-start | bytes 2949128 | tf_op jit(solution)/shard_map/ppermute | solution.py:187
  12.4 26.9 %collective-permute-start.1 = (bf16[160,3072]{1,0:T(8,128)(2,1)}, bf16[160,3072]{1,0:T(8,128)(2,1)}, u32[]{:S(2)}, u32[]{:S(2)}) collective-permute-start(bf16[160,3072]{1,0:T(8,128)(2,1)} %acts_a.3), channel_id=1, source_target_pairs={{0,4},{4,0},{1,5},{5,1},{2,6},{6,2},{3,7},{7,3},{8,12},{12,8},{9,1... | collective-permute-start | bytes 2949128 | tf_op jit(solution)/shard_map/ppermute | solution.py:197
  14.3 25.0 %collective-permute-start = (bf16[480,1024]{1,0:T(8,128)(2,1)}, bf16[480,1024]{1,0:T(8,128)(2,1)}, u32[]{:S(2)}, u32[]{:S(2)}) collective-permute-start(bf16[480,1024]{1,0:T(8,128)(2,1)} %get-tuple-element.61), channel_id=1, source_target_pairs={{0,1},{1,0},{2,3},{3,2},{4,5},{5,4},{6,7},{7,6},{8,9},{9,8},{10,11... | collective-permute-start | bytes 2949128 | tf_op jit(solution)/shard_map/ppermute | solution.py:211
  15.8 23.2 %all-to-all-start = ((f32[8,2,160]{2,1,0:T(2,128)}), f32[8,2,160]{2,1,0:T(2,128)S(1)}, u32[]{:S(2)}, u32[]{:S(2)}) async-start(f32[8,2,160]{2,1,0:T(2,128)} %reshape.18), calls=%async_computation | async-start | bytes 32768 | tf_op jit(solution)/shard_map/all_to_all | solution.py:214
  19.9 1.5 copy-start.7
  27.0 1.2 copy-start.3
  28.2 1.1 copy-start.12
  39.3 7.0 %collective-permute-start.5 = (bf16[4,120,1536]{2,1,0:T(8,128)(2,1)}, bf16[4,120,1536]{2,1,0:T(8,128)(2,1)S(1)}, u32[]{:S(2)}, u32[]{:S(2)}) collective-permute-start(bf16[4,120,1536]{2,1,0:T(8,128)(2,1)} %copy-done.12), channel_id=1, source_target_pairs={{0,2},{2,0},{1,3},{3,1},{4,6},{6,4},{5,7},{7,5},{8,10},{10,8},{9,1... | collective-permute-start | bytes 4423688 | tf_op jit(solution)/shard_map/ppermute | solution.py:187
  39.4 1.9 %copy-start.1 = (bf16[1,1024,1536]{2,1,0:T(8,128)(2,1)S(1)}, bf16[1,1024,1536]{2,1,0:T(8,128)(2,1)}, u32[]{:S(2)}) copy-start(bf16[1,1024,1536]{2,1,0:T(8,128)(2,1)} %param.11) | copy-start | bytes 9437188
  41.3 5.0 %copy-start.4 = (bf16[4,120,1536]{2,1,0:T(8,128)(2,1)S(1)}, bf16[4,120,1536]{2,1,0:T(8,128)(2,1)}, u32[]{:S(2)}) copy-start(bf16[4,120,1536]{2,1,0:T(8,128)(2,1)} %copy-done.3) | copy-start | bytes 4423684
  45.7 4.5 %copy-start.18 = (bf16[480,1024]{1,0:T(8,128)(2,1)S(1)}, bf16[480,1024]{1,0:T(8,128)(2,1)}, u32[]{:S(2)}) copy-start(bf16[480,1024]{1,0:T(8,128)(2,1)} %get-tuple-element.78) | copy-start | bytes 2949124
  45.7 6.1 %collective-permute-start.7 = (bf16[2,120,1536]{2,1,0:T(8,128)(2,1)S(1)}, bf16[2,120,1536]{2,1,0:T(8,128)(2,1)S(1)}, u32[]{:S(2)}, u32[]{:S(2)}) collective-permute-start(bf16[2,120,1536]{2,1,0:T(8,128)(2,1)S(1)} %get-tuple-element.72), channel_id=1, source_target_pairs={{0,2},{2,0},{1,3},{3,1},{4,6},{6,4},{5,7},{7,5},{8,10},{10,8},{9,1... | collective-permute-start | bytes 2211848 | tf_op jit(solution)/shard_map/ppermute | solution.py:187
  46.3 18.2 %copy-start.5 = (bf16[4,120,1536]{2,1,0:T(8,128)(2,1)}, bf16[4,120,1536]{2,1,0:T(8,128)(2,1)S(1)}, u32[]{:S(2)}) copy-start(bf16[4,120,1536]{2,1,0:T(8,128)(2,1)S(1)} %collective-permute-done.5.sibling) | copy-start | bytes 4423684
  47.6 13.2 %collective-permute-start.6 = (bf16[160,1536]{1,0:T(8,128)(2,1)S(1)}, bf16[160,1536]{1,0:T(8,128)(2,1)S(1)}, u32[]{:S(2)}, u32[]{:S(2)}) collective-permute-start(bf16[160,1536]{1,0:T(8,128)(2,1)S(1)} %shard_map.74), channel_id=1, source_target_pairs={{0,4},{4,0},{1,5},{5,1},{2,6},{6,2},{3,7},{7,3},{8,12},{12,8},{9,1... | collective-permute-start | bytes 1474568 | tf_op jit(solution)/shard_map/ppermute | solution.py:197
  48.2 25.5 %collective-permute-start.10 = (bf16[192,3072]{1,0:T(8,128)(2,1)}, bf16[192,3072]{1,0:T(8,128)(2,1)S(1)}, u32[]{:S(2)}, u32[]{:S(2)}) collective-permute-start(bf16[192,3072]{1,0:T(8,128)(2,1)} %collective-permute-done.2), channel_id=1, source_target_pairs={{8,16},{16,24},{9,17},{17,25},{10,18},{18,26},{11,19},{19,27},{12,... | collective-permute-start | bytes 3538952 | tf_op jit(solution)/shard_map/ppermute | solution.py:223
  48.9 32.4 %collective-permute-start.11 = (bf16[192,3072]{1,0:T(8,128)(2,1)}, bf16[192,3072]{1,0:T(8,128)(2,1)S(1)}, u32[]{:S(2)}, u32[]{:S(2)}) collective-permute-start(bf16[192,3072]{1,0:T(8,128)(2,1)} %collective-permute-done.3), channel_id=1, source_target_pairs={{8,0},{16,8},{9,1},{17,9},{10,2},{18,10},{11,3},{19,11},{12,4},{20... | collective-permute-start | bytes 3538952 | tf_op jit(solution)/shard_map/ppermute | solution.py:224
  50.3 23.5 %collective-permute-start.12 = (bf16[480,1024]{1,0:T(8,128)(2,1)S(1)}, bf16[480,1024]{1,0:T(8,128)(2,1)S(1)}, u32[]{:S(2)}, u32[]{:S(2)}) collective-permute-start(bf16[480,1024]{1,0:T(8,128)(2,1)S(1)} %copy-done.18), channel_id=1, source_target_pairs={{0,1},{1,0},{2,3},{3,2},{4,5},{5,4},{6,7},{7,6},{8,9},{9,8},{10,11... | collective-permute-start | bytes 2949128 | tf_op jit(solution)/shard_map/ppermute | solution.py:225
  60.9 20.5 %collective-permute-start.8 = (bf16[160,1536]{1,0:T(8,128)(2,1)S(1)}, bf16[160,1536]{1,0:T(8,128)(2,1)S(1)}, u32[]{:S(2)}, u32[]{:S(2)}) collective-permute-start(bf16[160,1536]{1,0:T(8,128)(2,1)S(1)} %shard_map.76), channel_id=1, source_target_pairs={{0,4},{4,0},{1,5},{5,1},{2,6},{6,2},{3,7},{7,3},{8,12},{12,8},{9,1... | collective-permute-start | bytes 1474568 | tf_op jit(solution)/shard_map/ppermute | solution.py:197
  62.5 18.9 %collective-permute-start.9 = (bf16[160,1536]{1,0:T(8,128)(2,1)S(1)}, bf16[160,1536]{1,0:T(8,128)(2,1)S(1)}, u32[]{:S(2)}, u32[]{:S(2)}) collective-permute-start(bf16[160,1536]{1,0:T(8,128)(2,1)S(1)} %get-tuple-element.129), channel_id=1, source_target_pairs={{24,16},{1,9},{26,18},{3,11},{28,20},{5,13},{30,22},{7,15}} | collective-permute-start | bytes 1474568 | tf_op jit(solution)/shard_map/ppermute | solution.py:194
  64.5 16.9 %copy-start.2 = (bf16[1,1024,1536]{2,1,0:T(8,128)(2,1)S(1)}, bf16[1,1024,1536]{2,1,0:T(8,128)(2,1)}, u32[]{:S(2)}) copy-start(bf16[1,1024,1536]{2,1,0:T(8,128)(2,1)} %param.11) | copy-start | bytes 9437188
  73.7 11.6 %copy-start.14 = (bf16[192,3072]{1,0:T(8,128)(2,1)}, bf16[192,3072]{1,0:T(8,128)(2,1)S(1)}, u32[]{:S(2)}) copy-start(bf16[192,3072]{1,0:T(8,128)(2,1)S(1)} %collective-permute-done.10) | copy-start | bytes 3538948
  81.4 4.0 %copy-start.16 = (bf16[192,3072]{1,0:T(8,128)(2,1)}, bf16[192,3072]{1,0:T(8,128)(2,1)S(1)}, u32[]{:S(2)}) copy-start(bf16[192,3072]{1,0:T(8,128)(2,1)S(1)} %collective-permute-done.11) | copy-start | bytes 3538948
  81.4 4.0 %copy-start.22 = (bf16[160,1536]{1,0:T(8,128)(2,1)}, bf16[160,1536]{1,0:T(8,128)(2,1)S(1)}, u32[]{:S(2)}) copy-start(bf16[160,1536]{1,0:T(8,128)(2,1)S(1)} %collective-permute-done.8) | copy-start | bytes 1474564
  81.4 4.0 %copy-start.20 = (bf16[160,1536]{1,0:T(8,128)(2,1)}, bf16[160,1536]{1,0:T(8,128)(2,1)S(1)}, u32[]{:S(2)}) copy-start(bf16[160,1536]{1,0:T(8,128)(2,1)S(1)} %collective-permute-done.9) | copy-start | bytes 1474564
  81.4 6.3 %copy-start.24 = (f32[160,12]{0,1:T(8,128)S(1)}, f32[160,12]{0,1:T(8,128)}, u32[]{:S(2)}) copy-start(f32[160,12]{0,1:T(8,128)} %param.9) | copy-start | bytes 23044
  81.4 6.2 %copy-start.25 = (s32[160,12]{0,1:T(8,128)S(1)}, s32[160,12]{0,1:T(8,128)}, u32[]{:S(2)}) copy-start(s32[160,12]{0,1:T(8,128)} %param.8) | copy-start | bytes 23044
  85.4 0.9 copy-start.9
  86.3 6.2 %collective-permute-start.17 = (bf16[2,120,1536]{2,1,0:T(8,128)(2,1)}, bf16[2,120,1536]{2,1,0:T(8,128)(2,1)}, u32[]{:S(2)}, u32[]{:S(2)}) collective-permute-start(bf16[2,120,1536]{2,1,0:T(8,128)(2,1)} %get-tuple-element.87), channel_id=1, source_target_pairs={{0,2},{2,0},{1,3},{3,1},{4,6},{6,4},{5,7},{7,5},{8,10},{10,8},{9,1... | collective-permute-start | bytes 2211848 | tf_op jit(solution)/shard_map/ppermute | solution.py:187
  86.3 13.9 %collective-permute-start.16 = (bf16[160,1536]{1,0:T(8,128)(2,1)}, bf16[160,1536]{1,0:T(8,128)(2,1)}, u32[]{:S(2)}, u32[]{:S(2)}) collective-permute-start(bf16[160,1536]{1,0:T(8,128)(2,1)} %shard_map.78), channel_id=1, source_target_pairs={{0,4},{4,0},{1,5},{5,1},{2,6},{6,2},{3,7},{7,3},{8,12},{12,8},{9,1... | collective-permute-start | bytes 1474568 | tf_op jit(solution)/shard_map/ppermute | solution.py:197
  87.7 1.4 copy-start.6
  89.0 1.3 copy-start.15
  89.0 2.1 %copy-start.17 = (bf16[192,3072]{1,0:T(8,128)(2,1)S(1)}, bf16[192,3072]{1,0:T(8,128)(2,1)}, u32[]{:S(2)}) copy-start(bf16[192,3072]{1,0:T(8,128)(2,1)} %copy-done.16) | copy-start | bytes 3538948
  89.0 3.4 %copy-start.10 = (bf16[2,120,1536]{2,1,0:T(8,128)(2,1)S(1)}, bf16[2,120,1536]{2,1,0:T(8,128)(2,1)}, u32[]{:S(2)}) copy-start(bf16[2,120,1536]{2,1,0:T(8,128)(2,1)} %copy-done.9) | copy-start | bytes 2211844
  90.4 25.3 %collective-permute-start.13 = (bf16[192,3072]{1,0:T(8,128)(2,1)S(1)}, bf16[192,3072]{1,0:T(8,128)(2,1)S(1)}, u32[]{:S(2)}, u32[]{:S(2)}) collective-permute-start(bf16[192,3072]{1,0:T(8,128)(2,1)S(1)} %copy-done.15), channel_id=1, source_target_pairs={{16,24},{17,25},{18,26},{19,27},{20,28},{21,29},{22,30},{23,31}} | collective-permute-start | bytes 3538952 | tf_op jit(solution)/shard_map/ppermute | solution.py:241
  91.1 30.0 %collective-permute-start.14 = (bf16[192,3072]{1,0:T(8,128)(2,1)S(1)}, bf16[192,3072]{1,0:T(8,128)(2,1)S(1)}, u32[]{:S(2)}, u32[]{:S(2)}) collective-permute-start(bf16[192,3072]{1,0:T(8,128)(2,1)S(1)} %copy-done.17), channel_id=1, source_target_pairs={{8,0},{9,1},{10,2},{11,3},{12,4},{13,5},{14,6},{15,7}} | collective-permute-start | bytes 3538952 | tf_op jit(solution)/shard_map/ppermute | solution.py:242
  92.5 7.8 %copy-start.23 = (bf16[160,1536]{1,0:T(8,128)(2,1)S(1)}, bf16[160,1536]{1,0:T(8,128)(2,1)}, u32[]{:S(2)}) copy-start(bf16[160,1536]{1,0:T(8,128)(2,1)} %copy-done.22) | copy-start | bytes 1474564
  100.2 9.5 %collective-permute-start.19 = (bf16[160,3072]{1,0:T(8,128)(2,1)}, bf16[160,3072]{1,0:T(8,128)(2,1)S(1)}, u32[]{:S(2)}, u32[]{:S(2)}) collective-permute-start(bf16[160,3072]{1,0:T(8,128)(2,1)} %collective-permute-done.1.acts_b), channel_id=1, source_target_pairs={{0,2},{2,0},{1,3},{3,1},{4,6},{6,4},{5,7},{7,5},{8,10},{10,8},{9,1... | collective-permute-start | bytes 2949128 | tf_op jit(solution)/shard_map/ppermute | solution.py:187
  100.4 15.3 %collective-permute-start.15 = (bf16[160,1536]{1,0:T(8,128)(2,1)S(1)}, bf16[160,1536]{1,0:T(8,128)(2,1)S(1)}, u32[]{:S(2)}, u32[]{:S(2)}) collective-permute-start(bf16[160,1536]{1,0:T(8,128)(2,1)S(1)} %get-tuple-element.127), channel_id=1, source_target_pairs={{0,8},{25,17},{2,10},{27,19},{4,12},{29,21},{6,14},{31,23}} | collective-permute-start | bytes 1474568 | tf_op jit(solution)/shard_map/ppermute | solution.py:194
  104.3 16.8 %collective-permute-start.18 = (bf16[160,1536]{1,0:T(8,128)(2,1)S(1)}, bf16[160,1536]{1,0:T(8,128)(2,1)S(1)}, u32[]{:S(2)}, u32[]{:S(2)}) collective-permute-start(bf16[160,1536]{1,0:T(8,128)(2,1)S(1)} %shard_map.81), channel_id=1, source_target_pairs={{0,4},{4,0},{1,5},{5,1},{2,6},{6,2},{3,7},{7,3},{8,12},{12,8},{9,1... | collective-permute-start | bytes 1474568 | tf_op jit(solution)/shard_map/ppermute | solution.py:197
  107.3 2.4 %copy-start.8 = (bf16[160,3072]{1,0:T(8,128)(2,1)S(1)}, bf16[160,3072]{1,0:T(8,128)(2,1)}, u32[]{:S(2)}) copy-start(bf16[160,3072]{1,0:T(8,128)(2,1)} %acts_a.3) | copy-start | bytes 2949124
  107.3 2.4 %copy-start.11 = (bf16[3072,192]{0,1:T(8,128)(2,1)S(1)}, bf16[3072,192]{0,1:T(8,128)(2,1)}, u32[]{:S(2)}) copy-start(bf16[3072,192]{0,1:T(8,128)(2,1)} %param.13) | copy-start | bytes 3538948
  124.4 2.1 %copy-start.21 = (bf16[160,1536]{1,0:T(8,128)(2,1)S(1)}, bf16[160,1536]{1,0:T(8,128)(2,1)}, u32[]{:S(2)}) copy-start(bf16[160,1536]{1,0:T(8,128)(2,1)} %copy-done.20) | copy-start | bytes 1474564
  124.8 1.7 %copy-start.13 = (f32[160,1536]{1,0:T(8,128)S(1)}, f32[160,1536]{1,0:T(8,128)}, u32[]{:S(2)}) copy-start(f32[160,1536]{1,0:T(8,128)} %get-tuple-element.103) | copy-start | bytes 2949124
  124.9 16.1 %collective-permute-start.20 = (bf16[2,4,160,192]{3,2,1,0:T(8,128)(2,1)S(1)}, bf16[2,4,160,192]{3,2,1,0:T(8,128)(2,1)S(1)}, u32[]{:S(2)}, u32[]{:S(2)}) collective-permute-start(bf16[2,4,160,192]{3,2,1,0:T(8,128)(2,1)S(1)} %pad_maximum_fusion), channel_id=1, source_target_pairs={{0,1},{1,0},{2,3},{3,2},{4,5},{5,4},{6,7},{7,6},{8,9},{9,8},{10,11... | collective-permute-start | bytes 1474568 | tf_op jit(solution)/shard_map/ppermute | solution.py:274
  128.1 15.4 %collective-permute-start.24 = (bf16[160,1536]{1,0:T(8,128)(2,1)S(1)}, bf16[160,1536]{1,0:T(8,128)(2,1)S(1)}, u32[]{:S(2)}, u32[]{:S(2)}) collective-permute-start(bf16[160,1536]{1,0:T(8,128)(2,1)S(1)} %get-tuple-element.111), channel_id=1, source_target_pairs={{24,16},{16,8},{1,9},{9,17},{26,18},{18,10},{3,11},{11,19},{28,20}... | collective-permute-start | bytes 1474568 | tf_op jit(solution)/shard_map/ppermute | solution.py:194
  128.8 14.7 %collective-permute-start.25 = (bf16[160,1536]{1,0:T(8,128)(2,1)S(1)}, bf16[160,1536]{1,0:T(8,128)(2,1)S(1)}, u32[]{:S(2)}, u32[]{:S(2)}) collective-permute-start(bf16[160,1536]{1,0:T(8,128)(2,1)S(1)} %get-tuple-element.112), channel_id=1, source_target_pairs={{0,8},{8,16},{25,17},{17,9},{2,10},{10,18},{27,19},{19,11},{4,12},... | collective-permute-start | bytes 1474568 | tf_op jit(solution)/shard_map/ppermute | solution.py:194
  141.2 8.7 %collective-permute-start.21 = (bf16[2,160,192]{2,1,0:T(8,128)(2,1)S(1)}, bf16[2,160,192]{2,1,0:T(8,128)(2,1)S(1)}, u32[]{:S(2)}, u32[]{:S(2)}) collective-permute-start(bf16[2,160,192]{2,1,0:T(8,128)(2,1)S(1)} %get-tuple-element.145), channel_id=1, source_target_pairs={{0,6},{2,4},{4,2},{6,0},{1,7},{3,5},{5,3},{7,1},{8,14},{10,12},{12... | collective-permute-start | bytes 368648 | tf_op jit(solution)/shard_map/ppermute | solution.py:294
  141.3 8.5 %collective-permute-start.23 = (bf16[2,160,192]{2,1,0:T(8,128)(2,1)S(1)}, bf16[2,160,192]{2,1,0:T(8,128)(2,1)S(1)}, u32[]{:S(2)}, u32[]{:S(2)}) collective-permute-start(bf16[2,160,192]{2,1,0:T(8,128)(2,1)S(1)} %get-tuple-element.146), channel_id=1, source_target_pairs={{0,2},{2,0},{1,3},{3,1},{4,6},{6,4},{5,7},{7,5},{8,10},{10,8},{9,1... | collective-permute-start | bytes 368648 | tf_op jit(solution)/shard_map/ppermute | solution.py:292
  142.1 7.8 %collective-permute-start.22 = (bf16[2,160,192]{2,1,0:T(8,128)(2,1)S(1)}, bf16[2,160,192]{2,1,0:T(8,128)(2,1)S(1)}, u32[]{:S(2)}, u32[]{:S(2)}) collective-permute-start(bf16[2,160,192]{2,1,0:T(8,128)(2,1)S(1)} %get-tuple-element.147), channel_id=1, source_target_pairs={{0,4},{4,0},{1,5},{5,1},{2,6},{6,2},{3,7},{7,3},{8,12},{12,8},{9,1... | collective-permute-start | bytes 368648 | tf_op jit(solution)/shard_map/ppermute | solution.py:293
  144.0 14.7 %collective-permute-start.26 = (bf16[160,1536]{1,0:T(8,128)(2,1)S(1)}, bf16[160,1536]{1,0:T(8,128)(2,1)S(1)}, u32[]{:S(2)}, u32[]{:S(2)}) collective-permute-start(bf16[160,1536]{1,0:T(8,128)(2,1)S(1)} %get-tuple-element.136), channel_id=1, source_target_pairs={{8,0},{16,8},{24,16},{1,9},{9,17},{17,25},{10,2},{18,10},{26,18},{... | collective-permute-start | bytes 1474568 | tf_op jit(solution)/shard_map/ppermute | solution.py:194
  145.3 14.6 %collective-permute-start.27 = (bf16[160,1536]{1,0:T(8,128)(2,1)S(1)}, bf16[160,1536]{1,0:T(8,128)(2,1)S(1)}, u32[]{:S(2)}, u32[]{:S(2)}) collective-permute-start(bf16[160,1536]{1,0:T(8,128)(2,1)S(1)} %get-tuple-element.137), channel_id=1, source_target_pairs={{0,8},{8,16},{16,24},{9,1},{17,9},{25,17},{2,10},{10,18},{18,26},{... | collective-permute-start | bytes 1474568 | tf_op jit(solution)/shard_map/ppermute | solution.py:194
  150.2 9.6 %copy-start.19 = (bf16[160,1536]{1,0:T(8,128)(2,1)S(1)}, bf16[160,1536]{1,0:T(8,128)(2,1)}, u32[]{:S(2)}) copy-start(bf16[160,1536]{1,0:T(8,128)(2,1)} %param.7) | copy-start | bytes 1474564

commit v5 on v4

--- a/solution.py
+++ b/solution.py
@@ -291,7 +291,8 @@
     near = dense[:, 0, 0]
     by_c = lax.ppermute(dense[:, 1, 0].astype(BF16), "c", SWAP).astype(F32)
     by_y = lax.ppermute(dense[:, 0, 1].astype(BF16), "y", SWAP).astype(F32)
-    by_both = lax.ppermute(dense[:, 1, 1].astype(BF16), ("y", "c"), [(0, 3), (1, 2), (2, 1), (3, 0)]).astype(F32)
+    by_y, far_rows = tie((by_y, dense[:, 1, 1].astype(BF16)))
+    by_both = lax.ppermute(far_rows, ("y", "c"), [(0, 3), (1, 2), (2, 1), (3, 0)]).astype(F32)
 
     def ordered(first, second, swap):
         return jnp.where(swap, second, first), jnp.where(swap, first, second)

time: 162 us -> 161 us (level)
    ppermute x6, waiting for transfers between devices: 9.56 us -> 3.58 us  [hop(): return lax.ppermute(value.astype(BF16), ('z', 'tp'), pairs)]
    ppermute x1, waiting for transfers between devices: 0.01 us -> 5.78 us  [four_by_two(): lax.ppermute(far_rows, ('y', 'c'), [(0, 3), (1, 2), (2, 1), (3, 0)])]
  transfers between devices with their start and end apart: 29 -> 29, of which waited for: 9 -> 10; matrix products, arithmetic and copies ran while one was open for 4% -> 4% of each run, Pallas kernels for 18% -> 18%
where the time goes in v5:
time: 161 us; the launch traced here: 160 us
  waiting for transfers between devices  61 us (38%)
  starting transfers between devices  41.7 us (26%)
  Pallas kernels  36.2 us (22%)
  local copies, waits for them, and re-layouts  12.2 us (8%)
  other arithmetic  8.5 us (5%)
    pallas_call x3, Pallas kernels, expert_tables(): pl.pallas_call(tables_kernel, out_shape=(shape, shape), grid_spec=pltpu.P...  13.8 us
    pallas_call x8, Pallas kernels, combine(): pl.pallas_call(combine_kernel, out_shape=jax.ShapeDtypeStruct((tokens, fe...  13.4 us
    ppermute x6, starting transfers between devices, hop(): return lax.ppermute(value.astype(BF16), ('z', 'tp'), pairs)  13.2 us
    ppermute x5, waiting for transfers between devices, over_y(): return lax.ppermute(value, 'y', SWAP)  11.8 us
    ppermute x1, waiting for transfers between devices, four_by_two(): theirs = lax.ppermute(theirs, 'tp', SWAP)  9.98 us
    all_to_all x1, waiting for transfers between devices, four_by_two(): gates = lax.all_to_all(gates, ('z', 'y'), 0, 0, tiled=True)  9.72 us
    pallas_call x2, Pallas kernels, products(): pl.pallas_call(products_kernel, out_shape=[jax.ShapeDtypeStruct(shape, F3...  9.02 us
    unnamed x52, local copies, waits for them, and re-layouts  8.07 us
  transfers between devices with their start and end apart: 29, of which 10 were waited for; matrix products, arithmetic and copies ran while one was open for 4% of the time, Pallas kernels for 18%

profile of v5, /device:TPU:0, one launch (start us, length us, event | category | flops | bytes accessed | tf_op | source)
XLA Modules:
  0.0 160.3 jit_solution(6622149657253069173)
XLA Ops:
  0.0 0.8 select_reduce_fusion
  0.8 0.6 reshape.18
  1.4 3.1 %dynamic-slice_bitcast_fusion = (bf16[480,1024]{1,0:T(8,128)(2,1)}, bf16[480,1024]{1,0:T(8,128)(2,1)}) fusion(bf16[2,480,1024]{2,1,0:T(8,128)(2,1)} %bitcast.56, s32[]{:T(128)S(6)} %select_n.197, s32[]{:T(128)S(6)} %select_n.195), kind=kLoop, calls=%fused_computation.16 | loop fusion | bytes 3932168 | tf_op jit(solution)/shard_map/jit(dynamic_index_in_dim)/squeeze | solution.py:16
  4.5 1.3 collective-permute-start.3
  5.8 6.6 %collective-permute-start.2 = (bf16[192,3072]{1,0:T(8,128)(2,1)}, bf16[192,3072]{1,0:T(8,128)(2,1)}, u32[]{:S(2)}, u32[]{:S(2)}) collective-permute-start(bf16[192,3072]{1,0:T(8,128)(2,1)} %bitcast.59), channel_id=1, source_target_pairs={{0,8},{8,16},{16,24},{1,9},{9,17},{17,25},{2,10},{10,18},{18,26},{... | collective-permute-start | bytes 3538952 | tf_op jit(solution)/shard_map/ppermute | solution.py:209
  12.4 2.0 %collective-permute-start.1 = (bf16[160,3072]{1,0:T(8,128)(2,1)}, bf16[160,3072]{1,0:T(8,128)(2,1)}, u32[]{:S(2)}, u32[]{:S(2)}) collective-permute-start(bf16[160,3072]{1,0:T(8,128)(2,1)} %acts_a.3), channel_id=1, source_target_pairs={{0,4},{4,0},{1,5},{5,1},{2,6},{6,2},{3,7},{7,3},{8,12},{12,8},{9,1... | collective-permute-start | bytes 2949128 | tf_op jit(solution)/shard_map/ppermute | solution.py:197
  14.3 1.5 collective-permute-start
  15.8 4.0 %all-to-all-start = ((f32[8,2,160]{2,1,0:T(2,128)}), f32[8,2,160]{2,1,0:T(2,128)S(1)}, u32[]{:S(2)}, u32[]{:S(2)}) async-start(f32[8,2,160]{2,1,0:T(2,128)} %reshape.18), calls=%async_computation | async-start | bytes 32768 | tf_op jit(solution)/shard_map/all_to_all | solution.py:214
  19.9 1.5 copy-done.7
  21.5 5.5 %shard_map.73 = (bf16[4,120,1536]{2,1,0:T(8,128)(2,1)S(1)}, bf16[4,120,1536]{2,1,0:T(8,128)(2,1)S(1)}) custom-call(s32[3]{0:T(128)S(1)} %pad_add_fusion.here, bf16[4,2,120,1024]{3,2,1,0:T(8,128)(2,1)S(1)} %bitcast.57, bf16[1024,1536]{1,0:T(8,128)(2,1)S(1)} %bitcast.53), custom_call_target="tpu_custom_call" | custom-call | tf_op jit(solution)/shard_map/pallas_call | solution.py:119
  27.0 1.2 copy-done.3
  28.2 1.1 copy-done.12
  29.3 9.7 %all-to-all-done.gates = f32[8,2,160]{2,1,0:T(2,128)S(1)} async-done(((f32[8,2,160]{2,1,0:T(2,128)}), f32[8,2,160]{2,1,0:T(2,128)S(1)}, u32[]{:S(2)}, u32[]{:S(2)}) %all-to-all-start) | async-done | bytes 10272 | tf_op jit(solution)/shard_map/all_to_all | solution.py:214
  39.0 0.3 copy.32
  39.4 1.9 %copy-done.1 = bf16[1,1024,1536]{2,1,0:T(8,128)(2,1)S(1)} copy-done((bf16[1,1024,1536]{2,1,0:T(8,128)(2,1)S(1)}, bf16[1,1024,1536]{2,1,0:T(8,128)(2,1)}, u32[]{:S(2)}) %copy-start.1) | copy-done | bytes 3145752
  41.3 4.4 %shard_map.75 = (bf16[2,120,1536]{2,1,0:T(8,128)(2,1)S(1)}, bf16[2,120,1536]{2,1,0:T(8,128)(2,1)S(1)}) custom-call(s32[3]{0:T(128)S(1)} %pad_add_fusion.here, bf16[2,2,120,1024]{3,2,1,0:T(8,128)(2,1)} %bitcast.12.hidden, bf16[1024,1536]{1,0:T(8,128)(2,1)S(1)} %bitcast.54), custom_call_target="tpu_custom_call" | custom-call | tf_op jit(solution)/shard_map/pallas_call | solution.py:119
  45.7 0.6 collective-permute-start.7
  46.3 1.3 shard_map.74
  47.6 0.6 collective-permute-start.6
  48.2 0.7 collective-permute-start.10
  48.9 1.3 collective-permute-start.11
  50.3 1.6 collective-permute-start.12
  51.8 1.3 shard_map.76
  53.1 1.3 shard_map.77
  54.5 6.4 %collective-permute-done.6 = bf16[160,1536]{1,0:T(8,128)(2,1)S(1)} collective-permute-done((bf16[160,1536]{1,0:T(8,128)(2,1)S(1)}, bf16[160,1536]{1,0:T(8,128)(2,1)S(1)}, u32[]{:S(2)}, u32[]{:S(2)}) %collective-permute-start.6) | collective-permute-done | bytes 491552 | tf_op jit(solution)/shard_map/ppermute | solution.py:197
  60.9 0.5 collective-permute-start.8
  61.4 1.1 fusion.7
  62.5 0.7 collective-permute-start.9
  63.2 1.3 shard_map.79
  64.5 2.1 %shard_map.78 = bf16[160,1536]{1,0:T(8,128)(2,1)} custom-call(s32[3]{0:T(128)S(1)} %pad_add_fusion.here, f32[8,2,160]{2,1,0:T(2,128)S(1)} %all-to-all-done.gates, f32[8,160,2]{2,1,0:T(8,128)S(1)} %bitcast.49, bf16[4,120,1536]{2,1,0:T(8,128)(2,1)S(1)} %copy-done.4, bf16[4,120,1536]{2,1,0:T(8,128)(2,1)S(1)} %collective-permute-done.5.sibling), custom_call_target="tpu_custom_call" | custom-call | tf_op jit(solution)/shard_map/pallas_call | solution.py:83
  66.6 7.1 %collective-permute-done.12 = bf16[480,1024]{1,0:T(8,128)(2,1)S(1)} collective-permute-done((bf16[480,1024]{1,0:T(8,128)(2,1)S(1)}, bf16[480,1024]{1,0:T(8,128)(2,1)S(1)}, u32[]{:S(2)}, u32[]{:S(2)}) %collective-permute-start.12) | collective-permute-done | bytes 983072 | tf_op jit(solution)/shard_map/ppermute | solution.py:225
  73.7 7.6 %collective-permute-done.11 = bf16[192,3072]{1,0:T(8,128)(2,1)S(1)} collective-permute-done((bf16[192,3072]{1,0:T(8,128)(2,1)}, bf16[192,3072]{1,0:T(8,128)(2,1)S(1)}, u32[]{:S(2)}, u32[]{:S(2)}) %collective-permute-start.11) | collective-permute-done | bytes 1179680 | tf_op jit(solution)/shard_map/ppermute | solution.py:224
  81.4 3.9 %shard_map.80 = (bf16[2,120,1536]{2,1,0:T(8,128)(2,1)}, bf16[2,120,1536]{2,1,0:T(8,128)(2,1)S(1)}) custom-call(s32[3]{0:T(128)S(1)} %pad_add_fusion.here, bf16[2,2,120,1024]{3,2,1,0:T(8,128)(2,1)S(1)} %bitcast.61, bf16[1024,1536]{1,0:T(8,128)(2,1)S(1)} %bitcast.55), custom_call_target="tpu_custom_call" | custom-call | tf_op jit(solution)/shard_map/pallas_call | solution.py:119
  85.4 0.9 copy-done.9
  86.3 1.4 collective-permute-start.16
  87.7 1.4 copy-done.6
  89.0 1.3 shard_map.82
  90.4 0.7 collective-permute-start.13
  91.1 1.3 collective-permute-start.14
  92.5 2.3 %shard_map.81 = bf16[160,1536]{1,0:T(8,128)(2,1)S(1)} custom-call(s32[3]{0:T(128)S(1)} %pad_add_fusion.here, f32[8,2,160]{2,1,0:T(2,128)S(1)} %all-to-all-done.gates, f32[8,160,2]{2,1,0:T(8,128)S(1)} %bitcast.51, bf16[2,120,1536]{2,1,0:T(8,128)(2,1)S(1)} %copy-done.10, bf16[2,120,1536]{2,1,0:T(8,128)(2,1)} %collective-permute-done.17.sibling), custom_call_target="tpu_custom_call" | custom-call | tf_op jit(solution)/shard_map/pallas_call | solution.py:83
  94.8 5.4 %collective-permute-done.16 = bf16[160,1536]{1,0:T(8,128)(2,1)} collective-permute-done((bf16[160,1536]{1,0:T(8,128)(2,1)}, bf16[160,1536]{1,0:T(8,128)(2,1)}, u32[]{:S(2)}, u32[]{:S(2)}) %collective-permute-start.16) | collective-permute-done | bytes 491552 | tf_op jit(solution)/shard_map/ppermute | solution.py:197
  100.4 3.9 %collective-permute-start.15 = (bf16[160,1536]{1,0:T(8,128)(2,1)S(1)}, bf16[160,1536]{1,0:T(8,128)(2,1)S(1)}, u32[]{:S(2)}, u32[]{:S(2)}) collective-permute-start(bf16[160,1536]{1,0:T(8,128)(2,1)S(1)} %get-tuple-element.131), channel_id=1, source_target_pairs={{0,8},{25,17},{2,10},{27,19},{4,12},{29,21},{6,14},{31,23}} | collective-permute-start | bytes 1474568 | tf_op jit(solution)/shard_map/ppermute | solution.py:194
  104.3 1.5 collective-permute-start.18
  105.8 1.5 broadcast_select_fusion
  107.3 2.4 %shard_map.83 = f32[160,1536]{1,0:T(8,128)S(1)} custom-call(s32[3]{0:T(128)S(1)} %pad_add_fusion.here, f32[8,2,160]{2,1,0:T(2,128)S(1)} %all-to-all-done.gates, f32[8,160,2]{2,1,0:T(8,128)S(1)} %bitcast.52, bf16[2,120,1536]{2,1,0:T(8,128)(2,1)S(1)} %copy-done.10, bf16[2,120,1536]{2,1,0:T(8,128)(2,1)} %collective-permute-done.17.sibling), custom_call_target="tpu_custom_call" | custom-call | tf_op jit(solution)/shard_map/pallas_call | solution.py:83
  109.8 5.9 %shard_map.84 = (f32[4,160,192]{2,1,0:T(8,128)S(1)}, f32[4,160,192]{2,1,0:T(8,128)S(1)}, f32[4,160,192]{2,1,0:T(8,128)S(1)}) custom-call(bf16[160,3072]{1,0:T(8,128)(2,1)S(1)} %copy-done.8, bf16[160,3072]{1,0:T(8,128)(2,1)} %collective-permute-done.1.acts_b, bf16[160,3072]{1,0:T(8,128)(2,1)} %collective-permute-done.4.acts_c, ...), custom_call_target="tpu_custom_call" | custom-call | tf_op jit(solution)/shard_map/pallas_call | solution.py:157
  115.7 5.4 %collective-permute-done.14 = bf16[192,3072]{1,0:T(8,128)(2,1)S(1)} collective-permute-done((bf16[192,3072]{1,0:T(8,128)(2,1)S(1)}, bf16[192,3072]{1,0:T(8,128)(2,1)S(1)}, u32[]{:S(2)}, u32[]{:S(2)}) %collective-permute-start.14) | collective-permute-done | bytes 1179680 | tf_op jit(solution)/shard_map/ppermute | solution.py:242
  121.3 3.1 %shard_map.85 = f32[4,160,192]{2,1,0:T(8,128)S(1)} custom-call(bf16[160,3072]{1,0:T(8,128)(2,1)S(1)} %copy-done.8, bf16[160,3072]{1,0:T(8,128)(2,1)} %collective-permute-done.1.acts_b, bf16[160,3072]{1,0:T(8,128)(2,1)} %collective-permute-done.4.acts_c, bf16[160,3072]{1,0:T(8,128)(2,1)S(1)} %collective-permute-done.19.acts_d, ...), custom_call_target="tpu_custom_call" | custom-call | tf_op jit(solution)/shard_map/pallas_call | solution.py:157
  124.4 0.4 fusion.2
  124.9 1.6 collective-permute-start.20
  126.5 1.6 select_convert_fusion.2
  128.1 0.7 collective-permute-start.24
  128.8 2.1 %collective-permute-start.25 = (bf16[160,1536]{1,0:T(8,128)(2,1)S(1)}, bf16[160,1536]{1,0:T(8,128)(2,1)S(1)}, u32[]{:S(2)}, u32[]{:S(2)}) collective-permute-start(bf16[160,1536]{1,0:T(8,128)(2,1)S(1)} %get-tuple-element.116), channel_id=1, source_target_pairs={{0,8},{8,16},{25,17},{17,9},{2,10},{10,18},{27,19},{19,11},{4,12},... | collective-permute-start | bytes 1474568 | tf_op jit(solution)/shard_map/ppermute | solution.py:194
  131.1 10.0 %collective-permute-done.20 = bf16[2,4,160,192]{3,2,1,0:T(8,128)(2,1)S(1)} collective-permute-done((bf16[2,4,160,192]{3,2,1,0:T(8,128)(2,1)S(1)}, bf16[2,4,160,192]{3,2,1,0:T(8,128)(2,1)S(1)}, u32[]{:S(2)}, u32[]{:S(2)}) %collective-permute-start.20) | collective-permute-done | bytes 491552 | tf_op jit(solution)/shard_map/ppermute | solution.py:274
  141.3 0.7 collective-permute-start.21
  142.1 0.5 select_convert_fusion.1
  142.6 1.3 collective-permute-start.26
  143.9 4.6 %collective-permute-start.27 = (bf16[160,1536]{1,0:T(8,128)(2,1)S(1)}, bf16[160,1536]{1,0:T(8,128)(2,1)S(1)}, u32[]{:S(2)}, u32[]{:S(2)}) collective-permute-start(bf16[160,1536]{1,0:T(8,128)(2,1)S(1)} %get-tuple-element.141), channel_id=1, source_target_pairs={{0,8},{8,16},{16,24},{9,1},{17,9},{25,17},{2,10},{10,18},{18,26},{... | collective-permute-start | bytes 1474568 | tf_op jit(solution)/shard_map/ppermute | solution.py:194
  148.5 0.6 collective-permute-start.22
  149.2 5.8 %collective-permute-done.22 = bf16[2,160,192]{2,1,0:T(8,128)(2,1)S(1)} collective-permute-done((bf16[2,160,192]{2,1,0:T(8,128)(2,1)S(1)}, bf16[2,160,192]{2,1,0:T(8,128)(2,1)S(1)}, u32[]{:S(2)}, u32[]{:S(2)}) %collective-permute-start.22) | collective-permute-done | bytes 122912 | tf_op jit(solution)/shard_map/ppermute | solution.py:295
  155.0 0.2 fusion.5
  155.4 2.4 %collective-permute-done.26 = bf16[160,1536]{1,0:T(8,128)(2,1)S(1)} collective-permute-done((bf16[160,1536]{1,0:T(8,128)(2,1)S(1)}, bf16[160,1536]{1,0:T(8,128)(2,1)S(1)}, u32[]{:S(2)}, u32[]{:S(2)}) %collective-permute-start.26) | collective-permute-done | bytes 491552 | tf_op jit(solution)/shard_map/ppermute | solution.py:194
  157.8 1.2 collective-permute-done.27
  158.9 1.4 fusion.1
  (83 shorter events, 1.4 us)
Async XLA Ops:
  1.4 18.5 %copy-start = (bf16[1,1024,1536]{2,1,0:T(8,128)(2,1)S(1)}, bf16[1,1024,1536]{2,1,0:T(8,128)(2,1)}, u32[]{:S(2)}) copy-start(bf16[1,1024,1536]{2,1,0:T(8,128)(2,1)} %param.11) | copy-start | bytes 9437188
  4.5 34.8 %collective-permute-start.3 = (bf16[192,3072]{1,0:T(8,128)(2,1)}, bf16[192,3072]{1,0:T(8,128)(2,1)}, u32[]{:S(2)}, u32[]{:S(2)}) collective-permute-start(bf16[192,3072]{1,0:T(8,128)(2,1)} %bitcast.58), channel_id=1, source_target_pairs={{8,0},{16,8},{24,16},{9,1},{17,9},{25,17},{10,2},{18,10},{26,18},{... | collective-permute-start | bytes 3538952 | tf_op jit(solution)/shard_map/ppermute | solution.py:210
  5.8 33.5 %collective-permute-start.2 = (bf16[192,3072]{1,0:T(8,128)(2,1)}, bf16[192,3072]{1,0:T(8,128)(2,1)}, u32[]{:S(2)}, u32[]{:S(2)}) collective-permute-start(bf16[192,3072]{1,0:T(8,128)(2,1)} %bitcast.59), channel_id=1, source_target_pairs={{0,8},{8,16},{16,24},{1,9},{9,17},{17,25},{2,10},{10,18},{18,26},{... | collective-permute-start | bytes 3538952 | tf_op jit(solution)/shard_map/ppermute | solution.py:209
  12.4 26.9 %collective-permute-start.4 = (bf16[160,3072]{1,0:T(8,128)(2,1)}, bf16[160,3072]{1,0:T(8,128)(2,1)}, u32[]{:S(2)}, u32[]{:S(2)}) collective-permute-start(bf16[160,3072]{1,0:T(8,128)(2,1)} %acts_a.3), channel_id=1, source_target_pairs={{0,2},{2,0},{1,3},{3,1},{4,6},{6,4},{5,7},{7,5},{8,10},{10,8},{9,1... | collective-permute-start | bytes 2949128 | tf_op jit(solution)/shard_map/ppermute | solution.py:187
  12.4 26.9 %collective-permute-start.1 = (bf16[160,3072]{1,0:T(8,128)(2,1)}, bf16[160,3072]{1,0:T(8,128)(2,1)}, u32[]{:S(2)}, u32[]{:S(2)}) collective-permute-start(bf16[160,3072]{1,0:T(8,128)(2,1)} %acts_a.3), channel_id=1, source_target_pairs={{0,4},{4,0},{1,5},{5,1},{2,6},{6,2},{3,7},{7,3},{8,12},{12,8},{9,1... | collective-permute-start | bytes 2949128 | tf_op jit(solution)/shard_map/ppermute | solution.py:197
  14.3 25.0 %collective-permute-start = (bf16[480,1024]{1,0:T(8,128)(2,1)}, bf16[480,1024]{1,0:T(8,128)(2,1)}, u32[]{:S(2)}, u32[]{:S(2)}) collective-permute-start(bf16[480,1024]{1,0:T(8,128)(2,1)} %get-tuple-element.63), channel_id=1, source_target_pairs={{0,1},{1,0},{2,3},{3,2},{4,5},{5,4},{6,7},{7,6},{8,9},{9,8},{10,11... | collective-permute-start | bytes 2949128 | tf_op jit(solution)/shard_map/ppermute | solution.py:211
  15.8 23.2 %all-to-all-start = ((f32[8,2,160]{2,1,0:T(2,128)}), f32[8,2,160]{2,1,0:T(2,128)S(1)}, u32[]{:S(2)}, u32[]{:S(2)}) async-start(f32[8,2,160]{2,1,0:T(2,128)} %reshape.18), calls=%async_computation | async-start | bytes 32768 | tf_op jit(solution)/shard_map/all_to_all | solution.py:214
  19.9 1.5 copy-start.7
  27.0 1.2 copy-start.3
  28.2 1.1 copy-start.12
  39.3 7.0 %collective-permute-start.5 = (bf16[4,120,1536]{2,1,0:T(8,128)(2,1)}, bf16[4,120,1536]{2,1,0:T(8,128)(2,1)S(1)}, u32[]{:S(2)}, u32[]{:S(2)}) collective-permute-start(bf16[4,120,1536]{2,1,0:T(8,128)(2,1)} %copy-done.12), channel_id=1, source_target_pairs={{0,2},{2,0},{1,3},{3,1},{4,6},{6,4},{5,7},{7,5},{8,10},{10,8},{9,1... | collective-permute-start | bytes 4423688 | tf_op jit(solution)/shard_map/ppermute | solution.py:187
  39.4 1.9 %copy-start.1 = (bf16[1,1024,1536]{2,1,0:T(8,128)(2,1)S(1)}, bf16[1,1024,1536]{2,1,0:T(8,128)(2,1)}, u32[]{:S(2)}) copy-start(bf16[1,1024,1536]{2,1,0:T(8,128)(2,1)} %param.11) | copy-start | bytes 9437188
  41.3 5.0 %copy-start.4 = (bf16[4,120,1536]{2,1,0:T(8,128)(2,1)S(1)}, bf16[4,120,1536]{2,1,0:T(8,128)(2,1)}, u32[]{:S(2)}) copy-start(bf16[4,120,1536]{2,1,0:T(8,128)(2,1)} %copy-done.3) | copy-start | bytes 4423684
  45.7 4.5 %copy-start.18 = (bf16[480,1024]{1,0:T(8,128)(2,1)S(1)}, bf16[480,1024]{1,0:T(8,128)(2,1)}, u32[]{:S(2)}) copy-start(bf16[480,1024]{1,0:T(8,128)(2,1)} %get-tuple-element.80) | copy-start | bytes 2949124
  45.7 6.1 %collective-permute-start.7 = (bf16[2,120,1536]{2,1,0:T(8,128)(2,1)S(1)}, bf16[2,120,1536]{2,1,0:T(8,128)(2,1)S(1)}, u32[]{:S(2)}, u32[]{:S(2)}) collective-permute-start(bf16[2,120,1536]{2,1,0:T(8,128)(2,1)S(1)} %get-tuple-element.74), channel_id=1, source_target_pairs={{0,2},{2,0},{1,3},{3,1},{4,6},{6,4},{5,7},{7,5},{8,10},{10,8},{9,1... | collective-permute-start | bytes 2211848 | tf_op jit(solution)/shard_map/ppermute | solution.py:187
  46.3 18.2 %copy-start.5 = (bf16[4,120,1536]{2,1,0:T(8,128)(2,1)}, bf16[4,120,1536]{2,1,0:T(8,128)(2,1)S(1)}, u32[]{:S(2)}) copy-start(bf16[4,120,1536]{2,1,0:T(8,128)(2,1)S(1)} %collective-permute-done.5.sibling) | copy-start | bytes 4423684
  47.6 13.2 %collective-permute-start.6 = (bf16[160,1536]{1,0:T(8,128)(2,1)S(1)}, bf16[160,1536]{1,0:T(8,128)(2,1)S(1)}, u32[]{:S(2)}, u32[]{:S(2)}) collective-permute-start(bf16[160,1536]{1,0:T(8,128)(2,1)S(1)} %shard_map.74), channel_id=1, source_target_pairs={{0,4},{4,0},{1,5},{5,1},{2,6},{6,2},{3,7},{7,3},{8,12},{12,8},{9,1... | collective-permute-start | bytes 1474568 | tf_op jit(solution)/shard_map/ppermute | solution.py:197
  48.2 25.5 %collective-permute-start.10 = (bf16[192,3072]{1,0:T(8,128)(2,1)}, bf16[192,3072]{1,0:T(8,128)(2,1)S(1)}, u32[]{:S(2)}, u32[]{:S(2)}) collective-permute-start(bf16[192,3072]{1,0:T(8,128)(2,1)} %collective-permute-done.2), channel_id=1, source_target_pairs={{8,16},{16,24},{9,17},{17,25},{10,18},{18,26},{11,19},{19,27},{12,... | collective-permute-start | bytes 3538952 | tf_op jit(solution)/shard_map/ppermute | solution.py:223
  48.9 32.4 %collective-permute-start.11 = (bf16[192,3072]{1,0:T(8,128)(2,1)}, bf16[192,3072]{1,0:T(8,128)(2,1)S(1)}, u32[]{:S(2)}, u32[]{:S(2)}) collective-permute-start(bf16[192,3072]{1,0:T(8,128)(2,1)} %collective-permute-done.3), channel_id=1, source_target_pairs={{8,0},{16,8},{9,1},{17,9},{10,2},{18,10},{11,3},{19,11},{12,4},{20... | collective-permute-start | bytes 3538952 | tf_op jit(solution)/shard_map/ppermute | solution.py:224
  50.3 23.5 %collective-permute-start.12 = (bf16[480,1024]{1,0:T(8,128)(2,1)S(1)}, bf16[480,1024]{1,0:T(8,128)(2,1)S(1)}, u32[]{:S(2)}, u32[]{:S(2)}) collective-permute-start(bf16[480,1024]{1,0:T(8,128)(2,1)S(1)} %copy-done.18), channel_id=1, source_target_pairs={{0,1},{1,0},{2,3},{3,2},{4,5},{5,4},{6,7},{7,6},{8,9},{9,8},{10,11... | collective-permute-start | bytes 2949128 | tf_op jit(solution)/shard_map/ppermute | solution.py:225
  60.9 20.5 %collective-permute-start.8 = (bf16[160,1536]{1,0:T(8,128)(2,1)S(1)}, bf16[160,1536]{1,0:T(8,128)(2,1)S(1)}, u32[]{:S(2)}, u32[]{:S(2)}) collective-permute-start(bf16[160,1536]{1,0:T(8,128)(2,1)S(1)} %shard_map.76), channel_id=1, source_target_pairs={{0,4},{4,0},{1,5},{5,1},{2,6},{6,2},{3,7},{7,3},{8,12},{12,8},{9,1... | collective-permute-start | bytes 1474568 | tf_op jit(solution)/shard_map/ppermute | solution.py:197
  62.5 18.9 %collective-permute-start.9 = (bf16[160,1536]{1,0:T(8,128)(2,1)S(1)}, bf16[160,1536]{1,0:T(8,128)(2,1)S(1)}, u32[]{:S(2)}, u32[]{:S(2)}) collective-permute-start(bf16[160,1536]{1,0:T(8,128)(2,1)S(1)} %get-tuple-element.133), channel_id=1, source_target_pairs={{24,16},{1,9},{26,18},{3,11},{28,20},{5,13},{30,22},{7,15}} | collective-permute-start | bytes 1474568 | tf_op jit(solution)/shard_map/ppermute | solution.py:194
  64.5 16.9 %copy-start.2 = (bf16[1,1024,1536]{2,1,0:T(8,128)(2,1)S(1)}, bf16[1,1024,1536]{2,1,0:T(8,128)(2,1)}, u32[]{:S(2)}) copy-start(bf16[1,1024,1536]{2,1,0:T(8,128)(2,1)} %param.11) | copy-start | bytes 9437188
  73.7 11.6 %copy-start.14 = (bf16[192,3072]{1,0:T(8,128)(2,1)}, bf16[192,3072]{1,0:T(8,128)(2,1)S(1)}, u32[]{:S(2)}) copy-start(bf16[192,3072]{1,0:T(8,128)(2,1)S(1)} %collective-permute-done.10) | copy-start | bytes 3538948
  81.4 4.0 %copy-start.16 = (bf16[192,3072]{1,0:T(8,128)(2,1)}, bf16[192,3072]{1,0:T(8,128)(2,1)S(1)}, u32[]{:S(2)}) copy-start(bf16[192,3072]{1,0:T(8,128)(2,1)S(1)} %collective-permute-done.11) | copy-start | bytes 3538948
  81.4 4.0 %copy-start.22 = (bf16[160,1536]{1,0:T(8,128)(2,1)}, bf16[160,1536]{1,0:T(8,128)(2,1)S(1)}, u32[]{:S(2)}) copy-start(bf16[160,1536]{1,0:T(8,128)(2,1)S(1)} %collective-permute-done.8) | copy-start | bytes 1474564
  81.4 4.0 %copy-start.20 = (bf16[160,1536]{1,0:T(8,128)(2,1)}, bf16[160,1536]{1,0:T(8,128)(2,1)S(1)}, u32[]{:S(2)}) copy-start(bf16[160,1536]{1,0:T(8,128)(2,1)S(1)} %collective-permute-done.9) | copy-start | bytes 1474564
  81.4 6.3 %copy-start.24 = (f32[160,12]{0,1:T(8,128)S(1)}, f32[160,12]{0,1:T(8,128)}, u32[]{:S(2)}) copy-start(f32[160,12]{0,1:T(8,128)} %param.9) | copy-start | bytes 23044
  81.4 6.2 %copy-start.25 = (s32[160,12]{0,1:T(8,128)S(1)}, s32[160,12]{0,1:T(8,128)}, u32[]{:S(2)}) copy-start(s32[160,12]{0,1:T(8,128)} %param.8) | copy-start | bytes 23044
  85.4 0.9 copy-start.9
  86.3 6.2 %collective-permute-start.17 = (bf16[2,120,1536]{2,1,0:T(8,128)(2,1)}, bf16[2,120,1536]{2,1,0:T(8,128)(2,1)}, u32[]{:S(2)}, u32[]{:S(2)}) collective-permute-start(bf16[2,120,1536]{2,1,0:T(8,128)(2,1)} %get-tuple-element.89), channel_id=1, source_target_pairs={{0,2},{2,0},{1,3},{3,1},{4,6},{6,4},{5,7},{7,5},{8,10},{10,8},{9,1... | collective-permute-start | bytes 2211848 | tf_op jit(solution)/shard_map/ppermute | solution.py:187
  86.3 13.9 %collective-permute-start.16 = (bf16[160,1536]{1,0:T(8,128)(2,1)}, bf16[160,1536]{1,0:T(8,128)(2,1)}, u32[]{:S(2)}, u32[]{:S(2)}) collective-permute-start(bf16[160,1536]{1,0:T(8,128)(2,1)} %shard_map.78), channel_id=1, source_target_pairs={{0,4},{4,0},{1,5},{5,1},{2,6},{6,2},{3,7},{7,3},{8,12},{12,8},{9,1... | collective-permute-start | bytes 1474568 | tf_op jit(solution)/shard_map/ppermute | solution.py:197
  87.7 1.4 copy-start.6
  89.0 1.3 copy-start.15
  89.0 2.1 %copy-start.17 = (bf16[192,3072]{1,0:T(8,128)(2,1)S(1)}, bf16[192,3072]{1,0:T(8,128)(2,1)}, u32[]{:S(2)}) copy-start(bf16[192,3072]{1,0:T(8,128)(2,1)} %copy-done.16) | copy-start | bytes 3538948
  89.0 3.4 %copy-start.10 = (bf16[2,120,1536]{2,1,0:T(8,128)(2,1)S(1)}, bf16[2,120,1536]{2,1,0:T(8,128)(2,1)}, u32[]{:S(2)}) copy-start(bf16[2,120,1536]{2,1,0:T(8,128)(2,1)} %copy-done.9) | copy-start | bytes 2211844
  90.4 25.3 %collective-permute-start.13 = (bf16[192,3072]{1,0:T(8,128)(2,1)S(1)}, bf16[192,3072]{1,0:T(8,128)(2,1)S(1)}, u32[]{:S(2)}, u32[]{:S(2)}) collective-permute-start(bf16[192,3072]{1,0:T(8,128)(2,1)S(1)} %copy-done.15), channel_id=1, source_target_pairs={{16,24},{17,25},{18,26},{19,27},{20,28},{21,29},{22,30},{23,31}} | collective-permute-start | bytes 3538952 | tf_op jit(solution)/shard_map/ppermute | solution.py:241
  91.1 30.0 %collective-permute-start.14 = (bf16[192,3072]{1,0:T(8,128)(2,1)S(1)}, bf16[192,3072]{1,0:T(8,128)(2,1)S(1)}, u32[]{:S(2)}, u32[]{:S(2)}) collective-permute-start(bf16[192,3072]{1,0:T(8,128)(2,1)S(1)} %copy-done.17), channel_id=1, source_target_pairs={{8,0},{9,1},{10,2},{11,3},{12,4},{13,5},{14,6},{15,7}} | collective-permute-start | bytes 3538952 | tf_op jit(solution)/shard_map/ppermute | solution.py:242
  92.5 7.8 %copy-start.23 = (bf16[160,1536]{1,0:T(8,128)(2,1)S(1)}, bf16[160,1536]{1,0:T(8,128)(2,1)}, u32[]{:S(2)}) copy-start(bf16[160,1536]{1,0:T(8,128)(2,1)} %copy-done.22) | copy-start | bytes 1474564
  100.2 9.5 %collective-permute-start.19 = (bf16[160,3072]{1,0:T(8,128)(2,1)}, bf16[160,3072]{1,0:T(8,128)(2,1)S(1)}, u32[]{:S(2)}, u32[]{:S(2)}) collective-permute-start(bf16[160,3072]{1,0:T(8,128)(2,1)} %collective-permute-done.1.acts_b), channel_id=1, source_target_pairs={{0,2},{2,0},{1,3},{3,1},{4,6},{6,4},{5,7},{7,5},{8,10},{10,8},{9,1... | collective-permute-start | bytes 2949128 | tf_op jit(solution)/shard_map/ppermute | solution.py:187
  100.4 15.3 %collective-permute-start.15 = (bf16[160,1536]{1,0:T(8,128)(2,1)S(1)}, bf16[160,1536]{1,0:T(8,128)(2,1)S(1)}, u32[]{:S(2)}, u32[]{:S(2)}) collective-permute-start(bf16[160,1536]{1,0:T(8,128)(2,1)S(1)} %get-tuple-element.131), channel_id=1, source_target_pairs={{0,8},{25,17},{2,10},{27,19},{4,12},{29,21},{6,14},{31,23}} | collective-permute-start | bytes 1474568 | tf_op jit(solution)/shard_map/ppermute | solution.py:194
  104.3 16.8 %collective-permute-start.18 = (bf16[160,1536]{1,0:T(8,128)(2,1)S(1)}, bf16[160,1536]{1,0:T(8,128)(2,1)S(1)}, u32[]{:S(2)}, u32[]{:S(2)}) collective-permute-start(bf16[160,1536]{1,0:T(8,128)(2,1)S(1)} %shard_map.81), channel_id=1, source_target_pairs={{0,4},{4,0},{1,5},{5,1},{2,6},{6,2},{3,7},{7,3},{8,12},{12,8},{9,1... | collective-permute-start | bytes 1474568 | tf_op jit(solution)/shard_map/ppermute | solution.py:197
  107.3 2.4 %copy-start.8 = (bf16[160,3072]{1,0:T(8,128)(2,1)S(1)}, bf16[160,3072]{1,0:T(8,128)(2,1)}, u32[]{:S(2)}) copy-start(bf16[160,3072]{1,0:T(8,128)(2,1)} %acts_a.3) | copy-start | bytes 2949124
  107.3 2.4 %copy-start.11 = (bf16[3072,192]{0,1:T(8,128)(2,1)S(1)}, bf16[3072,192]{0,1:T(8,128)(2,1)}, u32[]{:S(2)}) copy-start(bf16[3072,192]{0,1:T(8,128)(2,1)} %param.13) | copy-start | bytes 3538948
  124.4 2.1 %copy-start.21 = (bf16[160,1536]{1,0:T(8,128)(2,1)S(1)}, bf16[160,1536]{1,0:T(8,128)(2,1)}, u32[]{:S(2)}) copy-start(bf16[160,1536]{1,0:T(8,128)(2,1)} %copy-done.20) | copy-start | bytes 1474564
  124.8 1.7 %copy-start.13 = (f32[160,1536]{1,0:T(8,128)S(1)}, f32[160,1536]{1,0:T(8,128)}, u32[]{:S(2)}) copy-start(f32[160,1536]{1,0:T(8,128)} %get-tuple-element.107) | copy-start | bytes 2949124
  124.9 16.1 %collective-permute-start.20 = (bf16[2,4,160,192]{3,2,1,0:T(8,128)(2,1)S(1)}, bf16[2,4,160,192]{3,2,1,0:T(8,128)(2,1)S(1)}, u32[]{:S(2)}, u32[]{:S(2)}) collective-permute-start(bf16[2,4,160,192]{3,2,1,0:T(8,128)(2,1)S(1)} %pad_maximum_fusion), channel_id=1, source_target_pairs={{0,1},{1,0},{2,3},{3,2},{4,5},{5,4},{6,7},{7,6},{8,9},{9,8},{10,11... | collective-permute-start | bytes 1474568 | tf_op jit(solution)/shard_map/ppermute | solution.py:274
  128.1 14.0 %collective-permute-start.24 = (bf16[160,1536]{1,0:T(8,128)(2,1)S(1)}, bf16[160,1536]{1,0:T(8,128)(2,1)S(1)}, u32[]{:S(2)}, u32[]{:S(2)}) collective-permute-start(bf16[160,1536]{1,0:T(8,128)(2,1)S(1)} %get-tuple-element.115), channel_id=1, source_target_pairs={{24,16},{16,8},{1,9},{9,17},{26,18},{18,10},{3,11},{11,19},{28,20}... | collective-permute-start | bytes 1474568 | tf_op jit(solution)/shard_map/ppermute | solution.py:194
  128.8 13.3 %collective-permute-start.25 = (bf16[160,1536]{1,0:T(8,128)(2,1)S(1)}, bf16[160,1536]{1,0:T(8,128)(2,1)S(1)}, u32[]{:S(2)}, u32[]{:S(2)}) collective-permute-start(bf16[160,1536]{1,0:T(8,128)(2,1)S(1)} %get-tuple-element.116), channel_id=1, source_target_pairs={{0,8},{8,16},{25,17},{17,9},{2,10},{10,18},{27,19},{19,11},{4,12},... | collective-permute-start | bytes 1474568 | tf_op jit(solution)/shard_map/ppermute | solution.py:194
  141.2 7.9 %collective-permute-start.23 = (bf16[2,160,192]{2,1,0:T(8,128)(2,1)S(1)}, bf16[2,160,192]{2,1,0:T(8,128)(2,1)S(1)}, u32[]{:S(2)}, u32[]{:S(2)}) collective-permute-start(bf16[2,160,192]{2,1,0:T(8,128)(2,1)S(1)} %get-tuple-element.150), channel_id=1, source_target_pairs={{0,2},{2,0},{1,3},{3,1},{4,6},{6,4},{5,7},{7,5},{8,10},{10,8},{9,1... | collective-permute-start | bytes 368648 | tf_op jit(solution)/shard_map/ppermute | solution.py:292
  141.3 7.1 %collective-permute-start.21 = (bf16[2,160,192]{2,1,0:T(8,128)(2,1)S(1)}, bf16[2,160,192]{2,1,0:T(8,128)(2,1)S(1)}, u32[]{:S(2)}, u32[]{:S(2)}) collective-permute-start(bf16[2,160,192]{2,1,0:T(8,128)(2,1)S(1)} %get-tuple-element.151), channel_id=1, source_target_pairs={{0,4},{4,0},{1,5},{5,1},{2,6},{6,2},{3,7},{7,3},{8,12},{12,8},{9,1... | collective-permute-start | bytes 368648 | tf_op jit(solution)/shard_map/ppermute | solution.py:293
  142.6 15.2 %collective-permute-start.26 = (bf16[160,1536]{1,0:T(8,128)(2,1)S(1)}, bf16[160,1536]{1,0:T(8,128)(2,1)S(1)}, u32[]{:S(2)}, u32[]{:S(2)}) collective-permute-start(bf16[160,1536]{1,0:T(8,128)(2,1)S(1)} %get-tuple-element.140), channel_id=1, source_target_pairs={{8,0},{16,8},{24,16},{1,9},{9,17},{17,25},{10,2},{18,10},{26,18},{... | collective-permute-start | bytes 1474568 | tf_op jit(solution)/shard_map/ppermute | solution.py:194
  143.9 15.1 %collective-permute-start.27 = (bf16[160,1536]{1,0:T(8,128)(2,1)S(1)}, bf16[160,1536]{1,0:T(8,128)(2,1)S(1)}, u32[]{:S(2)}, u32[]{:S(2)}) collective-permute-start(bf16[160,1536]{1,0:T(8,128)(2,1)S(1)} %get-tuple-element.141), channel_id=1, source_target_pairs={{0,8},{8,16},{16,24},{9,1},{17,9},{25,17},{2,10},{10,18},{18,26},{... | collective-permute-start | bytes 1474568 | tf_op jit(solution)/shard_map/ppermute | solution.py:194
  148.5 6.5 %collective-permute-start.22 = (bf16[2,160,192]{2,1,0:T(8,128)(2,1)S(1)}, bf16[2,160,192]{2,1,0:T(8,128)(2,1)S(1)}, u32[]{:S(2)}, u32[]{:S(2)}) collective-permute-start(bf16[2,160,192]{2,1,0:T(8,128)(2,1)S(1)} %get-tuple-element.105), channel_id=1, source_target_pairs={{0,6},{2,4},{4,2},{6,0},{1,7},{3,5},{5,3},{7,1},{8,14},{10,12},{12... | collective-permute-start | bytes 368648 | tf_op jit(solution)/shard_map/ppermute | solution.py:295
  155.3 3.7 %copy-start.19 = (bf16[160,1536]{1,0:T(8,128)(2,1)S(1)}, bf16[160,1536]{1,0:T(8,128)(2,1)}, u32[]{:S(2)}) copy-start(bf16[160,1536]{1,0:T(8,128)(2,1)} %param.7) | copy-start | bytes 1474564

commit v6 on v5

--- a/solution.py
+++ b/solution.py
@@ -205,7 +205,7 @@
     halves = hidden.reshape(2, 4 * capacity, hidden.shape[1])
     weights = dense_down.T
     gates = gate_rows(expert_ids, gate_weights, experts).reshape(8, 2, rows)
-    weights, hidden_0, gates = tie((weights, pick(halves, x), gates))
+    hidden_0 = pick(halves, x)
     weights_r1 = lax.ppermute(weights, "z", right)
     weights_l1 = lax.ppermute(weights, "z", left)
     hidden_0 = lax.ppermute(hidden_0, "tp", SWAP)

time: 161 us -> 159 us (0.988)
    all_to_all x1, waiting for transfers between devices: 9.72 us -> 5.91 us  [four_by_two(): gates = lax.all_to_all(gates, ('z', 'y'), 0, 0, tiled=True)]
    ppermute x1, waiting for transfers between devices: 0.01 us -> 2.38 us  [four_by_two(): hidden_0 = lax.ppermute(hidden_0, 'tp', SWAP)]
  transfers between devices with their start and end apart: 29 -> 29, of which waited for: 10 -> 11; matrix products, arithmetic and copies ran while one was open for 4% -> 6% of each run, Pallas kernels for 18% -> 19%
where the time goes in v6:
time: 159 us; the launch traced here: 158 us
  waiting for transfers between devices  59.4 us (37%)
  starting transfers between devices  41.7 us (26%)
  Pallas kernels  36.2 us (23%)
  local copies, waits for them, and re-layouts  12.2 us (8%)
  other arithmetic  7.77 us (5%)
    pallas_call x3, Pallas kernels, expert_tables(): pl.pallas_call(tables_kernel, out_shape=(shape, shape), grid_spec=pltpu.P...  13.8 us
    pallas_call x8, Pallas kernels, combine(): pl.pallas_call(combine_kernel, out_shape=jax.ShapeDtypeStruct((tokens, fe...  13.4 us
    ppermute x6, starting transfers between devices, hop(): return lax.ppermute(value.astype(BF16), ('z', 'tp'), pairs)  13.2 us
    ppermute x5, waiting for transfers between devices, over_y(): return lax.ppermute(value, 'y', SWAP)  11.7 us
    ppermute x1, waiting for transfers between devices, four_by_two(): theirs = lax.ppermute(theirs, 'tp', SWAP)  9.98 us
    pallas_call x2, Pallas kernels, products(): pl.pallas_call(products_kernel, out_shape=[jax.ShapeDtypeStruct(shape, F3...  9.03 us
    unnamed x52, local copies, waits for them, and re-layouts  8.07 us
    ppermute x1, waiting for transfers between devices, four_by_two(): weights_l2 = lax.ppermute(weights_l1, 'z', left[:2])  7.6 us
  transfers between devices with their start and end apart: 29, of which 11 were waited for; matrix products, arithmetic and copies ran while one was open for 6% of the time, Pallas kernels for 19%

profile of v6, /device:TPU:0, one launch (start us, length us, event | category | flops | bytes accessed | tf_op | source)
XLA Modules:
  0.0 157.8 jit_solution(1294493809301685877)
XLA Ops:
  0.0 1.3 collective-permute-start.3
  1.3 6.6 %collective-permute-start.2 = (bf16[192,3072]{1,0:T(8,128)(2,1)}, bf16[192,3072]{1,0:T(8,128)(2,1)}, u32[]{:S(2)}, u32[]{:S(2)}) collective-permute-start(bf16[192,3072]{1,0:T(8,128)(2,1)} %bitcast.59), channel_id=1, source_target_pairs={{0,8},{8,16},{16,24},{1,9},{9,17},{17,25},{2,10},{10,18},{18,26},{... | collective-permute-start | bytes 3538952 | tf_op jit(solution)/shard_map/ppermute | solution.py:209
  7.9 2.0 %collective-permute-start.1 = (bf16[160,3072]{1,0:T(8,128)(2,1)}, bf16[160,3072]{1,0:T(8,128)(2,1)}, u32[]{:S(2)}, u32[]{:S(2)}) collective-permute-start(bf16[160,3072]{1,0:T(8,128)(2,1)} %acts_a.3), channel_id=1, source_target_pairs={{0,4},{4,0},{1,5},{5,1},{2,6},{6,2},{3,7},{7,3},{8,12},{12,8},{9,1... | collective-permute-start | bytes 2949128 | tf_op jit(solution)/shard_map/ppermute | solution.py:197
  9.8 3.1 %dynamic-slice_bitcast_fusion = (bf16[480,1024]{1,0:T(8,128)(2,1)}, bf16[480,1024]{1,0:T(8,128)(2,1)}) fusion(bf16[2,480,1024]{2,1,0:T(8,128)(2,1)} %bitcast.56, s32[]{:T(128)S(6)} %select_n.197, s32[]{:T(128)S(6)} %select_n.195), kind=kLoop, calls=%fused_computation.16 | loop fusion | bytes 3932168 | tf_op jit(solution)/shard_map/jit(dynamic_index_in_dim)/squeeze | solution.py:16
  13.0 1.5 collective-permute-start
  14.5 0.6 reshape.18
  15.1 4.0 %all-to-all-start = ((f32[8,2,160]{2,1,0:T(2,128)}), f32[8,2,160]{2,1,0:T(2,128)S(1)}, u32[]{:S(2)}, u32[]{:S(2)}) async-start(f32[8,2,160]{2,1,0:T(2,128)} %reshape.18), calls=%async_computation | async-start | bytes 32768 | tf_op jit(solution)/shard_map/all_to_all | solution.py:214
  19.2 1.5 copy-done.7
  20.8 5.5 %shard_map.73 = (bf16[4,120,1536]{2,1,0:T(8,128)(2,1)S(1)}, bf16[4,120,1536]{2,1,0:T(8,128)(2,1)S(1)}) custom-call(s32[3]{0:T(128)S(1)} %pad_add_fusion.here, bf16[4,2,120,1024]{3,2,1,0:T(8,128)(2,1)S(1)} %bitcast.57, bf16[1024,1536]{1,0:T(8,128)(2,1)S(1)} %bitcast.53), custom_call_target="tpu_custom_call" | custom-call | tf_op jit(solution)/shard_map/pallas_call | solution.py:119
  26.3 1.2 copy-done.3
  27.5 1.1 copy-done.12
  28.6 5.9 %all-to-all-done.gates = f32[8,2,160]{2,1,0:T(2,128)S(1)} async-done(((f32[8,2,160]{2,1,0:T(2,128)}), f32[8,2,160]{2,1,0:T(2,128)S(1)}, u32[]{:S(2)}, u32[]{:S(2)}) %all-to-all-start) | async-done | bytes 10272 | tf_op jit(solution)/shard_map/all_to_all | solution.py:214
  34.5 0.3 copy.32
  34.8 2.4 %collective-permute-done = bf16[480,1024]{1,0:T(8,128)(2,1)} collective-permute-done((bf16[480,1024]{1,0:T(8,128)(2,1)}, bf16[480,1024]{1,0:T(8,128)(2,1)}, u32[]{:S(2)}, u32[]{:S(2)}) %collective-permute-start) | collective-permute-done | bytes 983072 | tf_op jit(solution)/shard_map/ppermute | solution.py:211
  37.2 1.9 %copy-done.1 = bf16[1,1024,1536]{2,1,0:T(8,128)(2,1)S(1)} copy-done((bf16[1,1024,1536]{2,1,0:T(8,128)(2,1)S(1)}, bf16[1,1024,1536]{2,1,0:T(8,128)(2,1)}, u32[]{:S(2)}) %copy-start.1) | copy-done | bytes 3145752
  39.1 4.4 %shard_map.75 = (bf16[2,120,1536]{2,1,0:T(8,128)(2,1)S(1)}, bf16[2,120,1536]{2,1,0:T(8,128)(2,1)S(1)}) custom-call(s32[3]{0:T(128)S(1)} %pad_add_fusion.here, bf16[2,2,120,1024]{3,2,1,0:T(8,128)(2,1)} %bitcast.12.hidden, bf16[1024,1536]{1,0:T(8,128)(2,1)S(1)} %bitcast.54), custom_call_target="tpu_custom_call" | custom-call | tf_op jit(solution)/shard_map/pallas_call | solution.py:119
  43.5 0.6 collective-permute-start.7
  44.1 1.3 shard_map.74
  45.4 0.3 collective-permute-start.6
  45.8 0.7 collective-permute-start.10
  46.5 1.3 collective-permute-start.11
  47.8 1.8 %collective-permute-start.12 = (bf16[480,1024]{1,0:T(8,128)(2,1)S(1)}, bf16[480,1024]{1,0:T(8,128)(2,1)S(1)}, u32[]{:S(2)}, u32[]{:S(2)}) collective-permute-start(bf16[480,1024]{1,0:T(8,128)(2,1)S(1)} %copy-done.18), channel_id=1, source_target_pairs={{0,1},{1,0},{2,3},{3,2},{4,5},{5,4},{6,7},{7,6},{8,9},{9,8},{10,11... | collective-permute-start | bytes 2949128 | tf_op jit(solution)/shard_map/ppermute | solution.py:225
  49.6 1.3 shard_map.76
  50.9 1.3 shard_map.77
  52.2 6.4 %collective-permute-done.6 = bf16[160,1536]{1,0:T(8,128)(2,1)S(1)} collective-permute-done((bf16[160,1536]{1,0:T(8,128)(2,1)S(1)}, bf16[160,1536]{1,0:T(8,128)(2,1)S(1)}, u32[]{:S(2)}, u32[]{:S(2)}) %collective-permute-start.6) | collective-permute-done | bytes 491552 | tf_op jit(solution)/shard_map/ppermute | solution.py:197
  58.6 0.3 collective-permute-start.8
  58.9 1.1 fusion.7
  60.0 0.7 collective-permute-start.9
  60.7 1.3 shard_map.79
  62.1 2.1 %shard_map.78 = bf16[160,1536]{1,0:T(8,128)(2,1)} custom-call(s32[3]{0:T(128)S(1)} %pad_add_fusion.here, f32[8,2,160]{2,1,0:T(2,128)S(1)} %all-to-all-done.gates, f32[8,160,2]{2,1,0:T(8,128)S(1)} %bitcast.49, bf16[4,120,1536]{2,1,0:T(8,128)(2,1)S(1)} %copy-done.4, bf16[4,120,1536]{2,1,0:T(8,128)(2,1)S(1)} %collective-permute-done.5.sibling), custom_call_target="tpu_custom_call" | custom-call | tf_op jit(solution)/shard_map/pallas_call | solution.py:83
  64.2 7.1 %collective-permute-done.12 = bf16[480,1024]{1,0:T(8,128)(2,1)S(1)} collective-permute-done((bf16[480,1024]{1,0:T(8,128)(2,1)S(1)}, bf16[480,1024]{1,0:T(8,128)(2,1)S(1)}, u32[]{:S(2)}, u32[]{:S(2)}) %collective-permute-start.12) | collective-permute-done | bytes 983072 | tf_op jit(solution)/shard_map/ppermute | solution.py:225
  71.3 7.6 %collective-permute-done.11 = bf16[192,3072]{1,0:T(8,128)(2,1)S(1)} collective-permute-done((bf16[192,3072]{1,0:T(8,128)(2,1)}, bf16[192,3072]{1,0:T(8,128)(2,1)S(1)}, u32[]{:S(2)}, u32[]{:S(2)}) %collective-permute-start.11) | collective-permute-done | bytes 1179680 | tf_op jit(solution)/shard_map/ppermute | solution.py:224
  78.9 3.9 %shard_map.80 = (bf16[2,120,1536]{2,1,0:T(8,128)(2,1)}, bf16[2,120,1536]{2,1,0:T(8,128)(2,1)S(1)}) custom-call(s32[3]{0:T(128)S(1)} %pad_add_fusion.here, bf16[2,2,120,1024]{3,2,1,0:T(8,128)(2,1)S(1)} %bitcast.61, bf16[1024,1536]{1,0:T(8,128)(2,1)S(1)} %bitcast.55), custom_call_target="tpu_custom_call" | custom-call | tf_op jit(solution)/shard_map/pallas_call | solution.py:119
  82.9 0.9 copy-done.9
  83.8 1.5 collective-permute-start.16
  85.3 1.4 copy-done.6
  86.7 1.3 shard_map.82
  88.1 0.7 collective-permute-start.13
  88.8 1.3 collective-permute-start.14
  90.1 2.3 %shard_map.81 = bf16[160,1536]{1,0:T(8,128)(2,1)S(1)} custom-call(s32[3]{0:T(128)S(1)} %pad_add_fusion.here, f32[8,2,160]{2,1,0:T(2,128)S(1)} %all-to-all-done.gates, f32[8,160,2]{2,1,0:T(8,128)S(1)} %bitcast.51, bf16[2,120,1536]{2,1,0:T(8,128)(2,1)S(1)} %copy-done.10, bf16[2,120,1536]{2,1,0:T(8,128)(2,1)} %collective-permute-done.17.sibling), custom_call_target="tpu_custom_call" | custom-call | tf_op jit(solution)/shard_map/pallas_call | solution.py:83
  92.5 5.3 %collective-permute-done.16 = bf16[160,1536]{1,0:T(8,128)(2,1)} collective-permute-done((bf16[160,1536]{1,0:T(8,128)(2,1)}, bf16[160,1536]{1,0:T(8,128)(2,1)}, u32[]{:S(2)}, u32[]{:S(2)}) %collective-permute-start.16) | collective-permute-done | bytes 491552 | tf_op jit(solution)/shard_map/ppermute | solution.py:197
  97.9 3.9 %collective-permute-start.15 = (bf16[160,1536]{1,0:T(8,128)(2,1)S(1)}, bf16[160,1536]{1,0:T(8,128)(2,1)S(1)}, u32[]{:S(2)}, u32[]{:S(2)}) collective-permute-start(bf16[160,1536]{1,0:T(8,128)(2,1)S(1)} %get-tuple-element.125), channel_id=1, source_target_pairs={{0,8},{25,17},{2,10},{27,19},{4,12},{29,21},{6,14},{31,23}} | collective-permute-start | bytes 1474568 | tf_op jit(solution)/shard_map/ppermute | solution.py:194
  101.8 1.6 %collective-permute-start.18 = (bf16[160,1536]{1,0:T(8,128)(2,1)S(1)}, bf16[160,1536]{1,0:T(8,128)(2,1)S(1)}, u32[]{:S(2)}, u32[]{:S(2)}) collective-permute-start(bf16[160,1536]{1,0:T(8,128)(2,1)S(1)} %shard_map.81), channel_id=1, source_target_pairs={{0,4},{4,0},{1,5},{5,1},{2,6},{6,2},{3,7},{7,3},{8,12},{12,8},{9,1... | collective-permute-start | bytes 1474568 | tf_op jit(solution)/shard_map/ppermute | solution.py:197
  103.4 1.5 broadcast_select_fusion
  104.9 2.4 %shard_map.83 = f32[160,1536]{1,0:T(8,128)S(1)} custom-call(s32[3]{0:T(128)S(1)} %pad_add_fusion.here, f32[8,2,160]{2,1,0:T(2,128)S(1)} %all-to-all-done.gates, f32[8,160,2]{2,1,0:T(8,128)S(1)} %bitcast.52, bf16[2,120,1536]{2,1,0:T(8,128)(2,1)S(1)} %copy-done.10, bf16[2,120,1536]{2,1,0:T(8,128)(2,1)} %collective-permute-done.17.sibling), custom_call_target="tpu_custom_call" | custom-call | tf_op jit(solution)/shard_map/pallas_call | solution.py:83
  107.4 5.9 %shard_map.84 = (f32[4,160,192]{2,1,0:T(8,128)S(1)}, f32[4,160,192]{2,1,0:T(8,128)S(1)}, f32[4,160,192]{2,1,0:T(8,128)S(1)}) custom-call(bf16[160,3072]{1,0:T(8,128)(2,1)S(1)} %copy-done.8, bf16[160,3072]{1,0:T(8,128)(2,1)} %collective-permute-done.1.acts_b, bf16[160,3072]{1,0:T(8,128)(2,1)} %collective-permute-done.4.acts_c, ...), custom_call_target="tpu_custom_call" | custom-call | tf_op jit(solution)/shard_map/pallas_call | solution.py:157
  113.3 5.5 %collective-permute-done.14 = bf16[192,3072]{1,0:T(8,128)(2,1)S(1)} collective-permute-done((bf16[192,3072]{1,0:T(8,128)(2,1)S(1)}, bf16[192,3072]{1,0:T(8,128)(2,1)S(1)}, u32[]{:S(2)}, u32[]{:S(2)}) %collective-permute-start.14) | collective-permute-done | bytes 1179680 | tf_op jit(solution)/shard_map/ppermute | solution.py:242
  119.0 3.1 %shard_map.85 = f32[4,160,192]{2,1,0:T(8,128)S(1)} custom-call(bf16[160,3072]{1,0:T(8,128)(2,1)S(1)} %copy-done.8, bf16[160,3072]{1,0:T(8,128)(2,1)} %collective-permute-done.1.acts_b, bf16[160,3072]{1,0:T(8,128)(2,1)} %collective-permute-done.4.acts_c, bf16[160,3072]{1,0:T(8,128)(2,1)S(1)} %collective-permute-done.19.acts_d, ...), custom_call_target="tpu_custom_call" | custom-call | tf_op jit(solution)/shard_map/pallas_call | solution.py:157
  122.1 0.4 fusion.2
  122.6 1.5 collective-permute-start.20
  124.2 1.6 %select_convert_fusion.2 = (bf16[160,1536]{1,0:T(8,128)(2,1)S(1)}, f32[160,1536]{1,0:T(8,128)S(1)}, bf16[160,1536]{1,0:T(8,128)(2,1)S(1)}, f32[160,1536]{1,0:T(8,128)S(1)}) fusion(f32[160,1536]{1,0:T(8,128)S(1)} %get-tuple-element.107, bf16[160,1536]{1,0:T(8,128)(2,1)S(1)} %collective-permute-done.15, pred[]{:T(512)S(6)} %eq.81, ...), kind=kLoop, calls=%fused_computation.10 | loop fusion | flops 2457600 | bytes 8847362 | tf_op jit(solution)/shard_map/convert_element_type | solution.py:276
  125.8 0.7 collective-permute-start.24
  126.5 2.1 %collective-permute-start.25 = (bf16[160,1536]{1,0:T(8,128)(2,1)S(1)}, bf16[160,1536]{1,0:T(8,128)(2,1)S(1)}, u32[]{:S(2)}, u32[]{:S(2)}) collective-permute-start(bf16[160,1536]{1,0:T(8,128)(2,1)S(1)} %get-tuple-element.110), channel_id=1, source_target_pairs={{0,8},{8,16},{25,17},{17,9},{2,10},{10,18},{27,19},{19,11},{4,12},... | collective-permute-start | bytes 1474568 | tf_op jit(solution)/shard_map/ppermute | solution.py:194
  128.7 10.0 %collective-permute-done.20 = bf16[2,4,160,192]{3,2,1,0:T(8,128)(2,1)S(1)} collective-permute-done((bf16[2,4,160,192]{3,2,1,0:T(8,128)(2,1)S(1)}, bf16[2,4,160,192]{3,2,1,0:T(8,128)(2,1)S(1)}, u32[]{:S(2)}, u32[]{:S(2)}) %collective-permute-start.20) | collective-permute-done | bytes 491552 | tf_op jit(solution)/shard_map/ppermute | solution.py:274
  139.0 0.5 collective-permute-start.21
  139.6 0.5 select_convert_fusion.1
  140.1 1.3 collective-permute-start.26
  141.4 4.6 %collective-permute-start.27 = (bf16[160,1536]{1,0:T(8,128)(2,1)S(1)}, bf16[160,1536]{1,0:T(8,128)(2,1)S(1)}, u32[]{:S(2)}, u32[]{:S(2)}) collective-permute-start(bf16[160,1536]{1,0:T(8,128)(2,1)S(1)} %get-tuple-element.135), channel_id=1, source_target_pairs={{0,8},{8,16},{16,24},{9,1},{17,9},{25,17},{2,10},{10,18},{18,26},{... | collective-permute-start | bytes 1474568 | tf_op jit(solution)/shard_map/ppermute | solution.py:194
  146.0 0.8 collective-permute-start.22
  146.9 5.6 %collective-permute-done.22 = bf16[2,160,192]{2,1,0:T(8,128)(2,1)S(1)} collective-permute-done((bf16[2,160,192]{2,1,0:T(8,128)(2,1)S(1)}, bf16[2,160,192]{2,1,0:T(8,128)(2,1)S(1)}, u32[]{:S(2)}, u32[]{:S(2)}) %collective-permute-start.22) | collective-permute-done | bytes 122912 | tf_op jit(solution)/shard_map/ppermute | solution.py:295
  152.5 0.2 fusion.5
  152.9 2.4 %collective-permute-done.26 = bf16[160,1536]{1,0:T(8,128)(2,1)S(1)} collective-permute-done((bf16[160,1536]{1,0:T(8,128)(2,1)S(1)}, bf16[160,1536]{1,0:T(8,128)(2,1)S(1)}, u32[]{:S(2)}, u32[]{:S(2)}) %collective-permute-start.26) | collective-permute-done | bytes 491552 | tf_op jit(solution)/shard_map/ppermute | solution.py:194
  155.3 1.2 collective-permute-done.27
  156.4 1.4 fusion.1
  (83 shorter events, 1.4 us)
Async XLA Ops:
  0.0 37.2 %collective-permute-start.3 = (bf16[192,3072]{1,0:T(8,128)(2,1)}, bf16[192,3072]{1,0:T(8,128)(2,1)}, u32[]{:S(2)}, u32[]{:S(2)}) collective-permute-start(bf16[192,3072]{1,0:T(8,128)(2,1)} %bitcast.58), channel_id=1, source_target_pairs={{8,0},{16,8},{24,16},{9,1},{17,9},{25,17},{10,2},{18,10},{26,18},{... | collective-permute-start | bytes 3538952 | tf_op jit(solution)/shard_map/ppermute | solution.py:210
  1.3 35.9 %collective-permute-start.2 = (bf16[192,3072]{1,0:T(8,128)(2,1)}, bf16[192,3072]{1,0:T(8,128)(2,1)}, u32[]{:S(2)}, u32[]{:S(2)}) collective-permute-start(bf16[192,3072]{1,0:T(8,128)(2,1)} %bitcast.59), channel_id=1, source_target_pairs={{0,8},{8,16},{16,24},{1,9},{9,17},{17,25},{2,10},{10,18},{18,26},{... | collective-permute-start | bytes 3538952 | tf_op jit(solution)/shard_map/ppermute | solution.py:209
  7.9 26.9 %collective-permute-start.4 = (bf16[160,3072]{1,0:T(8,128)(2,1)}, bf16[160,3072]{1,0:T(8,128)(2,1)}, u32[]{:S(2)}, u32[]{:S(2)}) collective-permute-start(bf16[160,3072]{1,0:T(8,128)(2,1)} %acts_a.3), channel_id=1, source_target_pairs={{0,2},{2,0},{1,3},{3,1},{4,6},{6,4},{5,7},{7,5},{8,10},{10,8},{9,1... | collective-permute-start | bytes 2949128 | tf_op jit(solution)/shard_map/ppermute | solution.py:187
  7.9 26.9 %collective-permute-start.1 = (bf16[160,3072]{1,0:T(8,128)(2,1)}, bf16[160,3072]{1,0:T(8,128)(2,1)}, u32[]{:S(2)}, u32[]{:S(2)}) collective-permute-start(bf16[160,3072]{1,0:T(8,128)(2,1)} %acts_a.3), channel_id=1, source_target_pairs={{0,4},{4,0},{1,5},{5,1},{2,6},{6,2},{3,7},{7,3},{8,12},{12,8},{9,1... | collective-permute-start | bytes 2949128 | tf_op jit(solution)/shard_map/ppermute | solution.py:197
  9.8 4.6 %copy-start.24 = (f32[160,12]{0,1:T(8,128)S(1)}, f32[160,12]{0,1:T(8,128)}, u32[]{:S(2)}) copy-start(f32[160,12]{0,1:T(8,128)} %param.9) | copy-start | bytes 23044
  9.8 4.6 %copy-start.25 = (s32[160,12]{0,1:T(8,128)S(1)}, s32[160,12]{0,1:T(8,128)}, u32[]{:S(2)}) copy-start(s32[160,12]{0,1:T(8,128)} %param.8) | copy-start | bytes 23044
  9.8 9.4 %copy-start = (bf16[1,1024,1536]{2,1,0:T(8,128)(2,1)S(1)}, bf16[1,1024,1536]{2,1,0:T(8,128)(2,1)}, u32[]{:S(2)}) copy-start(bf16[1,1024,1536]{2,1,0:T(8,128)(2,1)} %param.11) | copy-start | bytes 9437188
  13.0 24.2 %collective-permute-start = (bf16[480,1024]{1,0:T(8,128)(2,1)}, bf16[480,1024]{1,0:T(8,128)(2,1)}, u32[]{:S(2)}, u32[]{:S(2)}) collective-permute-start(bf16[480,1024]{1,0:T(8,128)(2,1)} %get-tuple-element.137), channel_id=1, source_target_pairs={{0,1},{1,0},{2,3},{3,2},{4,5},{5,4},{6,7},{7,6},{8,9},{9,8},{10,11... | collective-permute-start | bytes 2949128 | tf_op jit(solution)/shard_map/ppermute | solution.py:211
  15.1 19.4 %all-to-all-start = ((f32[8,2,160]{2,1,0:T(2,128)}), f32[8,2,160]{2,1,0:T(2,128)S(1)}, u32[]{:S(2)}, u32[]{:S(2)}) async-start(f32[8,2,160]{2,1,0:T(2,128)} %reshape.18), calls=%async_computation | async-start | bytes 32768 | tf_op jit(solution)/shard_map/all_to_all | solution.py:214
  19.2 1.5 copy-start.7
  26.3 1.2 copy-start.3
  27.5 1.1 copy-start.12
  37.2 6.9 %collective-permute-start.5 = (bf16[4,120,1536]{2,1,0:T(8,128)(2,1)}, bf16[4,120,1536]{2,1,0:T(8,128)(2,1)S(1)}, u32[]{:S(2)}, u32[]{:S(2)}) collective-permute-start(bf16[4,120,1536]{2,1,0:T(8,128)(2,1)} %copy-done.12), channel_id=1, source_target_pairs={{0,2},{2,0},{1,3},{3,1},{4,6},{6,4},{5,7},{7,5},{8,10},{10,8},{9,1... | collective-permute-start | bytes 4423688 | tf_op jit(solution)/shard_map/ppermute | solution.py:187
  37.2 1.9 %copy-start.1 = (bf16[1,1024,1536]{2,1,0:T(8,128)(2,1)S(1)}, bf16[1,1024,1536]{2,1,0:T(8,128)(2,1)}, u32[]{:S(2)}) copy-start(bf16[1,1024,1536]{2,1,0:T(8,128)(2,1)} %param.11) | copy-start | bytes 9437188
  39.1 5.0 %copy-start.4 = (bf16[4,120,1536]{2,1,0:T(8,128)(2,1)S(1)}, bf16[4,120,1536]{2,1,0:T(8,128)(2,1)}, u32[]{:S(2)}) copy-start(bf16[4,120,1536]{2,1,0:T(8,128)(2,1)} %copy-done.3) | copy-start | bytes 4423684
  43.5 4.3 %copy-start.18 = (bf16[480,1024]{1,0:T(8,128)(2,1)S(1)}, bf16[480,1024]{1,0:T(8,128)(2,1)}, u32[]{:S(2)}) copy-start(bf16[480,1024]{1,0:T(8,128)(2,1)} %get-tuple-element.74) | copy-start | bytes 2949124
  43.5 6.1 %collective-permute-start.7 = (bf16[2,120,1536]{2,1,0:T(8,128)(2,1)S(1)}, bf16[2,120,1536]{2,1,0:T(8,128)(2,1)S(1)}, u32[]{:S(2)}, u32[]{:S(2)}) collective-permute-start(bf16[2,120,1536]{2,1,0:T(8,128)(2,1)S(1)} %get-tuple-element.68), channel_id=1, source_target_pairs={{0,2},{2,0},{1,3},{3,1},{4,6},{6,4},{5,7},{7,5},{8,10},{10,8},{9,1... | collective-permute-start | bytes 2211848 | tf_op jit(solution)/shard_map/ppermute | solution.py:187
  44.1 18.0 %copy-start.5 = (bf16[4,120,1536]{2,1,0:T(8,128)(2,1)}, bf16[4,120,1536]{2,1,0:T(8,128)(2,1)S(1)}, u32[]{:S(2)}) copy-start(bf16[4,120,1536]{2,1,0:T(8,128)(2,1)S(1)} %collective-permute-done.5.sibling) | copy-start | bytes 4423684
  45.4 13.2 %collective-permute-start.6 = (bf16[160,1536]{1,0:T(8,128)(2,1)S(1)}, bf16[160,1536]{1,0:T(8,128)(2,1)S(1)}, u32[]{:S(2)}, u32[]{:S(2)}) collective-permute-start(bf16[160,1536]{1,0:T(8,128)(2,1)S(1)} %shard_map.74), channel_id=1, source_target_pairs={{0,4},{4,0},{1,5},{5,1},{2,6},{6,2},{3,7},{7,3},{8,12},{12,8},{9,1... | collective-permute-start | bytes 1474568 | tf_op jit(solution)/shard_map/ppermute | solution.py:197
  45.8 25.6 %collective-permute-start.10 = (bf16[192,3072]{1,0:T(8,128)(2,1)}, bf16[192,3072]{1,0:T(8,128)(2,1)S(1)}, u32[]{:S(2)}, u32[]{:S(2)}) collective-permute-start(bf16[192,3072]{1,0:T(8,128)(2,1)} %collective-permute-done.2), channel_id=1, source_target_pairs={{8,16},{16,24},{9,17},{17,25},{10,18},{18,26},{11,19},{19,27},{12,... | collective-permute-start | bytes 3538952 | tf_op jit(solution)/shard_map/ppermute | solution.py:223
  46.5 32.4 %collective-permute-start.11 = (bf16[192,3072]{1,0:T(8,128)(2,1)}, bf16[192,3072]{1,0:T(8,128)(2,1)S(1)}, u32[]{:S(2)}, u32[]{:S(2)}) collective-permute-start(bf16[192,3072]{1,0:T(8,128)(2,1)} %collective-permute-done.3), channel_id=1, source_target_pairs={{8,0},{16,8},{9,1},{17,9},{10,2},{18,10},{11,3},{19,11},{12,4},{20... | collective-permute-start | bytes 3538952 | tf_op jit(solution)/shard_map/ppermute | solution.py:224
  47.8 23.5 %collective-permute-start.12 = (bf16[480,1024]{1,0:T(8,128)(2,1)S(1)}, bf16[480,1024]{1,0:T(8,128)(2,1)S(1)}, u32[]{:S(2)}, u32[]{:S(2)}) collective-permute-start(bf16[480,1024]{1,0:T(8,128)(2,1)S(1)} %copy-done.18), channel_id=1, source_target_pairs={{0,1},{1,0},{2,3},{3,2},{4,5},{5,4},{6,7},{7,6},{8,9},{9,8},{10,11... | collective-permute-start | bytes 2949128 | tf_op jit(solution)/shard_map/ppermute | solution.py:225
  58.6 20.3 %collective-permute-start.8 = (bf16[160,1536]{1,0:T(8,128)(2,1)S(1)}, bf16[160,1536]{1,0:T(8,128)(2,1)S(1)}, u32[]{:S(2)}, u32[]{:S(2)}) collective-permute-start(bf16[160,1536]{1,0:T(8,128)(2,1)S(1)} %shard_map.76), channel_id=1, source_target_pairs={{0,4},{4,0},{1,5},{5,1},{2,6},{6,2},{3,7},{7,3},{8,12},{12,8},{9,1... | collective-permute-start | bytes 1474568 | tf_op jit(solution)/shard_map/ppermute | solution.py:197
  60.0 18.9 %collective-permute-start.9 = (bf16[160,1536]{1,0:T(8,128)(2,1)S(1)}, bf16[160,1536]{1,0:T(8,128)(2,1)S(1)}, u32[]{:S(2)}, u32[]{:S(2)}) collective-permute-start(bf16[160,1536]{1,0:T(8,128)(2,1)S(1)} %get-tuple-element.127), channel_id=1, source_target_pairs={{24,16},{1,9},{26,18},{3,11},{28,20},{5,13},{30,22},{7,15}} | collective-permute-start | bytes 1474568 | tf_op jit(solution)/shard_map/ppermute | solution.py:194
  62.1 16.9 %copy-start.2 = (bf16[1,1024,1536]{2,1,0:T(8,128)(2,1)S(1)}, bf16[1,1024,1536]{2,1,0:T(8,128)(2,1)}, u32[]{:S(2)}) copy-start(bf16[1,1024,1536]{2,1,0:T(8,128)(2,1)} %param.11) | copy-start | bytes 9437188
  71.3 11.6 %copy-start.14 = (bf16[192,3072]{1,0:T(8,128)(2,1)}, bf16[192,3072]{1,0:T(8,128)(2,1)S(1)}, u32[]{:S(2)}) copy-start(bf16[192,3072]{1,0:T(8,128)(2,1)S(1)} %collective-permute-done.10) | copy-start | bytes 3538948
  78.9 4.0 %copy-start.16 = (bf16[192,3072]{1,0:T(8,128)(2,1)}, bf16[192,3072]{1,0:T(8,128)(2,1)S(1)}, u32[]{:S(2)}) copy-start(bf16[192,3072]{1,0:T(8,128)(2,1)S(1)} %collective-permute-done.11) | copy-start | bytes 3538948
  78.9 4.0 %copy-start.22 = (bf16[160,1536]{1,0:T(8,128)(2,1)}, bf16[160,1536]{1,0:T(8,128)(2,1)S(1)}, u32[]{:S(2)}) copy-start(bf16[160,1536]{1,0:T(8,128)(2,1)S(1)} %collective-permute-done.8) | copy-start | bytes 1474564
  78.9 4.0 %copy-start.20 = (bf16[160,1536]{1,0:T(8,128)(2,1)}, bf16[160,1536]{1,0:T(8,128)(2,1)S(1)}, u32[]{:S(2)}) copy-start(bf16[160,1536]{1,0:T(8,128)(2,1)S(1)} %collective-permute-done.9) | copy-start | bytes 1474564
  82.9 0.9 copy-start.9
  83.8 6.3 %collective-permute-start.17 = (bf16[2,120,1536]{2,1,0:T(8,128)(2,1)}, bf16[2,120,1536]{2,1,0:T(8,128)(2,1)}, u32[]{:S(2)}, u32[]{:S(2)}) collective-permute-start(bf16[2,120,1536]{2,1,0:T(8,128)(2,1)} %get-tuple-element.83), channel_id=1, source_target_pairs={{0,2},{2,0},{1,3},{3,1},{4,6},{6,4},{5,7},{7,5},{8,10},{10,8},{9,1... | collective-permute-start | bytes 2211848 | tf_op jit(solution)/shard_map/ppermute | solution.py:187
  83.8 13.9 %collective-permute-start.16 = (bf16[160,1536]{1,0:T(8,128)(2,1)}, bf16[160,1536]{1,0:T(8,128)(2,1)}, u32[]{:S(2)}, u32[]{:S(2)}) collective-permute-start(bf16[160,1536]{1,0:T(8,128)(2,1)} %shard_map.78), channel_id=1, source_target_pairs={{0,4},{4,0},{1,5},{5,1},{2,6},{6,2},{3,7},{7,3},{8,12},{12,8},{9,1... | collective-permute-start | bytes 1474568 | tf_op jit(solution)/shard_map/ppermute | solution.py:197
  85.3 1.4 copy-start.6
  86.7 1.3 copy-start.15
  86.7 2.1 %copy-start.17 = (bf16[192,3072]{1,0:T(8,128)(2,1)S(1)}, bf16[192,3072]{1,0:T(8,128)(2,1)}, u32[]{:S(2)}) copy-start(bf16[192,3072]{1,0:T(8,128)(2,1)} %copy-done.16) | copy-start | bytes 3538948
  86.7 3.4 %copy-start.10 = (bf16[2,120,1536]{2,1,0:T(8,128)(2,1)S(1)}, bf16[2,120,1536]{2,1,0:T(8,128)(2,1)}, u32[]{:S(2)}) copy-start(bf16[2,120,1536]{2,1,0:T(8,128)(2,1)} %copy-done.9) | copy-start | bytes 2211844
  88.1 25.3 %collective-permute-start.13 = (bf16[192,3072]{1,0:T(8,128)(2,1)S(1)}, bf16[192,3072]{1,0:T(8,128)(2,1)S(1)}, u32[]{:S(2)}, u32[]{:S(2)}) collective-permute-start(bf16[192,3072]{1,0:T(8,128)(2,1)S(1)} %copy-done.15), channel_id=1, source_target_pairs={{16,24},{17,25},{18,26},{19,27},{20,28},{21,29},{22,30},{23,31}} | collective-permute-start | bytes 3538952 | tf_op jit(solution)/shard_map/ppermute | solution.py:241
  88.8 30.0 %collective-permute-start.14 = (bf16[192,3072]{1,0:T(8,128)(2,1)S(1)}, bf16[192,3072]{1,0:T(8,128)(2,1)S(1)}, u32[]{:S(2)}, u32[]{:S(2)}) collective-permute-start(bf16[192,3072]{1,0:T(8,128)(2,1)S(1)} %copy-done.17), channel_id=1, source_target_pairs={{8,0},{9,1},{10,2},{11,3},{12,4},{13,5},{14,6},{15,7}} | collective-permute-start | bytes 3538952 | tf_op jit(solution)/shard_map/ppermute | solution.py:242
  90.1 7.6 %copy-start.23 = (bf16[160,1536]{1,0:T(8,128)(2,1)S(1)}, bf16[160,1536]{1,0:T(8,128)(2,1)}, u32[]{:S(2)}) copy-start(bf16[160,1536]{1,0:T(8,128)(2,1)} %copy-done.22) | copy-start | bytes 1474564
  97.7 9.6 %collective-permute-start.19 = (bf16[160,3072]{1,0:T(8,128)(2,1)}, bf16[160,3072]{1,0:T(8,128)(2,1)S(1)}, u32[]{:S(2)}, u32[]{:S(2)}) collective-permute-start(bf16[160,3072]{1,0:T(8,128)(2,1)} %collective-permute-done.1.acts_b), channel_id=1, source_target_pairs={{0,2},{2,0},{1,3},{3,1},{4,6},{6,4},{5,7},{7,5},{8,10},{10,8},{9,1... | collective-permute-start | bytes 2949128 | tf_op jit(solution)/shard_map/ppermute | solution.py:187
  97.9 15.4 %collective-permute-start.15 = (bf16[160,1536]{1,0:T(8,128)(2,1)S(1)}, bf16[160,1536]{1,0:T(8,128)(2,1)S(1)}, u32[]{:S(2)}, u32[]{:S(2)}) collective-permute-start(bf16[160,1536]{1,0:T(8,128)(2,1)S(1)} %get-tuple-element.125), channel_id=1, source_target_pairs={{0,8},{25,17},{2,10},{27,19},{4,12},{29,21},{6,14},{31,23}} | collective-permute-start | bytes 1474568 | tf_op jit(solution)/shard_map/ppermute | solution.py:194
  101.8 17.0 %collective-permute-start.18 = (bf16[160,1536]{1,0:T(8,128)(2,1)S(1)}, bf16[160,1536]{1,0:T(8,128)(2,1)S(1)}, u32[]{:S(2)}, u32[]{:S(2)}) collective-permute-start(bf16[160,1536]{1,0:T(8,128)(2,1)S(1)} %shard_map.81), channel_id=1, source_target_pairs={{0,4},{4,0},{1,5},{5,1},{2,6},{6,2},{3,7},{7,3},{8,12},{12,8},{9,1... | collective-permute-start | bytes 1474568 | tf_op jit(solution)/shard_map/ppermute | solution.py:197
  104.9 2.4 %copy-start.8 = (bf16[160,3072]{1,0:T(8,128)(2,1)S(1)}, bf16[160,3072]{1,0:T(8,128)(2,1)}, u32[]{:S(2)}) copy-start(bf16[160,3072]{1,0:T(8,128)(2,1)} %acts_a.3) | copy-start | bytes 2949124
  104.9 2.4 %copy-start.11 = (bf16[3072,192]{0,1:T(8,128)(2,1)S(1)}, bf16[3072,192]{0,1:T(8,128)(2,1)}, u32[]{:S(2)}) copy-start(bf16[3072,192]{0,1:T(8,128)(2,1)} %param.13) | copy-start | bytes 3538948
  122.1 2.1 %copy-start.21 = (bf16[160,1536]{1,0:T(8,128)(2,1)S(1)}, bf16[160,1536]{1,0:T(8,128)(2,1)}, u32[]{:S(2)}) copy-start(bf16[160,1536]{1,0:T(8,128)(2,1)} %copy-done.20) | copy-start | bytes 1474564
  122.5 1.7 %copy-start.13 = (f32[160,1536]{1,0:T(8,128)S(1)}, f32[160,1536]{1,0:T(8,128)}, u32[]{:S(2)}) copy-start(f32[160,1536]{1,0:T(8,128)} %get-tuple-element.101) | copy-start | bytes 2949124
  122.6 16.1 %collective-permute-start.20 = (bf16[2,4,160,192]{3,2,1,0:T(8,128)(2,1)S(1)}, bf16[2,4,160,192]{3,2,1,0:T(8,128)(2,1)S(1)}, u32[]{:S(2)}, u32[]{:S(2)}) collective-permute-start(bf16[2,4,160,192]{3,2,1,0:T(8,128)(2,1)S(1)} %pad_maximum_fusion), channel_id=1, source_target_pairs={{0,1},{1,0},{2,3},{3,2},{4,5},{5,4},{6,7},{7,6},{8,9},{9,8},{10,11... | collective-permute-start | bytes 1474568 | tf_op jit(solution)/shard_map/ppermute | solution.py:274
  125.8 13.8 %collective-permute-start.24 = (bf16[160,1536]{1,0:T(8,128)(2,1)S(1)}, bf16[160,1536]{1,0:T(8,128)(2,1)S(1)}, u32[]{:S(2)}, u32[]{:S(2)}) collective-permute-start(bf16[160,1536]{1,0:T(8,128)(2,1)S(1)} %get-tuple-element.109), channel_id=1, source_target_pairs={{24,16},{16,8},{1,9},{9,17},{26,18},{18,10},{3,11},{11,19},{28,20}... | collective-permute-start | bytes 1474568 | tf_op jit(solution)/shard_map/ppermute | solution.py:194
  126.5 13.1 %collective-permute-start.25 = (bf16[160,1536]{1,0:T(8,128)(2,1)S(1)}, bf16[160,1536]{1,0:T(8,128)(2,1)S(1)}, u32[]{:S(2)}, u32[]{:S(2)}) collective-permute-start(bf16[160,1536]{1,0:T(8,128)(2,1)S(1)} %get-tuple-element.110), channel_id=1, source_target_pairs={{0,8},{8,16},{25,17},{17,9},{2,10},{10,18},{27,19},{19,11},{4,12},... | collective-permute-start | bytes 1474568 | tf_op jit(solution)/shard_map/ppermute | solution.py:194
  138.9 7.9 %collective-permute-start.23 = (bf16[2,160,192]{2,1,0:T(8,128)(2,1)S(1)}, bf16[2,160,192]{2,1,0:T(8,128)(2,1)S(1)}, u32[]{:S(2)}, u32[]{:S(2)}) collective-permute-start(bf16[2,160,192]{2,1,0:T(8,128)(2,1)S(1)} %get-tuple-element.144), channel_id=1, source_target_pairs={{0,2},{2,0},{1,3},{3,1},{4,6},{6,4},{5,7},{7,5},{8,10},{10,8},{9,1... | collective-permute-start | bytes 368648 | tf_op jit(solution)/shard_map/ppermute | solution.py:292
  139.0 6.9 %collective-permute-start.21 = (bf16[2,160,192]{2,1,0:T(8,128)(2,1)S(1)}, bf16[2,160,192]{2,1,0:T(8,128)(2,1)S(1)}, u32[]{:S(2)}, u32[]{:S(2)}) collective-permute-start(bf16[2,160,192]{2,1,0:T(8,128)(2,1)S(1)} %get-tuple-element.145), channel_id=1, source_target_pairs={{0,4},{4,0},{1,5},{5,1},{2,6},{6,2},{3,7},{7,3},{8,12},{12,8},{9,1... | collective-permute-start | bytes 368648 | tf_op jit(solution)/shard_map/ppermute | solution.py:293
  140.1 15.2 %collective-permute-start.26 = (bf16[160,1536]{1,0:T(8,128)(2,1)S(1)}, bf16[160,1536]{1,0:T(8,128)(2,1)S(1)}, u32[]{:S(2)}, u32[]{:S(2)}) collective-permute-start(bf16[160,1536]{1,0:T(8,128)(2,1)S(1)} %get-tuple-element.134), channel_id=1, source_target_pairs={{8,0},{16,8},{24,16},{1,9},{9,17},{17,25},{10,2},{18,10},{26,18},{... | collective-permute-start | bytes 1474568 | tf_op jit(solution)/shard_map/ppermute | solution.py:194
  141.4 15.1 %collective-permute-start.27 = (bf16[160,1536]{1,0:T(8,128)(2,1)S(1)}, bf16[160,1536]{1,0:T(8,128)(2,1)S(1)}, u32[]{:S(2)}, u32[]{:S(2)}) collective-permute-start(bf16[160,1536]{1,0:T(8,128)(2,1)S(1)} %get-tuple-element.135), channel_id=1, source_target_pairs={{0,8},{8,16},{16,24},{9,1},{17,9},{25,17},{2,10},{10,18},{18,26},{... | collective-permute-start | bytes 1474568 | tf_op jit(solution)/shard_map/ppermute | solution.py:194
  146.0 6.5 %collective-permute-start.22 = (bf16[2,160,192]{2,1,0:T(8,128)(2,1)S(1)}, bf16[2,160,192]{2,1,0:T(8,128)(2,1)S(1)}, u32[]{:S(2)}, u32[]{:S(2)}) collective-permute-start(bf16[2,160,192]{2,1,0:T(8,128)(2,1)S(1)} %get-tuple-element.99), channel_id=1, source_target_pairs={{0,6},{2,4},{4,2},{6,0},{1,7},{3,5},{5,3},{7,1},{8,14},{10,12},{12... | collective-permute-start | bytes 368648 | tf_op jit(solution)/shard_map/ppermute | solution.py:295
  152.8 3.7 %copy-start.19 = (bf16[160,1536]{1,0:T(8,128)(2,1)S(1)}, bf16[160,1536]{1,0:T(8,128)(2,1)}, u32[]{:S(2)}) copy-start(bf16[160,1536]{1,0:T(8,128)(2,1)} %param.7) | copy-start | bytes 1474564
